TPU v7x, 256 devices: a whole 4x4x8 slice. The times are simulated.
256 devices in a mesh: tile: 64 (over y, x_hi, z), vert: 4 (over x_lo, core).
Axes of the slice: x: 4 (x_hi: 2, x_lo: 2; x = x_hi * 2 + x_lo), y: 4, z: 8, core: 2. Of those that a mesh axis runs over, the one named last changes fastest.
Arguments:
- phase_init: float32 [7, 256, 16, 512], P(None, 'tile', None, 'vert'), may hold values from 0 to 0.25
- flow_init: float32 [19, 256, 16, 512], P(None, 'tile', None, 'vert'), may hold values from 0 to 0.2
- solid_mask: int32 [256, 16, 512], P('tile', None, 'vert'), may hold values from 0 to 1, as said below
- sensor_cells: int32 [3, 32768], replicated, may hold values from 0 to 510, as said below
- sensor_weights: float32 [32768], replicated, may hold values from 0.5 to 2
Outputs:
- grad_phase: float32 [7, 256, 16, 512], P(None, 'tile', None, 'vert')
- grad_flow: float32 [19, 256, 16, 512], P(None, 'tile', None, 'vert')
Inputs may be any that keep to these rules, and one draw needn't show every extreme that they name: `solid_mask`: 1 marks a solid cell, 0 a fluid one; every cell whose first index is 0 or 255, or whose third index is 0 or 511, is solid. `sensor_cells`: rows 0, 1, 2 hold a probe's cell indices along the first, second and third dimensions; each probe's cell is fluid; several probes may share a cell.
All inputs are finite; a program needn't handle non-finite values.
Results may differ from a plain program's by a relative error of at most 0.0003.
Values sent between devices are 32-bit elements; how exact they have to be, the bound alone decides.
No kernel may reach another device: no remote copies, remote signals or barrier semaphores. Data moves between devices by JAX's collectives and lax.ppermute only.
A program may use at most 64 MiB of HBM per device.

v0:
```python
import jax
import jax.numpy as jnp
import numpy as np
from jax import lax
from jax.sharding import PartitionSpec as P

flow_dirs = np.array(
    [
        [0, 0, 0],
        [1, 0, 0],
        [-1, 0, 0],
        [0, 1, 0],
        [0, -1, 0],
        [0, 0, 1],
        [0, 0, -1],
        [1, 1, 0],
        [-1, -1, 0],
        [1, -1, 0],
        [-1, 1, 0],
        [1, 0, 1],
        [-1, 0, -1],
        [1, 0, -1],
        [-1, 0, 1],
        [0, 1, 1],
        [0, -1, -1],
        [0, 1, -1],
        [0, -1, 1],
    ]
)
flow_weights = np.array([1.0 / 3.0] + [1.0 / 18.0] * 6 + [1.0 / 36.0] * 12)
flow_back = np.array([0, 2, 1, 4, 3, 6, 5, 8, 7, 10, 9, 12, 11, 14, 13, 16, 15, 18, 17])
phase_weights = np.array([0.25] + [0.125] * 6)
all_dirs = np.concatenate([flow_dirs[:7], flow_dirs])
rho_air = 0.05
tau_air = 0.6
tau_water = 0.9
tau_phase = 0.8
beta_bulk = 0.3
kappa_grad = 0.6
sharpen = 0.075
gravity = 0.02
shaking = 0.01
soft_floor = 0.01


def padded_2(cells, sides, width):
    for axis, dim in sides:
        count = lax.axis_size(axis)
        ends = count - 1
        head = lax.slice_in_dim(cells, 0, width, axis=dim)
        tail = lax.slice_in_dim(cells, cells.shape[dim] - width, cells.shape[dim], axis=dim)
        cells = jnp.concatenate(
            [
                lax.ppermute(tail, axis, [(i, (i + 1) % count) for i in range(ends)]),
                cells,
                lax.ppermute(head, axis, [((i + 1) % count, i) for i in range(ends)]),
            ],
            axis=dim,
        )
    return cells


def spread_table(matrix, vectors):
    return jnp.tensordot(matrix, vectors, axes=1, precision=lax.Precision.HIGHEST)


def neighbours(padded):
    centre = padded[1:-1, :, 1:-1]
    ahead_x = padded[2:, :, 1:-1]
    behind_x = padded[:-2, :, 1:-1]
    ahead_y = jnp.roll(centre, -1, axis=1)
    behind_y = jnp.roll(centre, 1, axis=1)
    ahead_z = padded[1:-1, :, 2:]
    behind_z = padded[1:-1, :, :-2]
    gradient = jnp.stack(
        [0.5 * (ahead_x - behind_x), 0.5 * (ahead_y - behind_y), 0.5 * (ahead_z - behind_z)]
    )
    laplace = ahead_x + behind_x + ahead_y + behind_y + ahead_z + behind_z - 6.0 * centre
    return (gradient, laplace)


def collide(phase_dist, flow_dist, gradient, laplace, solid_cells):
    velocity_table = jnp.asarray(flow_dirs, jnp.float32)
    weight_table = jnp.asarray(flow_weights, jnp.float32)[:, None, None, None]
    phase_weight = jnp.asarray(phase_weights, jnp.float32)[:, None, None, None]
    phase_sum = jnp.sum(phase_dist, axis=0)
    clipped = jnp.clip(phase_sum, 0.0, 1.0)
    density = rho_air + (1.0 - rho_air) * clipped
    relax_time = tau_air + (tau_water - tau_air) * clipped
    potential = (
        4.0 * beta_bulk * phase_sum * (phase_sum - 1.0) * (phase_sum - 0.5) - kappa_grad * laplace
    )
    pressure = jnp.sum(flow_dist, axis=0)
    momentum = spread_table(velocity_table.T, flow_dist)
    body_force = jnp.stack(
        [-shaking * density, jnp.zeros_like(density), -gravity * (density - rho_air)]
    )
    force = potential * gradient + body_force
    velocity = momentum + force / (2.0 * density)
    speed_sq = jnp.sum(velocity * velocity, axis=0)
    projected = spread_table(velocity_table, velocity)
    flow_equil = weight_table * (
        pressure + 3.0 * projected + 4.5 * projected * projected - 1.5 * speed_sq
    )
    force_along = spread_table(velocity_table, force)
    work_rate = jnp.sum(velocity * force, axis=0)
    source = (
        weight_table
        * (1.0 - 0.5 / relax_time)
        * (3.0 * (force_along - work_rate) + 9.0 * projected * force_along)
        / density
    )
    flow_post = flow_dist - (flow_dist - flow_equil) / relax_time + source
    flow_post = solid_cells * flow_dist[flow_back] + (1.0 - solid_cells) * flow_post
    grad_length = jnp.sqrt(jnp.sum(gradient * gradient, axis=0) + soft_floor)
    carried = (
        phase_sum * velocity + sharpen * phase_sum * (1.0 - phase_sum) * gradient / grad_length
    )
    phase_along = spread_table(velocity_table[:7], carried)
    phase_equil = phase_weight * (phase_sum + 4.0 * phase_along)
    phase_post = phase_dist - (phase_dist - phase_equil) / tau_phase
    phase_post = solid_cells * phase_dist[flow_back[:7]] + (1.0 - solid_cells) * phase_post
    return (phase_post, flow_post)


def advect(padded, velocity_set, rim_width, grow_by, direction):
    count_x = padded.shape[1] - 2 * (rim_width - grow_by)
    count_z = padded.shape[3] - 2 * (rim_width - grow_by)
    shifted_list = []
    for slot_index in range(velocity_set.shape[0]):
        step_x = int(velocity_set[slot_index][0])
        step_y = int(velocity_set[slot_index][1])
        step_z = int(velocity_set[slot_index][2])
        start_x = rim_width - grow_by - direction * step_x
        start_z = rim_width - grow_by - direction * step_z
        window_cut = padded[slot_index, start_x : start_x + count_x, :, start_z : start_z + count_z]
        shifted_list.append(jnp.roll(window_cut, direction * step_y, axis=1))
    return jnp.stack(shifted_list)


def spread_back(d_gradient, d_laplace):
    stacked = jnp.concatenate([d_gradient, d_laplace[None]])
    outside = padded_2(stacked, (("tile", 1), ("vert", 3)), 1)
    centre = outside[:, 1:-1, :, 1:-1]
    from_behind_x = outside[:, :-2, :, 1:-1]
    from_ahead_x = outside[:, 2:, :, 1:-1]
    from_behind_z = outside[:, 1:-1, :, :-2]
    from_ahead_z = outside[:, 1:-1, :, 2:]
    from_behind_y = jnp.roll(centre, 1, axis=2)
    from_ahead_y = jnp.roll(centre, -1, axis=2)
    result = (
        0.5 * (from_behind_x[0] - from_ahead_x[0])
        + 0.5 * (from_behind_y[1] - from_ahead_y[1])
        + 0.5 * (from_behind_z[2] - from_ahead_z[2])
    )
    result = (
        result
        + from_behind_x[3]
        + from_ahead_x[3]
        + from_behind_y[3]
        + from_ahead_y[3]
        + from_behind_z[3]
        + from_ahead_z[3]
        - 6.0 * centre[3]
    )
    return result


def retreat(collide_back, adj_phase, adj_flow):
    d_phase, d_flow, d_gradient, d_laplace = collide_back((adj_phase, adj_flow))
    d_sum = spread_back(d_gradient, d_laplace)
    return jnp.concatenate([d_phase + d_sum[None], d_flow])


def shards(phase_init, flow_init, solid_mask, sensor_cells, sensor_weights):
    solid_cells = solid_mask.astype(jnp.float32)
    size_x, layers, size_z = solid_cells.shape
    first_x = lax.axis_index("tile") * size_x
    first_z = lax.axis_index("vert") * size_z

    def local_collide(phase_dist, flow_dist, gradient, laplace):
        return collide(phase_dist, flow_dist, gradient, laplace, solid_cells)

    padded0 = padded_2(jnp.sum(phase_init, axis=0), (("tile", 0), ("vert", 2)), 1)
    (gradient0, laplace0), stencil_back0 = jax.vjp(neighbours, padded0)
    post_pair, collide_back0 = jax.vjp(local_collide, phase_init, flow_init, gradient0, laplace0)
    post_all = jnp.concatenate(post_pair)
    narrow = padded_2(post_all, (("tile", 1), ("vert", 3)), 1)
    state_mid = advect(narrow, all_dirs, 1, 0, 1)
    padded1 = padded_2(jnp.sum(state_mid[:7], axis=0), (("tile", 0), ("vert", 2)), 1)
    phase_mid = state_mid[:7]
    flow_mid = state_mid[7:]
    (gradient1, laplace1), stencil_back1 = jax.vjp(neighbours, padded1)
    _, collide_back1 = jax.vjp(local_collide, phase_mid, flow_mid, gradient1, laplace1)
    cells_x = sensor_cells[0] - first_x
    cells_z = sensor_cells[2] - first_z
    owned_probe = (cells_x >= 0) & (cells_x < size_x) & (cells_z >= 0) & (cells_z < size_z)
    local_x = jnp.where(owned_probe, cells_x, 0)
    local_z = jnp.where(owned_probe, cells_z, 0)
    probe_weight = jnp.where(owned_probe, sensor_weights, 0.0)
    seed_field = (
        jnp.zeros((size_x, layers, size_z), jnp.float32)
        .at[local_x, sensor_cells[1], local_z]
        .add(probe_weight)
    )
    seed_wide = padded_2(seed_field, (("tile", 0), ("vert", 2)), 1)
    adj_flow = advect(jnp.broadcast_to(seed_wide, (19,) + seed_wide.shape), flow_dirs, 1, 0, -1)
    adjoint_mid = retreat(collide_back1, jnp.zeros_like(phase_mid), adj_flow)
    adjoint_wide = padded_2(adjoint_mid, (("tile", 1), ("vert", 3)), 1)
    adj_post = advect(adjoint_wide, all_dirs, 1, 0, -1)
    result = retreat(collide_back0, adj_post[:7], adj_post[7:])
    return (result[:7], result[7:])


def solution(mesh):
    return jax.shard_map(
        shards,
        mesh=mesh,
        in_specs=(
            P(None, "tile", None, "vert"),
            P(None, "tile", None, "vert"),
            P("tile", None, "vert"),
            P(),
            P(),
        ),
        out_specs=(P(None, "tile", None, "vert"), P(None, "tile", None, "vert")),
        check_vma=False,
    )
```

profile of v0, /device:TPU:24, one launch (start us, length us, event | category | flops | bytes accessed | tf_op | source)
XLA Modules:
  0.0 382.2 jit_solution(10008838604449172510)
XLA Ops:
  1.7 10.4 %collective-permute-start = (f32[1,16,128]{2,1,0:T(8,128)S(1)}, f32[1,16,128]{2,1,0:T(8,128)S(1)}, u32[]{:S(2)}, u32[]{:S(2)}) collective-permute-start(f32[1,16,128]{2,1,0:T(8,128)S(1)} %get-tuple-element.217), channel_id=1, source_target_pairs={{4,0},{8,4},{12,8},{16,12},{20,16},{24,20},{28,24},{32,28},{36,32}... | collective-permute-start | bytes 24584 | tf_op jit(solution)/shard_map/ppermute | solution.py:56
  14.1 2.3 compare_select_fusion.2
  18.9 172.3 %scatter_custom_fusion.4 = f32[8192]{0:T(1024)S(1)} fusion(s32[32768]{0:T(1024)S(1)} %broadcast_select_fusion, f32[32768]{0:T(1024)S(1)} %broadcast_select_fusion.1, f32[]{:T(128)} %constant.46.clone.1), kind=kCustom, calls=%fused_computation.558 | custom fusion | flops 32768 | bytes 32772
  191.2 8.4 %collective-permute-start.12 = (f32[1,16,128]{2,1,0:T(8,128)S(1)}, f32[1,16,128]{2,1,0:T(8,128)S(1)}, u32[]{:S(2)}, u32[]{:S(2)}) collective-permute-start(f32[1,16,128]{2,1,0:T(8,128)S(1)} %get-tuple-element.187), channel_id=1, source_target_pairs={{4,0},{8,4},{12,8},{16,12},{20,16},{24,20},{28,24},{32,28},{36,32}... | collective-permute-start | bytes 24584 | tf_op jit(solution)/shard_map/ppermute | solution.py:56
  218.4 9.0 %collective-permute-start.5 = (f32[26,1,16,128]{3,2,1,0:T(8,128)S(1)}, f32[26,1,16,128]{3,2,1,0:T(8,128)S(1)}, u32[]{:S(2)}, u32[]{:S(2)}) collective-permute-start(f32[26,1,16,128]{3,2,1,0:T(8,128)S(1)} %get-tuple-element.98), channel_id=1, source_target_pairs={{4,0},{8,4},{12,8},{16,12},{20,16},{24,20},{28,24},{32,28},{36,32}... | collective-permute-start | bytes 638984 | tf_op jit(solution)/shard_map/ppermute | solution.py:56
  231.6 9.2 %collective-permute-done.4 = f32[26,1,16,128]{3,2,1,0:T(8,128)S(1)} collective-permute-done((f32[26,1,16,128]{3,2,1,0:T(8,128)S(1)}, f32[26,1,16,128]{3,2,1,0:T(8,128)S(1)}, u32[]{:S(2)}, u32[]{:S(2)}) %collective-permute-start.4) | collective-permute-done | bytes 213024 | tf_op jit(solution)/shard_map/ppermute | solution.py:54
  242.9 2.2 copy.266
  247.6 4.1 %collective-permute-start.6 = (f32[26,6,16,1]{0,2,3,1:T(8,128)S(1)}, f32[26,6,16,1]{0,2,3,1:T(8,128)}, u32[]{:S(2)}, u32[]{:S(2)}) collective-permute-start(f32[26,6,16,1]{0,2,3,1:T(8,128)S(1)} %copy.264), channel_id=1, source_target_pairs={{0,1},{1,2},{2,3},{4,5},{5,6},{6,7},{8,9},{9,10},{10,11},{12,13},{... | collective-permute-start | bytes 29960 | tf_op jit(solution)/shard_map/ppermute | solution.py:54
  262.0 3.9 %collective-permute-start.9 = (f32[1,16,128]{2,1,0:T(8,128)S(1)}, f32[1,16,128]{2,1,0:T(8,128)S(1)}, u32[]{:S(2)}, u32[]{:S(2)}) collective-permute-start(f32[1,16,128]{2,1,0:T(8,128)S(1)} %get-tuple-element.206), channel_id=1, source_target_pairs={{0,4},{4,8},{8,12},{12,16},{16,20},{20,24},{24,28},{28,32},{32,36}... | collective-permute-start | bytes 24584 | tf_op jit(solution)/shard_map/ppermute | solution.py:54
  268.3 3.8 collective-permute-done.9
  275.5 2.5 collective-permute-done.10
  285.8 3.3 collective-permute-start.17
  289.1 2.5 collective-permute-start.16
  291.8 2.2 scatter_fusion.1
  294.8 4.6 %collective-permute-done.16 = f32[4,1,16,128]{3,2,1,0:T(8,128)S(1)} collective-permute-done((f32[4,1,16,128]{3,2,1,0:T(8,128)S(1)}, f32[4,1,16,128]{3,2,1,0:T(8,128)S(1)}, u32[]{:S(2)}, u32[]{:S(2)}) %collective-permute-start.16) | collective-permute-done | bytes 32800 | tf_op jit(solution)/shard_map/ppermute | solution.py:54
  300.9 4.1 %collective-permute-start.18 = (f32[4,6,16,1]{3,2,1,0:T(8,128)S(1)}, f32[4,6,16,1]{3,2,1,0:T(8,128)S(1)}, u32[]{:S(2)}, u32[]{:S(2)}) collective-permute-start(f32[4,6,16,1]{3,2,1,0:T(8,128)S(1)} %get-tuple-element.119), channel_id=1, source_target_pairs={{0,1},{1,2},{2,3},{4,5},{5,6},{6,7},{8,9},{9,10},{10,11},{12,13},{... | collective-permute-start | bytes 4616 | tf_op jit(solution)/shard_map/ppermute | solution.py:54
  307.1 4.1 %collective-permute-start.20 = (f32[26,1,16,128]{3,2,1,0:T(8,128)S(1)}, f32[26,1,16,128]{3,2,1,0:T(8,128)S(1)}, u32[]{:S(2)}, u32[]{:S(2)}) collective-permute-start(f32[26,1,16,128]{3,2,1,0:T(8,128)S(1)} %get-tuple-element.96), channel_id=1, source_target_pairs={{4,0},{8,4},{12,8},{16,12},{20,16},{24,20},{28,24},{32,28},{36,32}... | collective-permute-start | bytes 638984 | tf_op jit(solution)/shard_map/ppermute | solution.py:56
  314.8 8.6 %collective-permute-done.21 = f32[26,1,16,128]{3,2,1,0:T(8,128)S(1)} collective-permute-done((f32[26,1,16,128]{3,2,1,0:T(8,128)S(1)}, f32[26,1,16,128]{3,2,1,0:T(8,128)S(1)}, u32[]{:S(2)}, u32[]{:S(2)}) %collective-permute-start.21) | collective-permute-done | bytes 213024 | tf_op jit(solution)/shard_map/ppermute | solution.py:54
  325.1 2.1 copy.296
  330.0 9.6 %collective-permute-start.23 = (f32[26,6,16,1]{0,2,3,1:T(8,128)}, f32[26,6,16,1]{0,2,3,1:T(8,128)}, u32[]{:S(2)}, u32[]{:S(2)}) collective-permute-start(f32[26,6,16,1]{0,2,3,1:T(8,128)} %copy.298), channel_id=1, source_target_pairs={{0,1},{1,2},{2,3},{4,5},{5,6},{6,7},{8,9},{9,10},{10,11},{12,13},{... | collective-permute-start | bytes 29960 | tf_op jit(solution)/shard_map/ppermute | solution.py:54
  361.6 3.9 %collective-permute-start.24 = (f32[4,1,16,128]{3,2,1,0:T(8,128)S(1)}, f32[4,1,16,128]{3,2,1,0:T(8,128)S(1)}, u32[]{:S(2)}, u32[]{:S(2)}) collective-permute-start(f32[4,1,16,128]{3,2,1,0:T(8,128)S(1)} %get-tuple-element.123), channel_id=1, source_target_pairs={{0,4},{4,8},{8,12},{12,16},{16,20},{20,24},{24,28},{28,32},{32,36}... | collective-permute-start | bytes 98312 | tf_op jit(solution)/shard_map/ppermute | solution.py:54
  365.7 6.2 %collective-permute-done.24 = f32[4,1,16,128]{3,2,1,0:T(8,128)S(1)} collective-permute-done((f32[4,1,16,128]{3,2,1,0:T(8,128)S(1)}, f32[4,1,16,128]{3,2,1,0:T(8,128)S(1)}, u32[]{:S(2)}, u32[]{:S(2)}) %collective-permute-start.24) | collective-permute-done | bytes 32800 | tf_op jit(solution)/shard_map/ppermute | solution.py:54
  373.3 4.3 %collective-permute-start.26 = (f32[4,6,16,1]{3,2,1,0:T(8,128)S(1)}, f32[4,6,16,1]{3,2,1,0:T(8,128)S(1)}, u32[]{:S(2)}, u32[]{:S(2)}) collective-permute-start(f32[4,6,16,1]{3,2,1,0:T(8,128)S(1)} %get-tuple-element.117), channel_id=1, source_target_pairs={{0,1},{1,2},{2,3},{4,5},{5,6},{6,7},{8,9},{9,10},{10,11},{12,13},{... | collective-permute-start | bytes 4616 | tf_op jit(solution)/shard_map/ppermute | solution.py:54
  377.7 2.2 scatter_fusion.3
  (464 shorter events, 92.9 us)
Async XLA Ops:
  1.7 203.4 %collective-permute-start = (f32[1,16,128]{2,1,0:T(8,128)S(1)}, f32[1,16,128]{2,1,0:T(8,128)S(1)}, u32[]{:S(2)}, u32[]{:S(2)}) collective-permute-start(f32[1,16,128]{2,1,0:T(8,128)S(1)} %get-tuple-element.217), channel_id=1, source_target_pairs={{4,0},{8,4},{12,8},{16,12},{20,16},{24,20},{28,24},{32,28},{36,32}... | collective-permute-start | bytes 24584 | tf_op jit(solution)/shard_map/ppermute | solution.py:56
  12.1 193.0 %collective-permute-start.1 = (f32[1,16,128]{2,1,0:T(8,128)S(1)}, f32[1,16,128]{2,1,0:T(8,128)S(1)}, u32[]{:S(2)}, u32[]{:S(2)}) collective-permute-start(f32[1,16,128]{2,1,0:T(8,128)S(1)} %get-tuple-element.216), channel_id=1, source_target_pairs={{0,4},{4,8},{8,12},{12,16},{16,20},{20,24},{24,28},{28,32},{32,36}... | collective-permute-start | bytes 24584 | tf_op jit(solution)/shard_map/ppermute | solution.py:54
  191.2 16.6 %collective-permute-start.12 = (f32[1,16,128]{2,1,0:T(8,128)S(1)}, f32[1,16,128]{2,1,0:T(8,128)S(1)}, u32[]{:S(2)}, u32[]{:S(2)}) collective-permute-start(f32[1,16,128]{2,1,0:T(8,128)S(1)} %get-tuple-element.187), channel_id=1, source_target_pairs={{4,0},{8,4},{12,8},{16,12},{20,16},{24,20},{28,24},{32,28},{36,32}... | collective-permute-start | bytes 24584 | tf_op jit(solution)/shard_map/ppermute | solution.py:56
  199.6 10.1 %collective-permute-start.13 = (f32[1,16,128]{2,1,0:T(8,128)S(1)}, f32[1,16,128]{2,1,0:T(8,128)S(1)}, u32[]{:S(2)}, u32[]{:S(2)}) collective-permute-start(f32[1,16,128]{2,1,0:T(8,128)S(1)} %get-tuple-element.186), channel_id=1, source_target_pairs={{0,4},{4,8},{8,12},{12,16},{16,20},{20,24},{24,28},{28,32},{32,36}... | collective-permute-start | bytes 24584 | tf_op jit(solution)/shard_map/ppermute | solution.py:54
  205.2 7.9 %collective-permute-start.3 = (f32[6,16,1]{2,1,0:T(8,128)S(1)}, f32[6,16,1]{2,1,0:T(8,128)S(1)}, u32[]{:S(2)}, u32[]{:S(2)}) collective-permute-start(f32[6,16,1]{2,1,0:T(8,128)S(1)} %get-tuple-element.144), channel_id=1, source_target_pairs={{0,1},{1,2},{2,3},{4,5},{5,6},{6,7},{8,9},{9,10},{10,11},{12,13},{... | collective-permute-start | bytes 1160 | tf_op jit(solution)/shard_map/ppermute | solution.py:54
  206.5 6.6 %collective-permute-start.2 = (f32[6,16,1]{2,1,0:T(8,128)S(1)}, f32[6,16,1]{2,1,0:T(8,128)S(1)}, u32[]{:S(2)}, u32[]{:S(2)}) collective-permute-start(f32[6,16,1]{2,1,0:T(8,128)S(1)} %get-tuple-element.145), channel_id=1, source_target_pairs={{1,0},{2,1},{3,2},{5,4},{6,5},{7,6},{9,8},{10,9},{11,10},{13,12},{... | collective-permute-start | bytes 1160 | tf_op jit(solution)/shard_map/ppermute | solution.py:56
  209.8 19.6 %collective-permute-start.15 = (f32[6,16,1]{2,1,0:T(8,128)S(1)}, f32[6,16,1]{2,1,0:T(8,128)S(1)}, u32[]{:S(2)}, u32[]{:S(2)}) collective-permute-start(f32[6,16,1]{2,1,0:T(8,128)S(1)} %get-tuple-element.136), channel_id=1, source_target_pairs={{0,1},{1,2},{2,3},{4,5},{5,6},{6,7},{8,9},{9,10},{10,11},{12,13},{... | collective-permute-start | bytes 1160 | tf_op jit(solution)/shard_map/ppermute | solution.py:54
  211.7 17.8 %collective-permute-start.14 = (f32[6,16,1]{2,1,0:T(8,128)S(1)}, f32[6,16,1]{2,1,0:T(8,128)S(1)}, u32[]{:S(2)}, u32[]{:S(2)}) collective-permute-start(f32[6,16,1]{2,1,0:T(8,128)S(1)} %get-tuple-element.137), channel_id=1, source_target_pairs={{1,0},{2,1},{3,2},{5,4},{6,5},{7,6},{9,8},{10,9},{11,10},{13,12},{... | collective-permute-start | bytes 1160 | tf_op jit(solution)/shard_map/ppermute | solution.py:56
  218.4 13.2 %collective-permute-start.5 = (f32[26,1,16,128]{3,2,1,0:T(8,128)S(1)}, f32[26,1,16,128]{3,2,1,0:T(8,128)S(1)}, u32[]{:S(2)}, u32[]{:S(2)}) collective-permute-start(f32[26,1,16,128]{3,2,1,0:T(8,128)S(1)} %get-tuple-element.98), channel_id=1, source_target_pairs={{4,0},{8,4},{12,8},{16,12},{20,16},{24,20},{28,24},{32,28},{36,32}... | collective-permute-start | bytes 638984 | tf_op jit(solution)/shard_map/ppermute | solution.py:56
  227.5 13.4 %collective-permute-start.4 = (f32[26,1,16,128]{3,2,1,0:T(8,128)S(1)}, f32[26,1,16,128]{3,2,1,0:T(8,128)S(1)}, u32[]{:S(2)}, u32[]{:S(2)}) collective-permute-start(f32[26,1,16,128]{3,2,1,0:T(8,128)S(1)} %get-tuple-element.97), channel_id=1, source_target_pairs={{0,4},{4,8},{8,12},{12,16},{16,20},{20,24},{24,28},{28,32},{32,36}... | collective-permute-start | bytes 638984 | tf_op jit(solution)/shard_map/ppermute | solution.py:54
  245.1 6.6 %collective-permute-start.7 = (f32[26,6,16,1]{0,2,3,1:T(8,128)S(1)}, f32[26,6,16,1]{0,2,3,1:T(8,128)S(1)}, u32[]{:S(2)}, u32[]{:S(2)}) collective-permute-start(f32[26,6,16,1]{0,2,3,1:T(8,128)S(1)} %copy.266), channel_id=1, source_target_pairs={{1,0},{2,1},{3,2},{5,4},{6,5},{7,6},{9,8},{10,9},{11,10},{13,12},{... | collective-permute-start | bytes 29960 | tf_op jit(solution)/shard_map/ppermute | solution.py:56
  247.6 8.5 %collective-permute-start.6 = (f32[26,6,16,1]{0,2,3,1:T(8,128)S(1)}, f32[26,6,16,1]{0,2,3,1:T(8,128)}, u32[]{:S(2)}, u32[]{:S(2)}) collective-permute-start(f32[26,6,16,1]{0,2,3,1:T(8,128)S(1)} %copy.264), channel_id=1, source_target_pairs={{0,1},{1,2},{2,3},{4,5},{5,6},{6,7},{8,9},{9,10},{10,11},{12,13},{... | collective-permute-start | bytes 29960 | tf_op jit(solution)/shard_map/ppermute | solution.py:54
  260.1 8.2 %collective-permute-start.8 = (f32[1,16,128]{2,1,0:T(8,128)S(1)}, f32[1,16,128]{2,1,0:T(8,128)S(1)}, u32[]{:S(2)}, u32[]{:S(2)}) collective-permute-start(f32[1,16,128]{2,1,0:T(8,128)S(1)} %get-tuple-element.207), channel_id=1, source_target_pairs={{4,0},{8,4},{12,8},{16,12},{20,16},{24,20},{28,24},{32,28},{36,32}... | collective-permute-start | bytes 24584 | tf_op jit(solution)/shard_map/ppermute | solution.py:56
  262.0 10.1 %collective-permute-start.9 = (f32[1,16,128]{2,1,0:T(8,128)S(1)}, f32[1,16,128]{2,1,0:T(8,128)S(1)}, u32[]{:S(2)}, u32[]{:S(2)}) collective-permute-start(f32[1,16,128]{2,1,0:T(8,128)S(1)} %get-tuple-element.206), channel_id=1, source_target_pairs={{0,4},{4,8},{8,12},{12,16},{16,20},{20,24},{24,28},{28,32},{32,36}... | collective-permute-start | bytes 24584 | tf_op jit(solution)/shard_map/ppermute | solution.py:54
  285.8 9.0 %collective-permute-start.17 = (f32[4,1,16,128]{3,2,1,0:T(8,128)S(1)}, f32[4,1,16,128]{3,2,1,0:T(8,128)S(1)}, u32[]{:S(2)}, u32[]{:S(2)}) collective-permute-start(f32[4,1,16,128]{3,2,1,0:T(8,128)S(1)} %get-tuple-element.128), channel_id=1, source_target_pairs={{4,0},{8,4},{12,8},{16,12},{20,16},{24,20},{28,24},{32,28},{36,32}... | collective-permute-start | bytes 98312 | tf_op jit(solution)/shard_map/ppermute | solution.py:56
  289.1 10.3 %collective-permute-start.16 = (f32[4,1,16,128]{3,2,1,0:T(8,128)S(1)}, f32[4,1,16,128]{3,2,1,0:T(8,128)S(1)}, u32[]{:S(2)}, u32[]{:S(2)}) collective-permute-start(f32[4,1,16,128]{3,2,1,0:T(8,128)S(1)} %get-tuple-element.127), channel_id=1, source_target_pairs={{0,4},{4,8},{8,12},{12,16},{16,20},{20,24},{24,28},{28,32},{32,36}... | collective-permute-start | bytes 98312 | tf_op jit(solution)/shard_map/ppermute | solution.py:54
  307.1 7.7 %collective-permute-start.20 = (f32[26,1,16,128]{3,2,1,0:T(8,128)S(1)}, f32[26,1,16,128]{3,2,1,0:T(8,128)S(1)}, u32[]{:S(2)}, u32[]{:S(2)}) collective-permute-start(f32[26,1,16,128]{3,2,1,0:T(8,128)S(1)} %get-tuple-element.96), channel_id=1, source_target_pairs={{4,0},{8,4},{12,8},{16,12},{20,16},{24,20},{28,24},{32,28},{36,32}... | collective-permute-start | bytes 638984 | tf_op jit(solution)/shard_map/ppermute | solution.py:56
  311.2 12.3 %collective-permute-start.21 = (f32[26,1,16,128]{3,2,1,0:T(8,128)S(1)}, f32[26,1,16,128]{3,2,1,0:T(8,128)S(1)}, u32[]{:S(2)}, u32[]{:S(2)}) collective-permute-start(f32[26,1,16,128]{3,2,1,0:T(8,128)S(1)} %get-tuple-element.95), channel_id=1, source_target_pairs={{0,4},{4,8},{8,12},{12,16},{16,20},{20,24},{24,28},{28,32},{32,36}... | collective-permute-start | bytes 638984 | tf_op jit(solution)/shard_map/ppermute | solution.py:54
  327.2 14.8 %collective-permute-start.22 = (f32[26,6,16,1]{0,2,3,1:T(8,128)S(1)}, f32[26,6,16,1]{0,2,3,1:T(8,128)}, u32[]{:S(2)}, u32[]{:S(2)}) collective-permute-start(f32[26,6,16,1]{0,2,3,1:T(8,128)S(1)} %copy.296), channel_id=1, source_target_pairs={{1,0},{2,1},{3,2},{5,4},{6,5},{7,6},{9,8},{10,9},{11,10},{13,12},{... | collective-permute-start | bytes 29960 | tf_op jit(solution)/shard_map/ppermute | solution.py:56
  330.0 14.1 %collective-permute-start.23 = (f32[26,6,16,1]{0,2,3,1:T(8,128)}, f32[26,6,16,1]{0,2,3,1:T(8,128)}, u32[]{:S(2)}, u32[]{:S(2)}) collective-permute-start(f32[26,6,16,1]{0,2,3,1:T(8,128)} %copy.298), channel_id=1, source_target_pairs={{0,1},{1,2},{2,3},{4,5},{5,6},{6,7},{8,9},{9,10},{10,11},{12,13},{... | collective-permute-start | bytes 29960 | tf_op jit(solution)/shard_map/ppermute | solution.py:54
  359.6 6.1 %collective-permute-start.25 = (f32[4,1,16,128]{3,2,1,0:T(8,128)S(1)}, f32[4,1,16,128]{3,2,1,0:T(8,128)S(1)}, u32[]{:S(2)}, u32[]{:S(2)}) collective-permute-start(f32[4,1,16,128]{3,2,1,0:T(8,128)S(1)} %get-tuple-element.124), channel_id=1, source_target_pairs={{4,0},{8,4},{12,8},{16,12},{20,16},{24,20},{28,24},{32,28},{36,32}... | collective-permute-start | bytes 98312 | tf_op jit(solution)/shard_map/ppermute | solution.py:56
  361.6 10.3 %collective-permute-start.24 = (f32[4,1,16,128]{3,2,1,0:T(8,128)S(1)}, f32[4,1,16,128]{3,2,1,0:T(8,128)S(1)}, u32[]{:S(2)}, u32[]{:S(2)}) collective-permute-start(f32[4,1,16,128]{3,2,1,0:T(8,128)S(1)} %get-tuple-element.123), channel_id=1, source_target_pairs={{0,4},{4,8},{8,12},{12,16},{16,20},{20,24},{24,28},{28,32},{32,36}... | collective-permute-start | bytes 98312 | tf_op jit(solution)/shard_map/ppermute | solution.py:54
  372.0 7.9 %collective-permute-start.27 = (f32[4,6,16,1]{3,2,1,0:T(8,128)S(1)}, f32[4,6,16,1]{3,2,1,0:T(8,128)S(1)}, u32[]{:S(2)}, u32[]{:S(2)}) collective-permute-start(f32[4,6,16,1]{3,2,1,0:T(8,128)S(1)} %get-tuple-element.118), channel_id=1, source_target_pairs={{1,0},{2,1},{3,2},{5,4},{6,5},{7,6},{9,8},{10,9},{11,10},{13,12},{... | collective-permute-start | bytes 4616 | tf_op jit(solution)/shard_map/ppermute | solution.py:56
  373.3 6.6 %collective-permute-start.26 = (f32[4,6,16,1]{3,2,1,0:T(8,128)S(1)}, f32[4,6,16,1]{3,2,1,0:T(8,128)S(1)}, u32[]{:S(2)}, u32[]{:S(2)}) collective-permute-start(f32[4,6,16,1]{3,2,1,0:T(8,128)S(1)} %get-tuple-element.117), channel_id=1, source_target_pairs={{0,1},{1,2},{2,3},{4,5},{5,6},{6,7},{8,9},{9,10},{10,11},{12,13},{... | collective-permute-start | bytes 4616 | tf_op jit(solution)/shard_map/ppermute | solution.py:54
  (110 other events, 1435.9 us)
where the time goes:
time: 387 us; the launch traced here: 382 us
  other arithmetic  206 us (53%)
  starting transfers between devices  93.7 us (24%)
  waiting for transfers between devices  38.3 us (10%)
  local copies, waits for them, and re-layouts  28.9 us (7%)
  matrix products  12.2 us (3%)
    unnamed x40, other arithmetic  181 us
    ppermute x14, starting transfers between devices, padded_2(): lax.ppermute(head, axis, [((i + 1) % count, i) for i in range(ends)])  48.3 us
    ppermute x14, starting transfers between devices, padded_2(): lax.ppermute(tail, axis, [(i, (i + 1) % count) for i in range(ends)])  45.3 us
    ppermute x14, waiting for transfers between devices, padded_2(): lax.ppermute(tail, axis, [(i, (i + 1) % count) for i in range(ends)])  35 us
    dot_general x15, matrix products, spread_table(): jnp.tensordot(matrix, vectors, axes=1, precision=lax.Precision.HIGHEST)  12.2 us
  transfers between devices with their start and end apart: 28, of which 10 were waited for; matrix products, arithmetic and copies ran while one was open for 54% of the time, Pallas kernels for 0%

commit v1 on v0

v1 whole, which is shorter than its diff:
```python
import functools

import jax
import jax.numpy as jnp
import numpy as np
from jax import lax
from jax.experimental import pallas as pl
from jax.experimental.pallas import tpu as pltpu
from jax.sharding import PartitionSpec as P

DIRS = [
    (0, 0, 0), (1, 0, 0), (-1, 0, 0), (0, 1, 0), (0, -1, 0), (0, 0, 1), (0, 0, -1),
    (1, 1, 0), (-1, -1, 0), (1, -1, 0), (-1, 1, 0), (1, 0, 1), (-1, 0, -1), (1, 0, -1),
    (-1, 0, 1), (0, 1, 1), (0, -1, -1), (0, 1, -1), (0, -1, 1),
]
BACK = [0, 2, 1, 4, 3, 6, 5, 8, 7, 10, 9, 12, 11, 14, 13, 16, 15, 18, 17]
W = [1.0 / 3.0] + [1.0 / 18.0] * 6 + [1.0 / 36.0] * 12
W0, W1, W2 = 1.0 / 3.0, 1.0 / 18.0, 1.0 / 36.0
PAIRS = [(q, q + 1) for q in range(1, 19, 2)]
TO_RIGHT = [q for q in range(19) if DIRS[q][0] == 1]
TO_LEFT = [q for q in range(19) if DIRS[q][0] == -1]
RIM = 8
SHARP = 0.075
FLUID = 26
F32 = jnp.float32
VMEM_LIMIT = 40 * 2**20


def lanes():
    return lax.broadcasted_iota(jnp.int32, (16, 128), 1)


def roll(x, shift, axis):
    shift = shift % x.shape[axis]
    return x if shift == 0 else pltpu.roll(x, shift, axis)


def load_pair(ref, *at):
    *head, row = at
    return (ref[(*head, 2 * row)], ref[(*head, 2 * row + 1)])


def store_pair(ref, pair, *at):
    *head, row = at
    ref[(*head, 2 * row)] = pair[0]
    ref[(*head, 2 * row + 1)] = pair[1]


def both(fn, *pairs):
    return tuple(fn(*each) for each in zip(*pairs))


def moved(pair, step_y, step_z):
    if step_y:
        pair = both(lambda t: roll(t, -step_y, 0), pair)
    if step_z:
        a = roll(pair[0], -step_z, 1)
        b = roll(pair[1], -step_z, 1)
        edge = lanes() == (127 if step_z > 0 else 0)
        pair = (jnp.where(edge, b, a), jnp.where(edge, a, b))
    return pair


def pack(msg_ref, fields):
    lane = lanes()
    count = len(fields)
    for base in range(0, count, 8):
        acc = jnp.zeros((16, 128), F32)
        for slot, (main, rim) in enumerate(fields[base : base + 8]):
            msg_ref[base + slot] = main
            acc = jnp.where(lane // 16 == slot, roll(rim, 8 + 16 * slot, 1), acc)
        msg_ref[count + base // 8] = acc


def unpack(msg_ref, count, k):
    return (msg_ref[k], roll(msg_ref[count + k // 8], -(8 + 16 * (k % 8)), 1))


def total(values):
    out = values[0]
    for value in values[1:]:
        out = out + value
    return out


def along(step, vec):
    out = None
    for c, v in zip(step, vec):
        if c == 0:
            continue
        if out is None:
            out = v if c > 0 else -v
        else:
            out = out + v if c > 0 else out - v
    return out


def momentum_of(pops, axis):
    plus = [pops[q] for q in range(19) if DIRS[q][axis] == 1]
    minus = [pops[q] for q in range(19) if DIRS[q][axis] == -1]
    return total([a - b for a, b in zip(plus, minus)])


def state_of(phi, mom, grad, lap):
    clipped = jnp.clip(phi, 0.0, 1.0)
    rho = 0.05 + 0.95 * clipped
    omega = 1.0 / (0.6 + 0.3 * clipped)
    inv_rho = 1.0 / rho
    potential = 1.2 * phi * (phi - 1.0) * (phi - 0.5) - 0.6 * lap
    force = (
        potential * grad[0] - 0.01 * rho,
        potential * grad[1],
        potential * grad[2] - 0.02 * (rho - 0.05),
    )
    half = 0.5 * inv_rho
    vel = tuple(m + f * half for m, f in zip(mom, force))
    kappa = (1.0 - 0.5 * omega) * inv_rho
    return dict(
        phi=phi, grad=grad, omega=omega, inv_rho=inv_rho, potential=potential, force=force,
        half=half, vel=vel, kappa=kappa,
    )


def dot(a, b):
    return a[0] * b[0] + a[1] * b[1] + a[2] * b[2]


def sharpening(s):
    inv_len = lax.rsqrt(dot(s["grad"], s["grad"]) + 0.01)
    return SHARP * s["phi"] * (1.0 - s["phi"]) * inv_len, inv_len


def carried_of(s, axis):
    sharp, _ = sharpening(s)
    return s["phi"] * s["vel"][axis] + sharp * s["grad"][axis]


def post_flow(pops, fluid, pressure, s, wanted):
    vel, force, omega, kappa = s["vel"], s["force"], s["omega"], s["kappa"]
    base = omega * (pressure - 1.5 * dot(vel, vel)) - 3.0 * kappa * dot(vel, force)
    odd_vec = tuple(3.0 * (omega * v + kappa * f) for v, f in zip(vel, force))
    even_vec = tuple(4.5 * omega * v + 9.0 * kappa * f for v, f in zip(vel, force))
    keep = 1.0 - omega
    out = {}
    if 0 in wanted:
        out[0] = jnp.where(fluid, keep * pops[0] + W0 * base, pops[0])
    for q, r in PAIRS:
        if q not in wanted and r not in wanted:
            continue
        step = DIRS[q]
        even = base + along(step, vel) * along(step, even_vec)
        odd = along(step, odd_vec)
        if q in wanted:
            out[q] = jnp.where(fluid, keep * pops[q] + W[q] * (even + odd), pops[r])
        if r in wanted:
            out[r] = jnp.where(fluid, keep * pops[r] + W[q] * (even - odd), pops[q])
    return out


def post_phase(pops, fluid, s, wanted):
    sharp, _ = sharpening(s)
    carried = tuple(s["phi"] * v + sharp * g for v, g in zip(s["vel"], s["grad"]))
    out = {}
    for q in wanted:
        if q == 0:
            out[q] = jnp.where(fluid, 0.3125 * s["phi"] - 0.25 * pops[0], pops[0])
        else:
            equil = 0.15625 * s["phi"] + 0.625 * along(DIRS[q], carried)
            out[q] = jnp.where(fluid, equil - 0.25 * pops[q], pops[BACK[q]])
    return out


def moments_of(adj):
    zero = None
    m0, m1 = [], [[], [], []]
    m2 = {}
    if 0 in adj:
        m0.append(W0 * adj[0])
    groups = {W1: [], W2: []}
    for q in range(1, 19):
        if q not in adj:
            continue
        a = adj[q]
        w = W[q]
        groups[w].append(a)
    for w, items in groups.items():
        if items:
            m0.append(w * total(items))

    def weighted(terms):
        parts = []
        for w in (W1, W2):
            mine = [(sign, a) for ww, sign, a in terms if ww == w]
            if not mine:
                continue
            acc = None
            for sign, a in mine:
                if acc is None:
                    acc = a if sign > 0 else -a
                else:
                    acc = acc + a if sign > 0 else acc - a
            parts.append(w * acc)
        return total(parts) if parts else None

    for i in range(3):
        m1[i] = weighted([(W[q], DIRS[q][i], adj[q]) for q in range(1, 19) if q in adj and DIRS[q][i]])
    for i in range(3):
        for j in range(i, 3):
            m2[(i, j)] = weighted(
                [
                    (W[q], DIRS[q][i] * DIRS[q][j], adj[q])
                    for q in range(1, 19)
                    if q in adj and DIRS[q][i] and DIRS[q][j]
                ]
            )
            m2[(j, i)] = m2[(i, j)]
    return total(m0), m1, m2


def apply_m2(m2, vec):
    out = []
    for i in range(3):
        terms = [m2[(i, j)] * vec[j] for j in range(3) if m2[(i, j)] is not None]
        out.append(total(terms))
    return out


def pull_stencil(s, m0, m1, m2, n1):
    vel, force = s["vel"], s["force"]
    omega, kappa, half = s["omega"], s["kappa"], s["half"]
    m2v = apply_m2(m2, vel)
    m2f = apply_m2(m2, force)
    m0_3 = 3.0 * m0
    lean = []
    for i in range(3):
        term = 9.0 * m2v[i] - m0_3 * vel[i]
        lean.append(term if m1[i] is None else term + 3.0 * m1[i])
    push = [9.0 * m2f[i] - m0_3 * force[i] for i in range(3)]
    d_vel = [omega * a + kappa * b for a, b in zip(lean, push)]
    if n1 is not None:
        five_phi = 5.0 * s["phi"]
        d_vel = [d + five_phi * n for d, n in zip(d_vel, n1)]
    d_force = [kappa * a + half * d for a, d in zip(lean, d_vel)]
    d_potential = dot(d_force, s["grad"])
    d_grad = [s["potential"] * x for x in d_force]
    if n1 is not None:
        sharp, inv_len = sharpening(s)
        tilt = dot(s["grad"], n1) * inv_len * inv_len
        sharp5 = 5.0 * sharp
        d_grad = [d + sharp5 * (n - g * tilt) for d, n, g in zip(d_grad, n1, s["grad"])]
    d_lap = -0.6 * d_potential
    return d_grad, d_lap, d_potential, d_force, d_vel, m2v, m2f


def pull_all(s, pressure, adj, kept, m0, m1, m2, n0, n1):
    d_grad, d_lap, d_potential, d_force, d_vel, m2v, m2f = pull_stencil(s, m0, m1, m2, n1)
    phi, vel, force = s["phi"], s["vel"], s["force"]
    omega, kappa, inv_rho, half = s["omega"], s["kappa"], s["inv_rho"], s["half"]
    relaxed = m0 * (pressure - 1.5 * dot(vel, vel)) + 3.0 * dot(m1, vel) + 4.5 * dot(m2v, vel)
    forced = 3.0 * dot(m1, force) - 3.0 * m0 * dot(vel, force) + 9.0 * dot(m2v, force)
    d_omega = relaxed - kept - 0.5 * inv_rho * forced
    d_rho = (
        -kappa * inv_rho * forced
        - 0.01 * d_force[0]
        - 0.02 * d_force[2]
        - dot(d_vel, force) * half * inv_rho
    )
    d_clip = 0.95 * d_rho - 0.3 * omega * omega * d_omega
    inside = jnp.where((phi > 0.0) & (phi < 1.0), 1.0, jnp.where((phi == 0.0) | (phi == 1.0), 0.5, 0.0))
    d_phi = d_potential * (1.2 * (3.0 * phi * (phi - 1.0) + 0.5)) + d_clip * inside
    if n1 is not None:
        _, inv_len = sharpening(s)
        d_phi = d_phi + 1.25 * n0 + 5.0 * (
            dot(n1, vel) + SHARP * (1.0 - 2.0 * phi) * inv_len * dot(n1, s["grad"])
        )
    d_pressure = omega * m0
    keep = 1.0 - omega
    d_flow = {0: keep * adj[0] + d_pressure}
    for q, r in PAIRS:
        lift = along(DIRS[q], d_vel)
        d_flow[q] = keep * adj[q] + (d_pressure + lift)
        d_flow[r] = keep * adj[r] + (d_pressure - lift)
    return d_flow, d_phi, d_grad, d_lap


def gradients(behind, centre, ahead):
    ahead_y, behind_y = moved(centre, 1, 0), moved(centre, -1, 0)
    ahead_z, behind_z = moved(centre, 0, 1), moved(centre, 0, -1)
    diff = lambda a, b: 0.5 * (a - b)
    lap = both(
        lambda a, b, c, d, e, f, m: a + b + c + d + e + f - 6.0 * m,
        ahead, behind, ahead_y, behind_y, ahead_z, behind_z, centre,
    )
    return both(diff, ahead, behind), both(diff, ahead_y, behind_y), both(diff, ahead_z, behind_z), lap


def behind_part(d_grad, d_lap):
    return 0.5 * d_grad + d_lap


def ahead_part(d_grad, d_lap):
    return d_lap - 0.5 * d_grad


def rim_kernel(g_ref, f_ref, solid_ref, up_ref, down_ref):
    lane = lanes()

    def row(x, carry):
        for tile in range(2):
            up = jnp.zeros((16, 128), F32)
            down = jnp.zeros((16, 128), F32)
            for slot in range(16):
                k = 16 * tile + slot
                if k > FLUID:
                    continue
                if k < 7:
                    cells = g_ref[k, x]
                elif k < 26:
                    cells = f_ref[k - 7, x]
                else:
                    cells = 1.0 - solid_ref[x].astype(F32)
                mine = lane // RIM == slot
                up = jnp.where(mine, roll(cells, 8 * slot + 8, 1), up)
                down = jnp.where(mine, roll(cells, 8 * slot, 1), down)
            up_ref[tile, x] = up
            down_ref[tile, x] = down
        return carry

    lax.fori_loop(0, 4, row, 0)


def ring_kernel(g_ref, f_ref, solid_ref, below_ref, above_ref, s_ref, right_ref, left_ref, phase_ref):
    lane = lanes()

    def row(x, carry):
        sums = [None, None]
        for k in range(27):
            if k < 7:
                cells = g_ref[k, x]
            elif k < 26:
                cells = f_ref[k - 7, x]
            else:
                cells = 1.0 - solid_ref[x].astype(F32)
            slot = k % 16
            above = roll(above_ref[k // 16, x], -8 * slot, 1)
            below = roll(below_ref[k // 16, x], 120 - 8 * slot, 1)
            rim = jnp.where(lane < 64, above, below)
            s_ref[k, 2 * x] = cells
            s_ref[k, 2 * x + 1] = rim
            if k < 7:
                sums = [a if b is None else a + b for a, b in zip((cells, rim), sums)]
        phase_ref[2 * x] = sums[0]
        phase_ref[2 * x + 1] = sums[1]
        return carry

    lax.fori_loop(0, 4, row, 0)

    for msg_ref, edge, inner, crossing in ((right_ref, 3, 2, TO_RIGHT), (left_ref, 0, 1, TO_LEFT)):
        pops = [load_pair(s_ref, 7 + q, edge) for q in range(19)]
        fluid = load_pair(s_ref, FLUID, edge)
        fields = [
            both(lambda a, b, f: jnp.where(f > 0.5, a, b), pops[q], pops[BACK[q]], fluid) for q in crossing
        ]
        fields += [load_pair(s_ref, q, edge) for q in range(7)]
        fields.append(both(lambda *p: total(p), *pops))
        for axis in range(3):
            fields.append(both(lambda *p: momentum_of(p, axis), *pops))
        fields.append(fluid)
        grads = gradients(*(load_pair(phase_ref, inner + d) for d in (-1, 0, 1)))
        phi = load_pair(phase_ref, inner)
        inner_pops = [load_pair(s_ref, 7 + q, inner) for q in range(19)]
        out = 1 if edge == 3 else 2
        crossing_phase = []
        for t in range(2):
            mom = [momentum_of([p[t] for p in inner_pops], 0)] + [jnp.zeros((16, 128), F32)] * 2
            s = state_of(phi[t], mom, tuple(g[t] for g in grads[:3]), grads[3][t])
            equil = 0.15625 * phi[t] + (0.625 if out == 1 else -0.625) * carried_of(s, 0)
            crossing_phase.append(
                jnp.where(
                    s_ref[FLUID, 2 * inner + t] > 0.5,
                    equil - 0.25 * s_ref[out, 2 * inner + t],
                    s_ref[BACK[out], 2 * inner + t],
                )
            )
        fields.append(tuple(crossing_phase))
        fields.append(phi)
        pack(msg_ref, fields)


PROBE_CHUNK = 2048


def probe_kernel(corner_ref, cells_ref, weights_ref, out_ref, acc_ref):
    first_x = corner_ref[0]
    first_z = corner_ref[1]
    acc_ref[...] = jnp.zeros_like(acc_ref)
    across = lax.broadcasted_iota(jnp.int32, (96, PROBE_CHUNK), 0)
    height = lax.broadcasted_iota(jnp.int32, (144, PROBE_CHUNK), 0)

    def chunk(i, carry):
        at = pl.ds(pl.multiple_of(i * PROBE_CHUNK, PROBE_CHUNK), PROBE_CHUNK)
        x = cells_ref[0:1, at] - (first_x - 1)
        y = cells_ref[1:2, at]
        z = cells_ref[2:3, at] - first_z
        code_xy = jnp.where((x >= 0) & (x < 6), x * 16 + y, -1)
        code_z = jnp.where((z >= -RIM) & (z < 128 + RIM), jnp.where(z >= 0, z, z + 144), -1)
        weight = weights_ref[0:1, at]
        high = weight.astype(jnp.bfloat16).astype(F32)
        low = weight - high
        hit = across == code_xy
        lhs = jnp.concatenate([jnp.where(hit, high, 0.0), jnp.where(hit, low, 0.0)], axis=0).astype(jnp.bfloat16)
        rhs = jnp.where(height == code_z, 1.0, 0.0).astype(jnp.bfloat16)
        acc_ref[...] += lax.dot_general(lhs, rhs, (((1,), (1,)), ((), ())), preferred_element_type=F32)
        return carry

    lax.fori_loop(0, cells_ref.shape[1] // PROBE_CHUNK, chunk, 0)
    lane = lanes()
    for x in range(6):
        rows = pl.ds(16 * x, 16)
        lows = pl.ds(96 + 16 * x, 16)
        out_ref[2 * x] = acc_ref[rows, 0:128] + acc_ref[lows, 0:128]
        rim = acc_ref[rows, 128:144] + acc_ref[lows, 128:144]
        rim = jnp.concatenate([rim, jnp.zeros((16, 112), F32)], axis=1)
        out_ref[2 * x + 1] = jnp.where(lane < RIM, rim, jnp.where(lane >= 120, roll(rim, 112, 1), 0.0))


N_FIRST = 19
N_SECOND = 8


def chunks(rows_from, rows_to, body):
    def step(i, carry):
        for h in range(2):
            body(i, slice(8 * h, 8 * h + 8))
        return carry

    lax.fori_loop(2 * rows_from, 2 * rows_to, step, 0)


def middle_kernel(
    s_ref, from_left_ref, from_right_ref, seed_ref,
    prim_ref, adj_ref, gamma_ref, edges_ref, to_right_ref, to_left_ref,
    phase_ref, post_ref, phase_mid_ref, grad_mid_ref, seeds_ref, back_ref, dphi_ref,
):
    sides = ((from_left_ref, 0, -2), (from_right_ref, 5, 5))
    for row in range(4):
        total_pair = both(lambda *p: total(p), *[load_pair(s_ref, q, row) for q in range(7)])
        store_pair(phase_ref, total_pair, row + 2)
    for msg_ref, at, _ in sides:
        got = [unpack(msg_ref, N_FIRST, k) for k in range(N_FIRST)]
        store_pair(phase_ref, both(lambda *p: total(p), *got[5:12]), at + 1)
        store_pair(phase_ref, got[18], 0 if at == 0 else 7)
        for i in range(4):
            store_pair(prim_ref, got[12 + i], 5 + i, at)
        store_pair(prim_ref, got[16], 9, at)
        crossing = TO_RIGHT if at == 0 else TO_LEFT
        for q, pair in zip(crossing, got[:5]):
            store_pair(post_ref, pair, 7 + q, at)
        for q in range(7):
            store_pair(post_ref, got[5 + q], q, at)
    for row in range(6):
        grads = gradients(*(load_pair(phase_ref, row + d) for d in (0, 1, 2)))
        store_pair(prim_ref, load_pair(phase_ref, row + 1), 0, row)
        for i in range(4):
            store_pair(prim_ref, grads[i], 1 + i, row)

    def prim_at(i, h):
        vals = [prim_ref[k, i, h, :] for k in range(10)]
        s = state_of(vals[0], vals[6:9], tuple(vals[1:4]), vals[4])
        return s, vals[5], vals[9] > 0.5

    def forward(i, h):
        g = [s_ref[q, i, h, :] for q in range(7)]
        f = [s_ref[7 + q, i, h, :] for q in range(19)]
        pressure = total(f)
        at = i + 2
        prim_ref[5, at, h, :] = pressure
        for axis in range(3):
            prim_ref[6 + axis, at, h, :] = momentum_of(f, axis)
        prim_ref[9, at, h, :] = s_ref[FLUID, i, h, :]
        s, pressure, fluid = prim_at(at, h)
        for q, v in post_flow(f, fluid, pressure, s, range(19)).items():
            post_ref[7 + q, at, h, :] = v
        for q, v in post_phase(g, fluid, s, range(7)).items():
            post_ref[q, at, h, :] = v

    chunks(0, 4, forward)

    for at, crossing, out in ((0, TO_RIGHT, 1), (5, TO_LEFT, 2)):

        def edge(i, h, crossing=crossing, out=out):
            s, pressure, fluid = prim_at(i, h)
            f = {q: post_ref[7 + q, i, h, :] for q in crossing}
            pops = {}
            for q in crossing:
                pops[q] = f[q]
                pops[BACK[q]] = f[q]
            for q, v in post_flow(pops, fluid, pressure, s, crossing).items():
                post_ref[7 + q, i, h, :] = v
            g = [post_ref[q, i, h, :] for q in range(7)]
            for q, v in post_phase(g, fluid, s, [0, 3, 4, 5, 6, out]).items():
                post_ref[q, i, h, :] = v

        chunks(at, at + 1, edge)

    for q in range(19):
        _, cy, cz = DIRS[q]
        if cy == 0 and cz == 0:
            continue
        rows = range(0, 6)
        for row in rows:
            here = row - 1 + DIRS[q][0]
            if 0 <= here < 4:
                store_pair(post_ref, moved(load_pair(post_ref, 7 + q, row), -cy, -cz), 7 + q, row)
    for row in range(6):
        parts = [load_pair(post_ref, 0, row)]
        for q in range(3, 7):
            parts.append(moved(load_pair(post_ref, q, row), -DIRS[q][1], -DIRS[q][2]))
        if row == 0:
            parts.append(unpack(from_left_ref, N_FIRST, 17))
        else:
            parts.append(load_pair(post_ref, 1, row - 1))
        if row == 5:
            parts.append(unpack(from_right_ref, N_FIRST, 17))
        else:
            parts.append(load_pair(post_ref, 2, row + 1))
        store_pair(phase_mid_ref, both(lambda *p: total(p), *parts), row)
    for row in range(4):
        grads = gradients(*(load_pair(phase_mid_ref, row + d) for d in (0, 1, 2)))
        for i in range(4):
            store_pair(grad_mid_ref, grads[i], i, row)
    shifts = sorted({(c[1], c[2]) for c in DIRS})
    for n, (cy, cz) in enumerate(shifts):
        for row in range(6):
            store_pair(seeds_ref, moved(load_pair(seed_ref, row), cy, cz), n, row)

    def backward(i, h):
        f = [post_ref[7 + q, i + 2 - 2 * DIRS[q][0], h, :] for q in range(19)]
        adj = [seeds_ref[shifts.index(DIRS[q][1:]), i + 2 + 2 * DIRS[q][0], h, :] for q in range(19)]
        fluid = s_ref[FLUID, i, h, :] > 0.5
        phi = phase_mid_ref[i + 2, h, :]
        pressure = total(f)
        mom = [momentum_of(f, axis) for axis in range(3)]
        s = state_of(phi, mom, tuple(grad_mid_ref[k, i, h, :] for k in range(3)), grad_mid_ref[3, i, h, :])
        kept = total([a * b for a, b in zip(adj, f)])
        m0, m1, m2 = moments_of(dict(enumerate(adj)))
        d_flow, d_phi, d_grad, d_lap = pull_all(s, pressure, adj, kept, m0, m1, m2, None, None)
        for q in range(19):
            adj_ref[q, i, h, :] = jnp.where(fluid, d_flow[q], adj[BACK[q]])
        dphi_ref[i, h, :] = jnp.where(fluid, d_phi, 0.0)
        for k in range(3):
            back_ref[k, i, h, :] = jnp.where(fluid, d_grad[k], 0.0)
        back_ref[3, i, h, :] = jnp.where(fluid, d_lap, 0.0)

    chunks(0, 4, backward)

    for q in range(19):
        _, cy, cz = DIRS[q]
        if cy or cz:
            for row in range(4):
                store_pair(adj_ref, moved(load_pair(adj_ref, q, row), cy, cz), q, row)

    for row in range(4):
        store_pair(gamma_ref, stencil_back(back_ref, dphi_ref, row), row)
    edge_parts = []
    for row, part in ((0, ahead_part), (3, behind_part)):
        pair = both(part, load_pair(back_ref, 0, row), load_pair(back_ref, 3, row))
        store_pair(edges_ref, pair, 0 if row == 0 else 1)
        edge_parts.append(pair)

    for msg_ref, row, out_dirs, part, sign, edge_pair in (
        (to_right_ref, 3, TO_RIGHT, behind_part, -1.0, edge_parts[1]),
        (to_left_ref, 0, TO_LEFT, ahead_part, 1.0, edge_parts[0]),
    ):
        gamma = load_pair(gamma_ref, row)
        next_gamma = load_pair(gamma_ref, row - 1 if row == 3 else row + 1)
        n1 = turn_gamma(both(lambda a: sign * a, next_gamma), gamma)
        partial = []
        for t in range(2):
            vals = [prim_ref[k, 2 * (row + 1) + t] for k in range(10)]
            s = state_of(vals[0], vals[6:9], tuple(vals[1:4]), vals[4])
            adj = {
                q: adj_ref[q, 2 * (row + DIRS[q][0]) + t] for q in range(19) if q not in out_dirs
            }
            m0, m1, m2 = moments_of(adj)
            d_grad, d_lap = pull_stencil(s, m0, m1, m2, [n[t] for n in n1])[:2]
            partial.append(jnp.where(vals[9] > 0.5, part(d_grad[0], d_lap), 0.0))
        back_dirs = TO_LEFT if row == 3 else TO_RIGHT
        fields = [load_pair(adj_ref, q, row) for q in back_dirs]
        fields += [gamma, edge_pair, tuple(partial)]
        pack(msg_ref, fields)


def turn_gamma(along_x, centre):
    diff = lambda a, b: 0.125 * (a - b)
    return (
        both(lambda a: 0.125 * a, along_x),
        both(diff, moved(centre, 1, 0), moved(centre, -1, 0)),
        both(diff, moved(centre, 0, 1), moved(centre, 0, -1)),
    )


def stencil_back(back_ref, start_ref, row, first=None, last=None):
    gy, gz, lap = (load_pair(back_ref, k, row) for k in (1, 2, 3))
    fold = lambda s, l, gyb, gya, lyb, lya, gzb, gza, lzb, lza: (
        s - 6.0 * l + 0.5 * (gyb - gya) + lyb + lya + 0.5 * (gzb - gza) + lzb + lza
    )
    out = both(
        fold, load_pair(start_ref, row), lap,
        moved(gy, -1, 0), moved(gy, 1, 0), moved(lap, -1, 0), moved(lap, 1, 0),
        moved(gz, 0, -1), moved(gz, 0, 1), moved(lap, 0, -1), moved(lap, 0, 1),
    )
    add = lambda a, b: a + b
    if row > 0:
        out = both(add, out, both(behind_part, load_pair(back_ref, 0, row - 1), load_pair(back_ref, 3, row - 1)))
    elif first is not None:
        out = both(add, out, first)
    if row < 3:
        out = both(add, out, both(ahead_part, load_pair(back_ref, 0, row + 1), load_pair(back_ref, 3, row + 1)))
    elif last is not None:
        out = both(add, out, last)
    return out


def last_kernel(
    s_ref, prim_ref, adj_ref, gamma_ref, edges_ref, from_left_ref, from_right_ref,
    out_g_ref, out_f_ref,
    adj_wide_ref, gamma_wide_ref, turn_ref, turned_ref, back_ref, dphi_ref,
):
    add = lambda a, b: a + b
    got_left = [unpack(from_left_ref, N_SECOND, k) for k in range(N_SECOND)]
    got_right = [unpack(from_right_ref, N_SECOND, k) for k in range(N_SECOND)]
    own_first = load_pair(edges_ref, 0)
    own_last = load_pair(edges_ref, 1)
    for row in range(1, 3):
        store_pair(gamma_wide_ref, load_pair(gamma_ref, row), row + 1)
    store_pair(gamma_wide_ref, both(add, load_pair(gamma_ref, 0), got_left[6]), 1)
    store_pair(gamma_wide_ref, both(add, load_pair(gamma_ref, 3), got_right[6]), 4)
    store_pair(gamma_wide_ref, both(add, got_left[5], own_first), 0)
    store_pair(gamma_wide_ref, both(add, got_right[5], own_last), 5)
    for q, pair in zip(TO_LEFT, got_left[:5]):
        store_pair(adj_wide_ref, pair, q, 0)
    for q, pair in zip(TO_RIGHT, got_right[:5]):
        store_pair(adj_wide_ref, pair, q, 1)
    for row in range(4):
        centre = load_pair(gamma_wide_ref, row + 1)
        for n, (cy, cz) in enumerate(((1, 0), (-1, 0), (0, 1), (0, -1))):
            store_pair(turned_ref, moved(centre, cy, cz), n, row)

    edge_parts = []
    for got, prim_row, row, own, out_dirs, part, sign in (
        (got_left, 0, 0, own_first, TO_RIGHT, behind_part, 1.0),
        (got_right, 5, 3, own_last, TO_LEFT, ahead_part, -1.0),
    ):
        gamma = load_pair(gamma_wide_ref, row + 1)
        n1 = turn_gamma(both(lambda a: sign * a, gamma), own)
        pair = []
        for t in range(2):
            vals = [prim_ref[k, 2 * prim_row + t] for k in range(10)]
            s = state_of(vals[0], vals[6:9], tuple(vals[1:4]), vals[4])
            adj = {q: adj_ref[q, 2 * row + t] for q in out_dirs}
            m0, m1, m2 = moments_of(adj)
            d_grad, d_lap = pull_stencil(s, m0, m1, m2, [n[t] for n in n1])[:2]
            pair.append(got[7][t] + jnp.where(vals[9] > 0.5, part(d_grad[0], d_lap), 0.0))
        edge_parts.append(tuple(pair))

    def gathered(row, t, h):
        adj = []
        for q in range(19):
            at = row + DIRS[q][0]
            if at < 0:
                adj.append(adj_wide_ref[q, t, h, :])
            elif at > 3:
                adj.append(adj_wide_ref[q, 2 + t, h, :])
            else:
                adj.append(adj_ref[q, 2 * at + t, h, :])
        i = 2 * row + t
        phase_adj = [
            gamma_wide_ref[i + 2, h, :],
            gamma_wide_ref[i + 4, h, :],
            gamma_wide_ref[i, h, :],
        ] + [turned_ref[n, i, h, :] for n in range(4)]
        vals = [prim_ref[k, i + 2, h, :] for k in range(10)]
        s = state_of(vals[0], vals[6:9], tuple(vals[1:4]), vals[4])
        n1 = [0.125 * (phase_adj[a] - phase_adj[a + 1]) for a in (1, 3, 5)]
        return adj, phase_adj, s, vals[5], vals[9] > 0.5, n1

    for row in range(4):
        for h in (slice(0, 8), slice(8, 16)):
            adj, phase_adj, s, pressure, fluid, n1 = gathered(row, 0, h)
            kept = total([a * s_ref[7 + q, 2 * row, h, :] for q, a in enumerate(adj)])
            n0 = 0.25 * phase_adj[0] + 0.125 * total(phase_adj[1:])
            m0, m1, m2 = moments_of(dict(enumerate(adj)))
            d_flow, d_phi, d_grad, d_lap = pull_all(s, pressure, adj, kept, m0, m1, m2, n0, n1)
            for q in range(19):
                out_f_ref[q, row, h, :] = jnp.where(fluid, d_flow[q], adj[BACK[q]])
            dphi_ref[2 * row, h, :] = jnp.where(fluid, d_phi, 0.0)
            for k in range(3):
                back_ref[k, 2 * row, h, :] = jnp.where(fluid, d_grad[k], 0.0)
            back_ref[3, 2 * row, h, :] = jnp.where(fluid, d_lap, 0.0)

            adj, phase_adj, s, pressure, fluid, n1 = gathered(row, 1, h)
            m0, m1, m2 = moments_of(dict(enumerate(adj)))
            d_grad, d_lap = pull_stencil(s, m0, m1, m2, n1)[:2]
            for k in range(3):
                back_ref[k, 2 * row + 1, h, :] = jnp.where(fluid, d_grad[k], 0.0)
            back_ref[3, 2 * row + 1, h, :] = jnp.where(fluid, d_lap, 0.0)
            dphi_ref[2 * row + 1, h, :] = jnp.zeros((8, 128), F32)

    for row in range(4):
        base = stencil_back(back_ref, dphi_ref, row, edge_parts[0], edge_parts[1])[0]
        fluid = prim_ref[9, 2 * row + 2] > 0.5
        d_phi = dphi_ref[2 * row]
        rest = base - d_phi
        i = 2 * row
        phase_adj = [gamma_wide_ref[i + 2], gamma_wide_ref[i + 4], gamma_wide_ref[i]]
        phase_adj += [turned_ref[n, i] for n in range(4)]
        for q in range(7):
            out_g_ref[q, row] = jnp.where(fluid, base - 0.25 * phase_adj[q], rest + phase_adj[BACK[q]])


def call(kernel, outs, scratch=(), flops=0, n_smem=0, n_in=0, name=None):
    vmem = pl.BlockSpec(memory_space=pltpu.VMEM)
    smem = pl.BlockSpec(memory_space=pltpu.SMEM)
    return pl.pallas_call(
        kernel,
        out_shape=[jax.ShapeDtypeStruct(shape, F32) for shape in outs],
        in_specs=[smem] * n_smem + [vmem] * n_in,
        out_specs=[vmem] * len(outs),
        scratch_shapes=[pltpu.VMEM(shape, F32) for shape in scratch],
        compiler_params=pltpu.CompilerParams(vmem_limit_bytes=VMEM_LIMIT),
        cost_estimate=pl.CostEstimate(flops=flops, bytes_accessed=flops // 8, transcendentals=0),
        name=name,
    )


def to_ahead(x, axis):
    count = lax.axis_size(axis)
    return lax.ppermute(x, axis, [(i, i + 1) for i in range(count - 1)])


def to_behind(x, axis):
    count = lax.axis_size(axis)
    return lax.ppermute(x, axis, [(i + 1, i) for i in range(count - 1)])


def shards(phase_init, flow_init, solid_mask, sensor_cells, sensor_weights):
    size_x, layers, size_z = solid_mask.shape
    corner = jnp.stack([lax.axis_index("tile") * size_x, lax.axis_index("vert") * size_z]).astype(jnp.int32)
    tile = (16, 128)
    up, down = call(rim_kernel, [(2, 4) + tile] * 2, n_in=3, flops=10**6, name="rim")(
        phase_init, flow_init, solid_mask
    )
    below = to_ahead(up, "vert")
    above = to_behind(down, "vert")
    state, right, left = call(
        ring_kernel, [(27, 8) + tile, (22,) + tile, (22,) + tile], scratch=[(8,) + tile], n_in=5, flops=10**7,
        name="ring",
    )(phase_init, flow_init, solid_mask, below, above)
    from_left = to_ahead(right, "tile")
    from_right = to_behind(left, "tile")
    (seed,) = call(probe_kernel, [(12,) + tile], scratch=[(192, 144)], n_smem=1, n_in=2, flops=2 * 10**9, name="probes")(
        corner, sensor_cells, sensor_weights.reshape(1, -1)
    )
    prim, adj, gamma, edges, right2, left2 = call(
        middle_kernel,
        [(10, 12) + tile, (19, 8) + tile, (8,) + tile, (4,) + tile, (9,) + tile, (9,) + tile],
        scratch=[
            (16,) + tile, (26, 12) + tile, (12,) + tile, (4, 8) + tile, (9, 12) + tile, (4, 8) + tile, (8,) + tile,
        ],
        n_in=4, flops=10**8, name="middle",
    )(state, from_left, from_right, seed)
    from_left2 = to_ahead(right2, "tile")
    from_right2 = to_behind(left2, "tile")
    out_g, out_f = call(
        last_kernel,
        [(7, 4) + tile, (19, 4) + tile],
        scratch=[(19, 4) + tile, (12,) + tile, (1, 8) + tile, (4, 8) + tile, (4, 8) + tile, (8,) + tile],
        n_in=7, flops=10**8, name="last",
    )(state, prim, adj, gamma, edges, from_left2, from_right2)
    return out_g, out_f


def solution(mesh):
    return jax.shard_map(
        shards,
        mesh=mesh,
        in_specs=(
            P(None, "tile", None, "vert"),
            P(None, "tile", None, "vert"),
            P("tile", None, "vert"),
            P(),
            P(),
        ),
        out_specs=(P(None, "tile", None, "vert"), P(None, "tile", None, "vert")),
        check_vma=False,
    )
```

time: 387 us -> 53.4 us (0.14)
  the two profiles are of different devices: /device:TPU:24 before, /device:TPU:25 now
where the time goes in v1:
time: 53.4 us; the launch traced here: 52.9 us
  starting transfers between devices  27.1 us (51%)
  Pallas kernels  14.4 us (27%)
  local copies, waits for them, and re-layouts  5.54 us (10%)
  waiting for transfers between devices  4.96 us (9%)
  between operations  0.76 us (1%)
    ppermute x3, starting transfers between devices, to_behind(): return lax.ppermute(x, axis, [(i + 1, i) for i in range(count - 1)])  18 us
    ppermute x3, starting transfers between devices, to_ahead(): return lax.ppermute(x, axis, [(i, i + 1) for i in range(count - 1)])  9.14 us
    pallas_call x1, Pallas kernels, shards(): call(probe_kernel, [(12,) + tile], scratch=[(192, 144)], n_smem=1, n_in=2...  7.5 us
    unnamed x16, local copies, waits for them, and re-layouts  5.54 us
    ppermute x3, waiting for transfers between devices, to_behind(): return lax.ppermute(x, axis, [(i + 1, i) for i in range(count - 1)])  4.95 us
    pallas_call x1, Pallas kernels, shards(): call(middle_kernel, [(10, 12) + tile, (19, 8) + tile, (8,) + tile, (4,) +...  3.46 us
    pallas_call x1, Pallas kernels, shards(): call(last_kernel, [(7, 4) + tile, (19, 4) + tile], scratch=[(19, 4) + til...  1.78 us
  transfers between devices with their start and end apart: 6, of which 2 were waited for; matrix products, arithmetic and copies ran while one was open for 0% of the time, Pallas kernels for 14%

profile of v1, /device:TPU:25, one launch (start us, length us, event | category | flops | bytes accessed | tf_op | source)
XLA Modules:
  0.0 52.9 jit_solution(8645844151579709653)
XLA Ops:
  0.6 0.0 copy-start
  0.6 1.1 %copy-done = f32[19,4,16,128]{3,2,1,0:T(8,128)S(1)} copy-done((f32[19,4,16,128]{3,2,1,0:T(8,128)S(1)}, f32[19,4,16,128]{3,2,1,0:T(8,128)}, u32[]{:S(2)}) %copy-start) | copy-done | bytes 622616
  1.7 0.9 %copy-done.2 = f32[7,4,16,128]{3,2,1,0:T(8,128)S(1)} copy-done((f32[7,4,16,128]{3,2,1,0:T(8,128)S(1)}, f32[7,4,16,128]{3,2,1,0:T(8,128)}, u32[]{:S(2)}) %copy-start.2) | copy-done | bytes 229400
  2.6 0.8 %copy-done.4 = s32[4,16,128]{2,1,0:T(8,128)S(1)} copy-done((s32[4,16,128]{2,1,0:T(8,128)S(1)}, s32[4,16,128]{2,1,0:T(8,128)}, u32[]{:S(2)}) %copy-start.4) | copy-done | bytes 32792
  3.4 0.7 %rim.1 = (f32[2,4,16,128]{3,2,1,0:T(8,128)S(1)}, f32[2,4,16,128]{3,2,1,0:T(8,128)S(1)}) custom-call(f32[7,4,16,128]{3,2,1,0:T(8,128)S(1)} %copy-done.2, f32[19,4,16,128]{3,2,1,0:T(8,128)S(1)} %copy-done, s32[4,16,128]{2,1,0:T(8,128)S(1)} %copy-done.4), custom_call_target="tpu_custom_call" | custom-call | flops 1000000 | bytes 125000 | tf_op jit(solution)/shard_map/rim/pallas_call | solution.py:751
  4.1 3.7 %collective-permute-start = (f32[2,4,16,128]{3,2,1,0:T(8,128)S(1)}, f32[2,4,16,128]{3,2,1,0:T(8,128)S(1)}, u32[]{:S(2)}, u32[]{:S(2)}) collective-permute-start(f32[2,4,16,128]{3,2,1,0:T(8,128)S(1)} %get-tuple-element.13), channel_id=1, source_target_pairs={{0,1},{1,2},{2,3},{4,5},{5,6},{6,7},{8,9},{9,10},{10,11},{12,13},{... | collective-permute-start | bytes 196616 | tf_op jit(solution)/shard_map/ppermute | solution.py:739
  7.8 1.9 %collective-permute-start.1 = (f32[2,4,16,128]{3,2,1,0:T(8,128)S(1)}, f32[2,4,16,128]{3,2,1,0:T(8,128)S(1)}, u32[]{:S(2)}, u32[]{:S(2)}) collective-permute-start(f32[2,4,16,128]{3,2,1,0:T(8,128)S(1)} %get-tuple-element.14), channel_id=1, source_target_pairs={{1,0},{2,1},{3,2},{5,4},{6,5},{7,6},{9,8},{10,9},{11,10},{13,12},{... | collective-permute-start | bytes 196616 | tf_op jit(solution)/shard_map/ppermute | solution.py:744
  9.7 0.1 pad_add_fusion.corner_ref
  9.8 0.0 collective-permute-done.below_ref
  9.8 3.6 %collective-permute-done.1.above_ref = f32[2,4,16,128]{3,2,1,0:T(8,128)S(1)} collective-permute-done((f32[2,4,16,128]{3,2,1,0:T(8,128)S(1)}, f32[2,4,16,128]{3,2,1,0:T(8,128)S(1)}, u32[]{:S(2)}, u32[]{:S(2)}) %collective-permute-start.1) | collective-permute-done | bytes 65568 | tf_op jit(solution)/shard_map/ppermute | solution.py:744
  13.4 1.1 %copy-done.1 = f32[19,4,16,128]{3,2,1,0:T(8,128)S(1)} copy-done((f32[19,4,16,128]{3,2,1,0:T(8,128)S(1)}, f32[19,4,16,128]{3,2,1,0:T(8,128)}, u32[]{:S(2)}) %copy-start.1) | copy-done | bytes 622616
  14.5 0.9 %copy-done.3 = f32[7,4,16,128]{3,2,1,0:T(8,128)S(1)} copy-done((f32[7,4,16,128]{3,2,1,0:T(8,128)S(1)}, f32[7,4,16,128]{3,2,1,0:T(8,128)}, u32[]{:S(2)}) %copy-start.3) | copy-done | bytes 229400
  15.4 0.8 %copy-done.5 = s32[4,16,128]{2,1,0:T(8,128)S(1)} copy-done((s32[4,16,128]{2,1,0:T(8,128)S(1)}, s32[4,16,128]{2,1,0:T(8,128)}, u32[]{:S(2)}) %copy-start.5) | copy-done | bytes 32792
  16.2 0.9 %ring.1 = (f32[27,8,16,128]{3,2,1,0:T(8,128)S(1)}, f32[22,16,128]{2,1,0:T(8,128)S(1)}, f32[22,16,128]{2,1,0:T(8,128)S(1)}) custom-call(f32[7,4,16,128]{3,2,1,0:T(8,128)S(1)} %copy-done.3, f32[19,4,16,128]{3,2,1,0:T(8,128)S(1)} %copy-done.1, s32[4,16,128]{2,1,0:T(8,128)S(1)} %copy-done.5, f32[2,4,16,128]{3,2,1,0:T(8,128)S(1)} %collective-permute-done.below_ref, ...), custom_call_target="tpu_custom_call" | custom-call | flops 10000000 | bytes 1250000 | tf_op jit(solution)/shard_map/ring/pallas_call | solution.py:756
  17.1 3.5 %collective-permute-start.2 = (f32[22,16,128]{2,1,0:T(8,128)S(1)}, f32[22,16,128]{2,1,0:T(8,128)S(1)}, u32[]{:S(2)}, u32[]{:S(2)}) collective-permute-start(f32[22,16,128]{2,1,0:T(8,128)S(1)} %get-tuple-element.16), channel_id=1, source_target_pairs={{0,4},{4,8},{8,12},{12,16},{16,20},{20,24},{24,28},{28,32},{32,36}... | collective-permute-start | bytes 540680 | tf_op jit(solution)/shard_map/ppermute | solution.py:739
  20.7 8.2 %collective-permute-start.3 = (f32[22,16,128]{2,1,0:T(8,128)S(1)}, f32[22,16,128]{2,1,0:T(8,128)S(1)}, u32[]{:S(2)}, u32[]{:S(2)}) collective-permute-start(f32[22,16,128]{2,1,0:T(8,128)S(1)} %get-tuple-element.17), channel_id=1, source_target_pairs={{4,0},{8,4},{12,8},{16,12},{20,16},{24,20},{28,24},{32,28},{36,32}... | collective-permute-start | bytes 540680 | tf_op jit(solution)/shard_map/ppermute | solution.py:744
  28.9 7.5 %probes.1.seed_ref = f32[12,16,128]{2,1,0:T(8,128)S(1)} custom-call(s32[2]{0:T(128)S(1)} %pad_add_fusion.corner_ref, s32[3,32768]{1,0:T(4,128)S(1)} %copy-done.6, f32[1,32768]{1,0:T(1,128)S(1)} %bitcast.3), custom_call_target="tpu_custom_call" | custom-call | flops 2000000000 | bytes 250000000 | tf_op jit(solution)/shard_map/probes/pallas_call | solution.py:762
  36.4 0.0 collective-permute-done.2.from_left_ref
  36.4 0.0 collective-permute-done.3.from_right_ref
  36.4 3.5 %middle.1 = (f32[10,12,16,128]{3,2,1,0:T(8,128)S(1)}, f32[19,8,16,128]{3,2,1,0:T(8,128)S(1)}, f32[8,16,128]{2,1,0:T(8,128)S(1)}, f32[4,16,128]{2,1,0:T(8,128)S(1...) custom-call(f32[27,8,16,128]{3,2,1,0:T(8,128)S(1)} %get-tuple-element.15.s_ref, ...), custom_call_target="tpu_custom_call" | custom-call | flops 100000000 | bytes 12500000 | tf_op jit(solution)/shard_map/middle/pallas_call | solution.py:765
  39.9 1.9 %collective-permute-start.4 = (f32[9,16,128]{2,1,0:T(8,128)S(1)}, f32[9,16,128]{2,1,0:T(8,128)S(1)}, u32[]{:S(2)}, u32[]{:S(2)}) collective-permute-start(f32[9,16,128]{2,1,0:T(8,128)S(1)} %get-tuple-element.22), channel_id=1, source_target_pairs={{0,4},{4,8},{8,12},{12,16},{16,20},{20,24},{24,28},{28,32},{32,36}... | collective-permute-start | bytes 221192 | tf_op jit(solution)/shard_map/ppermute | solution.py:739
  41.8 7.9 %collective-permute-start.5 = (f32[9,16,128]{2,1,0:T(8,128)S(1)}, f32[9,16,128]{2,1,0:T(8,128)S(1)}, u32[]{:S(2)}, u32[]{:S(2)}) collective-permute-start(f32[9,16,128]{2,1,0:T(8,128)S(1)} %get-tuple-element.23), channel_id=1, source_target_pairs={{4,0},{8,4},{12,8},{16,12},{20,16},{24,20},{28,24},{32,28},{36,32}... | collective-permute-start | bytes 221192 | tf_op jit(solution)/shard_map/ppermute | solution.py:744
  49.7 1.4 %collective-permute-done.5.from_right_ref = f32[9,16,128]{2,1,0:T(8,128)S(1)} collective-permute-done((f32[9,16,128]{2,1,0:T(8,128)S(1)}, f32[9,16,128]{2,1,0:T(8,128)S(1)}, u32[]{:S(2)}, u32[]{:S(2)}) %collective-permute-start.5) | collective-permute-done | bytes 73760 | tf_op jit(solution)/shard_map/ppermute | solution.py:744
  51.1 1.8 %last.1 = (f32[7,4,16,128]{3,2,1,0:T(8,128)}, f32[19,4,16,128]{3,2,1,0:T(8,128)}) custom-call(f32[27,8,16,128]{3,2,1,0:T(8,128)S(1)} %get-tuple-element.15.s_ref, f32[10,12,16,128]{3,2,1,0:T(8,128)S(1)} %get-tuple-element.18.prim_ref, f32[19,8,16,128]{3,2,1,0:T(8,128)S(1)} %get-tuple-element.19.adj_ref, f32[8,16,128]{2,1,0:T(8,128)S(1)} %get-tuple-element.20.gamma_ref, ...), custom_call_target="tpu_custom_call" | custom-call | flops 100000000 | bytes 12500000 | tf_op jit(solution)/shard_map/last/pallas_call | solution.py:775
  (10 shorter events, 0.0 us)
Async XLA Ops:
  0.6 1.1 %copy-start = (f32[19,4,16,128]{3,2,1,0:T(8,128)S(1)}, f32[19,4,16,128]{3,2,1,0:T(8,128)}, u32[]{:S(2)}) copy-start(f32[19,4,16,128]{3,2,1,0:T(8,128)} %f_ref.3) | copy-start | bytes 1867780
  1.7 0.9 %copy-start.2 = (f32[7,4,16,128]{3,2,1,0:T(8,128)S(1)}, f32[7,4,16,128]{3,2,1,0:T(8,128)}, u32[]{:S(2)}) copy-start(f32[7,4,16,128]{3,2,1,0:T(8,128)} %g_ref.3) | copy-start | bytes 688132
  2.6 0.8 %copy-start.4 = (s32[4,16,128]{2,1,0:T(8,128)S(1)}, s32[4,16,128]{2,1,0:T(8,128)}, u32[]{:S(2)}) copy-start(s32[4,16,128]{2,1,0:T(8,128)} %solid_ref.3) | copy-start | bytes 98308
  3.4 25.5 %copy-start.6 = (s32[3,32768]{1,0:T(4,128)S(1)}, s32[3,32768]{1,0:T(4,128)}, u32[]{:S(2)}) copy-start(s32[3,32768]{1,0:T(4,128)} %cells_ref.1) | copy-start | bytes 1179652
  3.4 25.5 %copy-start.7 = (f32[32768]{0:T(1024)S(1)}, f32[32768]{0:T(1024)}, u32[]{:S(2)}) copy-start(f32[32768]{0:T(1024)} %param.9) | copy-start | bytes 393220
  4.1 5.7 %collective-permute-start = (f32[2,4,16,128]{3,2,1,0:T(8,128)S(1)}, f32[2,4,16,128]{3,2,1,0:T(8,128)S(1)}, u32[]{:S(2)}, u32[]{:S(2)}) collective-permute-start(f32[2,4,16,128]{3,2,1,0:T(8,128)S(1)} %get-tuple-element.13), channel_id=1, source_target_pairs={{0,1},{1,2},{2,3},{4,5},{5,6},{6,7},{8,9},{9,10},{10,11},{12,13},{... | collective-permute-start | bytes 196616 | tf_op jit(solution)/shard_map/ppermute | solution.py:739
  7.8 5.6 %collective-permute-start.1 = (f32[2,4,16,128]{3,2,1,0:T(8,128)S(1)}, f32[2,4,16,128]{3,2,1,0:T(8,128)S(1)}, u32[]{:S(2)}, u32[]{:S(2)}) collective-permute-start(f32[2,4,16,128]{3,2,1,0:T(8,128)S(1)} %get-tuple-element.14), channel_id=1, source_target_pairs={{1,0},{2,1},{3,2},{5,4},{6,5},{7,6},{9,8},{10,9},{11,10},{13,12},{... | collective-permute-start | bytes 196616 | tf_op jit(solution)/shard_map/ppermute | solution.py:744
  13.4 1.1 %copy-start.1 = (f32[19,4,16,128]{3,2,1,0:T(8,128)S(1)}, f32[19,4,16,128]{3,2,1,0:T(8,128)}, u32[]{:S(2)}) copy-start(f32[19,4,16,128]{3,2,1,0:T(8,128)} %f_ref.3) | copy-start | bytes 1867780
  14.5 0.9 %copy-start.3 = (f32[7,4,16,128]{3,2,1,0:T(8,128)S(1)}, f32[7,4,16,128]{3,2,1,0:T(8,128)}, u32[]{:S(2)}) copy-start(f32[7,4,16,128]{3,2,1,0:T(8,128)} %g_ref.3) | copy-start | bytes 688132
  15.4 0.8 %copy-start.5 = (s32[4,16,128]{2,1,0:T(8,128)S(1)}, s32[4,16,128]{2,1,0:T(8,128)}, u32[]{:S(2)}) copy-start(s32[4,16,128]{2,1,0:T(8,128)} %solid_ref.3) | copy-start | bytes 98308
  17.1 19.3 %collective-permute-start.2 = (f32[22,16,128]{2,1,0:T(8,128)S(1)}, f32[22,16,128]{2,1,0:T(8,128)S(1)}, u32[]{:S(2)}, u32[]{:S(2)}) collective-permute-start(f32[22,16,128]{2,1,0:T(8,128)S(1)} %get-tuple-element.16), channel_id=1, source_target_pairs={{0,4},{4,8},{8,12},{12,16},{16,20},{20,24},{24,28},{28,32},{32,36}... | collective-permute-start | bytes 540680 | tf_op jit(solution)/shard_map/ppermute | solution.py:739
  20.7 15.8 %collective-permute-start.3 = (f32[22,16,128]{2,1,0:T(8,128)S(1)}, f32[22,16,128]{2,1,0:T(8,128)S(1)}, u32[]{:S(2)}, u32[]{:S(2)}) collective-permute-start(f32[22,16,128]{2,1,0:T(8,128)S(1)} %get-tuple-element.17), channel_id=1, source_target_pairs={{4,0},{8,4},{12,8},{16,12},{20,16},{24,20},{28,24},{32,28},{36,32}... | collective-permute-start | bytes 540680 | tf_op jit(solution)/shard_map/ppermute | solution.py:744
  39.9 9.8 %collective-permute-start.4 = (f32[9,16,128]{2,1,0:T(8,128)S(1)}, f32[9,16,128]{2,1,0:T(8,128)S(1)}, u32[]{:S(2)}, u32[]{:S(2)}) collective-permute-start(f32[9,16,128]{2,1,0:T(8,128)S(1)} %get-tuple-element.22), channel_id=1, source_target_pairs={{0,4},{4,8},{8,12},{12,16},{16,20},{20,24},{24,28},{28,32},{32,36}... | collective-permute-start | bytes 221192 | tf_op jit(solution)/shard_map/ppermute | solution.py:739
  41.8 9.3 %collective-permute-start.5 = (f32[9,16,128]{2,1,0:T(8,128)S(1)}, f32[9,16,128]{2,1,0:T(8,128)S(1)}, u32[]{:S(2)}, u32[]{:S(2)}) collective-permute-start(f32[9,16,128]{2,1,0:T(8,128)S(1)} %get-tuple-element.23), channel_id=1, source_target_pairs={{4,0},{8,4},{12,8},{16,12},{20,16},{24,20},{28,24},{32,28},{36,32}... | collective-permute-start | bytes 221192 | tf_op jit(solution)/shard_map/ppermute | solution.py:744

commit v2 on v1

v2 whole, which is shorter than its diff:
```python
import functools

import jax
import jax.numpy as jnp
import numpy as np
from jax import lax
from jax.experimental import pallas as pl
from jax.experimental.pallas import tpu as pltpu
from jax.sharding import PartitionSpec as P

DIRS = [
    (0, 0, 0), (1, 0, 0), (-1, 0, 0), (0, 1, 0), (0, -1, 0), (0, 0, 1), (0, 0, -1),
    (1, 1, 0), (-1, -1, 0), (1, -1, 0), (-1, 1, 0), (1, 0, 1), (-1, 0, -1), (1, 0, -1),
    (-1, 0, 1), (0, 1, 1), (0, -1, -1), (0, 1, -1), (0, -1, 1),
]
BACK = [0, 2, 1, 4, 3, 6, 5, 8, 7, 10, 9, 12, 11, 14, 13, 16, 15, 18, 17]
W = [1.0 / 3.0] + [1.0 / 18.0] * 6 + [1.0 / 36.0] * 12
W0, W1, W2 = 1.0 / 3.0, 1.0 / 18.0, 1.0 / 36.0
PAIRS = [(q, q + 1) for q in range(1, 19, 2)]
TO_RIGHT = [q for q in range(19) if DIRS[q][0] == 1]
TO_LEFT = [q for q in range(19) if DIRS[q][0] == -1]
RIM = 8
SHARP = 0.075
FLUID = 26
F32 = jnp.float32
VMEM_LIMIT = 40 * 2**20


def lanes():
    return lax.broadcasted_iota(jnp.int32, (16, 128), 1)


def roll(x, shift, axis):
    shift = shift % x.shape[axis]
    return x if shift == 0 else pltpu.roll(x, shift, axis)


def load_pair(ref, *at):
    *head, row = at
    return (ref[(*head, 2 * row)], ref[(*head, 2 * row + 1)])


def store_pair(ref, pair, *at):
    *head, row = at
    ref[(*head, 2 * row)] = pair[0]
    ref[(*head, 2 * row + 1)] = pair[1]


def both(fn, *pairs):
    return tuple(fn(*each) for each in zip(*pairs))


def moved(pair, step_y, step_z):
    if step_y:
        pair = both(lambda t: roll(t, -step_y, 0), pair)
    if step_z:
        a = roll(pair[0], -step_z, 1)
        b = roll(pair[1], -step_z, 1)
        edge = lanes() == (127 if step_z > 0 else 0)
        pair = (jnp.where(edge, b, a), jnp.where(edge, a, b))
    return pair


def is_odd(axis):
    return jnp.full((16, 128), lax.rem(lax.axis_index(axis), 2), jnp.int32) == 1


def rim_slots(count, wide):
    slots, at = [], 0
    for k in range(count):
        width = 8 if k in wide else 4
        if at % 128 + 2 * width > 128:
            at += 128 - at % 128
        slots.append((at // 128, at % 128, width))
        at += 2 * width
    return slots


def message_tiles(count, wide=()):
    return count + rim_slots(count, wide)[-1][0] + 1


def packed(fields, wide):
    lane = lanes()
    out = [main for main, _ in fields]
    slots = rim_slots(len(fields), wide)
    for tile in range(slots[-1][0] + 1):
        acc = jnp.zeros((16, 128), F32)
        for (at, first, width), (_, rim) in zip(slots, fields):
            if at == tile:
                mine = (lane >= first) & (lane < first + 2 * width)
                acc = jnp.where(mine, roll(rim, first + width, 1), acc)
        out.append(acc)
    return out


def pack(odd_ref, even_ref, right, left, wide=()):
    odd = is_odd("tile")
    for n, (r, l) in enumerate(zip(packed(right, wide), packed(left, wide))):
        odd_ref[n] = jnp.where(odd, r, l)
        even_ref[n] = jnp.where(odd, l, r)


def received(odd_ref, even_ref, count, wide=()):
    odd = is_odd("tile")
    slots = rim_slots(count, wide)
    tiles = message_tiles(count, wide)
    got_odd = [odd_ref[n] for n in range(tiles)]
    got_even = [even_ref[n] for n in range(tiles)]
    sides = []
    for one, two in ((got_even, got_odd), (got_odd, got_even)):
        msg = [jnp.where(odd, a, b) for a, b in zip(one, two)]
        sides.append(
            [(msg[k], roll(msg[count + at], -(first + width), 1)) for k, (at, first, width) in enumerate(slots)]
        )
    return sides


def total(values):
    out = values[0]
    for value in values[1:]:
        out = out + value
    return out


def along(step, vec):
    out = None
    for c, v in zip(step, vec):
        if c == 0:
            continue
        if out is None:
            out = v if c > 0 else -v
        else:
            out = out + v if c > 0 else out - v
    return out


def momentum_of(pops, axis):
    plus = [pops[q] for q in range(19) if DIRS[q][axis] == 1]
    minus = [pops[q] for q in range(19) if DIRS[q][axis] == -1]
    return total([a - b for a, b in zip(plus, minus)])


def state_of(phi, mom, grad, lap):
    clipped = jnp.clip(phi, 0.0, 1.0)
    rho = 0.05 + 0.95 * clipped
    omega = 1.0 / (0.6 + 0.3 * clipped)
    inv_rho = 1.0 / rho
    potential = 1.2 * phi * (phi - 1.0) * (phi - 0.5) - 0.6 * lap
    force = (
        potential * grad[0] - 0.01 * rho,
        potential * grad[1],
        potential * grad[2] - 0.02 * (rho - 0.05),
    )
    half = 0.5 * inv_rho
    vel = tuple(m + f * half for m, f in zip(mom, force))
    kappa = (1.0 - 0.5 * omega) * inv_rho
    return dict(
        phi=phi, grad=grad, omega=omega, inv_rho=inv_rho, potential=potential, force=force,
        half=half, vel=vel, kappa=kappa,
    )


def dot(a, b):
    return a[0] * b[0] + a[1] * b[1] + a[2] * b[2]


def sharpening(s):
    inv_len = lax.rsqrt(dot(s["grad"], s["grad"]) + 0.01)
    return SHARP * s["phi"] * (1.0 - s["phi"]) * inv_len, inv_len


def carried_of(s, axis):
    sharp, _ = sharpening(s)
    return s["phi"] * s["vel"][axis] + sharp * s["grad"][axis]


def post_flow(pops, fluid, pressure, s, wanted):
    vel, force, omega, kappa = s["vel"], s["force"], s["omega"], s["kappa"]
    base = omega * (pressure - 1.5 * dot(vel, vel)) - 3.0 * kappa * dot(vel, force)
    odd_vec = tuple(3.0 * (omega * v + kappa * f) for v, f in zip(vel, force))
    even_vec = tuple(4.5 * omega * v + 9.0 * kappa * f for v, f in zip(vel, force))
    keep = 1.0 - omega
    out = {}
    if 0 in wanted:
        out[0] = jnp.where(fluid, keep * pops[0] + W0 * base, pops[0])
    for q, r in PAIRS:
        if q not in wanted and r not in wanted:
            continue
        step = DIRS[q]
        even = base + along(step, vel) * along(step, even_vec)
        odd = along(step, odd_vec)
        if q in wanted:
            out[q] = jnp.where(fluid, keep * pops[q] + W[q] * (even + odd), pops[r])
        if r in wanted:
            out[r] = jnp.where(fluid, keep * pops[r] + W[q] * (even - odd), pops[q])
    return out


def post_phase(pops, fluid, s, wanted):
    sharp, _ = sharpening(s)
    carried = tuple(s["phi"] * v + sharp * g for v, g in zip(s["vel"], s["grad"]))
    out = {}
    for q in wanted:
        if q == 0:
            out[q] = jnp.where(fluid, 0.3125 * s["phi"] - 0.25 * pops[0], pops[0])
        else:
            equil = 0.15625 * s["phi"] + 0.625 * along(DIRS[q], carried)
            out[q] = jnp.where(fluid, equil - 0.25 * pops[q], pops[BACK[q]])
    return out


def moments_of(adj):
    zero = None
    m0, m1 = [], [[], [], []]
    m2 = {}
    if 0 in adj:
        m0.append(W0 * adj[0])
    groups = {W1: [], W2: []}
    for q in range(1, 19):
        if q not in adj:
            continue
        a = adj[q]
        w = W[q]
        groups[w].append(a)
    for w, items in groups.items():
        if items:
            m0.append(w * total(items))

    def weighted(terms):
        parts = []
        for w in (W1, W2):
            mine = [(sign, a) for ww, sign, a in terms if ww == w]
            if not mine:
                continue
            acc = None
            for sign, a in mine:
                if acc is None:
                    acc = a if sign > 0 else -a
                else:
                    acc = acc + a if sign > 0 else acc - a
            parts.append(w * acc)
        return total(parts) if parts else None

    for i in range(3):
        m1[i] = weighted([(W[q], DIRS[q][i], adj[q]) for q in range(1, 19) if q in adj and DIRS[q][i]])
    for i in range(3):
        for j in range(i, 3):
            m2[(i, j)] = weighted(
                [
                    (W[q], DIRS[q][i] * DIRS[q][j], adj[q])
                    for q in range(1, 19)
                    if q in adj and DIRS[q][i] and DIRS[q][j]
                ]
            )
            m2[(j, i)] = m2[(i, j)]
    return total(m0), m1, m2


def apply_m2(m2, vec):
    out = []
    for i in range(3):
        terms = [m2[(i, j)] * vec[j] for j in range(3) if m2[(i, j)] is not None]
        out.append(total(terms))
    return out


def pull_stencil(s, m0, m1, m2, n1):
    vel, force = s["vel"], s["force"]
    omega, kappa, half = s["omega"], s["kappa"], s["half"]
    m2v = apply_m2(m2, vel)
    m2f = apply_m2(m2, force)
    m0_3 = 3.0 * m0
    lean = []
    for i in range(3):
        term = 9.0 * m2v[i] - m0_3 * vel[i]
        lean.append(term if m1[i] is None else term + 3.0 * m1[i])
    push = [9.0 * m2f[i] - m0_3 * force[i] for i in range(3)]
    d_vel = [omega * a + kappa * b for a, b in zip(lean, push)]
    if n1 is not None:
        five_phi = 5.0 * s["phi"]
        d_vel = [d + five_phi * n for d, n in zip(d_vel, n1)]
    d_force = [kappa * a + half * d for a, d in zip(lean, d_vel)]
    d_potential = dot(d_force, s["grad"])
    d_grad = [s["potential"] * x for x in d_force]
    if n1 is not None:
        sharp, inv_len = sharpening(s)
        tilt = dot(s["grad"], n1) * inv_len * inv_len
        sharp5 = 5.0 * sharp
        d_grad = [d + sharp5 * (n - g * tilt) for d, n, g in zip(d_grad, n1, s["grad"])]
    d_lap = -0.6 * d_potential
    return d_grad, d_lap, d_potential, d_force, d_vel, m2v, m2f


def inside_clip(phi):
    return jnp.where((phi > 0.0) & (phi < 1.0), 1.0, jnp.where((phi == 0.0) | (phi == 1.0), 0.5, 0.0))


def pull_all(s, pressure, adj, kept, m0, m1, m2, n0, n1):
    d_grad, d_lap, d_potential, d_force, d_vel, m2v, m2f = pull_stencil(s, m0, m1, m2, n1)
    phi, vel, force = s["phi"], s["vel"], s["force"]
    omega, kappa, inv_rho, half = s["omega"], s["kappa"], s["inv_rho"], s["half"]
    relaxed = m0 * (pressure - 1.5 * dot(vel, vel)) + 3.0 * dot(m1, vel) + 4.5 * dot(m2v, vel)
    forced = 3.0 * dot(m1, force) - 3.0 * m0 * dot(vel, force) + 9.0 * dot(m2v, force)
    d_omega = relaxed - kept - 0.5 * inv_rho * forced
    d_rho = (
        -kappa * inv_rho * forced
        - 0.01 * d_force[0]
        - 0.02 * d_force[2]
        - dot(d_vel, force) * half * inv_rho
    )
    d_clip = 0.95 * d_rho - 0.3 * omega * omega * d_omega
    d_phi = d_potential * (1.2 * (3.0 * phi * (phi - 1.0) + 0.5)) + d_clip * inside_clip(phi)
    if n1 is not None:
        _, inv_len = sharpening(s)
        d_phi = d_phi + 1.25 * n0 + 5.0 * (
            dot(n1, vel) + SHARP * (1.0 - 2.0 * phi) * inv_len * dot(n1, s["grad"])
        )
    d_pressure = omega * m0
    keep = 1.0 - omega
    kept_part = lambda q, rest: keep * adj[q] + rest if q in adj else rest
    d_flow = {0: kept_part(0, d_pressure)}
    for q, r in PAIRS:
        lift = along(DIRS[q], d_vel)
        d_flow[q] = kept_part(q, d_pressure + lift)
        d_flow[r] = kept_part(r, d_pressure - lift)
    return d_flow, d_phi, d_grad, d_lap


def pull_along_x(s, n0, n):
    phi, grad = s["phi"], s["grad"]
    sharp, inv_len = sharpening(s)
    d_vel = 5.0 * phi * n
    d_force = s["half"] * d_vel
    d_potential = d_force * grad[0]
    sharp5 = 5.0 * sharp
    tilt = sharp5 * (grad[0] * n * inv_len * inv_len)
    d_grad = [s["potential"] * d_force + sharp5 * n - grad[0] * tilt, -grad[1] * tilt, -grad[2] * tilt]
    d_rho = -0.01 * d_force - d_force * s["force"][0] * s["inv_rho"]
    d_phi = (
        d_potential * (1.2 * (3.0 * phi * (phi - 1.0) + 0.5))
        + 0.95 * d_rho * inside_clip(phi)
        + 1.25 * n0
        + 5.0 * n * (s["vel"][0] + SHARP * (1.0 - 2.0 * phi) * inv_len * grad[0])
    )
    return d_vel, d_phi, d_grad, -0.6 * d_potential


def gradients(behind, centre, ahead):
    ahead_y, behind_y = moved(centre, 1, 0), moved(centre, -1, 0)
    ahead_z, behind_z = moved(centre, 0, 1), moved(centre, 0, -1)
    diff = lambda a, b: 0.5 * (a - b)
    lap = both(
        lambda a, b, c, d, e, f, m: a + b + c + d + e + f - 6.0 * m,
        ahead, behind, ahead_y, behind_y, ahead_z, behind_z, centre,
    )
    return both(diff, ahead, behind), both(diff, ahead_y, behind_y), both(diff, ahead_z, behind_z), lap


def behind_part(d_grad, d_lap):
    return 0.5 * d_grad + d_lap


def ahead_part(d_grad, d_lap):
    return d_lap - 0.5 * d_grad


def rim_kernel(
    g_ref, f_ref, solid_ref, cells_ref, weights_ref,
    main_ref, probes_ref, probe_weights_ref, odd_ref, even_ref, mask_ref, sems,
):
    copies = [pltpu.make_async_copy(solid_ref, mask_ref, sems.at[0])]
    copies.append(pltpu.make_async_copy(g_ref, main_ref.at[pl.ds(0, 7)], sems.at[1]))
    for n, (first, count) in enumerate(((0, 5), (5, 5), (10, 5), (15, 4))):
        copies.append(
            pltpu.make_async_copy(
                f_ref.at[pl.ds(first, count)], main_ref.at[pl.ds(7 + first, count)], sems.at[2 + n]
            )
        )
    later = [pltpu.make_async_copy(weights_ref, probe_weights_ref, sems.at[6])]
    for i in range(3):
        later.append(pltpu.make_async_copy(cells_ref.at[:, i, :], probes_ref.at[i], sems.at[7 + i]))
    for copy in copies + later:
        copy.start()
    for copy in copies:
        copy.wait()
    lane = lanes()
    odd = is_odd("vert")

    def row(x, carry):
        main_ref[FLUID, x] = 1.0 - mask_ref[x].astype(F32)
        for tile in range(2):
            up = jnp.zeros((16, 128), F32)
            down = jnp.zeros((16, 128), F32)
            for slot in range(16):
                k = 16 * tile + slot
                if k > FLUID:
                    continue
                cells = main_ref[k, x]
                turned = roll(cells, 8 * slot + 8, 1)
                up = jnp.where(lane // RIM == slot, turned, up)
                down = jnp.where(lane // RIM == (slot + 1) % 16, turned, down)
            odd_ref[tile, x] = jnp.where(odd, up, down)
            even_ref[tile, x] = jnp.where(odd, down, up)
        return carry

    lax.fori_loop(0, 4, row, 0)
    for copy in later:
        copy.wait()


def ring_kernel(seeds_ref, main_ref, odd_in_ref, even_in_ref, rim_ref, phase_ref, odd_ref, even_ref):
    del seeds_ref
    lane = lanes()
    odd = is_odd("vert")

    def row(x, carry):
        above = [jnp.where(odd, odd_in_ref[t, x], even_in_ref[t, x]) for t in range(2)]
        below = [jnp.where(odd, even_in_ref[t, x], odd_in_ref[t, x]) for t in range(2)]
        even_group = lane // RIM % 2 == 0
        mixed = [
            (jnp.where(even_group, b, a), jnp.where(even_group, a, b)) for a, b in zip(above, below)
        ]
        sums = [None, None]
        for k in range(27):
            cells = main_ref[k, x]
            slot = k % 16
            rim = roll(mixed[k // 16][slot % 2], 120 - 8 * slot, 1)
            rim_ref[k, x] = rim
            if k < 7:
                sums = [a if b is None else a + b for a, b in zip((cells, rim), sums)]
        phase_ref[2 * x] = sums[0]
        phase_ref[2 * x + 1] = sums[1]
        return carry

    lax.fori_loop(0, 4, row, 0)

    def cells_of(k, row):
        return (main_ref[k, row], rim_ref[k, row])

    messages = []
    for edge, inner, crossing, out in ((3, 2, TO_RIGHT, 1), (0, 1, TO_LEFT, 2)):
        pops = [cells_of(7 + q, edge) for q in range(19)]
        g = [cells_of(q, edge) for q in range(7)]
        fluid = both(lambda a: a > 0.5, cells_of(FLUID, edge))
        phi = load_pair(phase_ref, edge)
        pressure = both(lambda *p: total(p), *pops)
        omega = both(lambda p: 1.0 / (0.6 + 0.3 * jnp.clip(p, 0.0, 1.0)), phi)
        fields = [
            both(
                lambda a, b, f, o, p: jnp.where(f, (1.0 - o) * a + W[q] * (o * p), b),
                pops[q], pops[BACK[q]], fluid, omega, pressure,
            )
            for q in crossing
        ]
        turn = lambda a, b, f: jnp.where(f, -0.25 * a, b)
        fields.append(both(turn, g[out], g[BACK[out]], fluid))
        parts = [both(turn, g[0], g[0], fluid)]
        for q in range(3, 7):
            parts.append(moved(both(turn, g[q], g[BACK[q]], fluid), -DIRS[q][1], -DIRS[q][2]))
        grads = gradients(*(load_pair(phase_ref, inner + d) for d in (-1, 0, 1)))
        inner_phi = load_pair(phase_ref, inner)
        inner_pops = [cells_of(7 + q, inner) for q in range(19)]
        crossing_phase = []
        for t in range(2):
            mom = [momentum_of([p[t] for p in inner_pops], 0)] + [jnp.zeros((16, 128), F32)] * 2
            s = state_of(inner_phi[t], mom, tuple(gr[t] for gr in grads[:3]), grads[3][t])
            equil = 0.15625 * inner_phi[t] + (0.625 if out == 1 else -0.625) * carried_of(s, 0)
            crossing_phase.append(
                jnp.where(
                    cells_of(FLUID, inner)[t] > 0.5,
                    equil - 0.25 * cells_of(out, inner)[t],
                    cells_of(BACK[out], inner)[t],
                )
            )
        parts.append(tuple(crossing_phase))
        fields.append(both(lambda *p: total(p), *parts))
        fields.append(phi)
        for axis in range(3):
            fields.append(both(lambda *p: momentum_of(p, axis), *pops))
        fields.append(cells_of(FLUID, edge))
        fields.append(inner_phi)
        messages.append(fields)
    pack(odd_ref, even_ref, *messages, wide=WIDE_FIRST)


SHIFTS = sorted({c[1:] for c in DIRS})
BF16 = jnp.bfloat16


def probe_kernel(probes_ref, weights_ref, out_ref, acc_ref, code_ref):
    first_x = lax.axis_index("tile") * 4
    first_z = lax.axis_index("vert") * 128
    acc_ref[...] = jnp.zeros_like(acc_ref)
    count = jnp.zeros((8, 128), jnp.int32)
    groups = probes_ref.shape[1] // 8
    for i in range(groups):
        at = slice(8 * i, 8 * i + 8)
        x = probes_ref[0, at, :] - (first_x - 1)
        y = probes_ref[1, at, :]
        z = probes_ref[2, at, :] - first_z
        here = (x >= 0) & (x < 6) & (z >= -RIM) & (z < 128 + RIM)
        ring = jnp.where(z >= 0, z, z + 144)
        code_ref[at, :] = jnp.where(here, (x * 16 + y) * 256 + ring, -1)
        count = count + here.astype(jnp.int32)
    passes = jnp.max(count)
    across = lax.broadcasted_iota(jnp.int32, (96, 128), 0).astype(F32).astype(BF16)
    height = lax.broadcasted_iota(jnp.int32, (144, 128), 0).astype(F32).astype(BF16)
    zero = jnp.zeros((), BF16)
    one = jnp.ones((), BF16)

    def one_pass(i, carry):
        code = jnp.full((8, 128), -1, jnp.int32)
        weight = jnp.zeros((8, 128), F32)
        for i in range(groups):
            at = slice(8 * i, 8 * i + 8)
            here = code_ref[at, :]
            take = (here >= 0) & (code < 0)
            code = jnp.where(take, here, code)
            weight = jnp.where(take, weights_ref[at, :], weight)
            code_ref[at, :] = jnp.where(take, -1, here)
        code_xy = (code >> 8).astype(F32)
        code_z = (code & 255).astype(F32)
        high = weight.astype(BF16).astype(F32)
        low = weight - high
        lhs, rhs = [], []
        for n in range(8):
            line = lambda v: v[n : n + 1, :].astype(BF16)
            hit = across == line(code_xy)
            lhs.append(
                jnp.concatenate([jnp.where(hit, line(high), zero), jnp.where(hit, line(low), zero)], axis=0)
            )
            rhs.append(jnp.where(height == line(code_z), one, zero))
        acc_ref[...] += lax.dot_general(
            jnp.concatenate(lhs, axis=1), jnp.concatenate(rhs, axis=1), (((1,), (1,)), ((), ())),
            preferred_element_type=F32,
        )
        return carry

    lax.fori_loop(0, passes, one_pass, 0)
    lane = lanes()
    for x in range(6):
        rows = pl.ds(16 * x, 16)
        lows = pl.ds(96 + 16 * x, 16)
        main = acc_ref[rows, 0:128] + acc_ref[lows, 0:128]
        rim = acc_ref[rows, 128:144] + acc_ref[lows, 128:144]
        rim = jnp.concatenate([rim, jnp.zeros((16, 112), F32)], axis=1)
        rim = jnp.where(lane < RIM, rim, jnp.where(lane >= 120, roll(rim, 112, 1), 0.0))
        for n, (cy, cz) in enumerate(SHIFTS):
            store_pair(out_ref, moved((main, rim), cy, cz), n, x)


N_FIRST = 13
WIDE_FIRST = (7,)
N_SECOND = 8
HALVES = (slice(0, 8), slice(8, 16))
M2_KEYS = ((0, 0), (0, 1), (0, 2), (1, 1), (1, 2), (2, 2))


def spot(refs, row):
    if row in (1, 2):
        return refs[0], row - 1
    return refs[1], {-1: 0, 0: 1, 3: 2, 4: 3}[row]


def prim_at(prims, row, t, h):
    ref, at = spot(prims, row)
    vals = [ref[k, 2 * at + t, h, :] for k in range(10)]
    return state_of(vals[0], vals[6:9], tuple(vals[1:4]), vals[4]), vals[5], vals[9] > 0.5


def put_gradients(prims, phase_pairs, row):
    ref, at = spot(prims, row)
    grads = gradients(*phase_pairs)
    store_pair(ref, phase_pairs[1], 0, at)
    for i in range(4):
        store_pair(ref, grads[i], 1 + i, at)


def forward(cells_ref, prims, posts, row, t):
    prim_ref, at = spot(prims, row)
    post_ref, _ = spot(posts, row)
    i = 2 * at + t
    for h in HALVES:
        g = [cells_ref[q, row, h, :] for q in range(7)]
        f = [cells_ref[7 + q, row, h, :] for q in range(19)]
        prim_ref[5, i, h, :] = total(f)
        for axis in range(3):
            prim_ref[6 + axis, i, h, :] = momentum_of(f, axis)
        prim_ref[9, i, h, :] = cells_ref[FLUID, row, h, :]
        s, pressure, fluid = prim_at(prims, row, t, h)
        for q, v in post_flow(f, fluid, pressure, s, range(19)).items():
            post_ref[7 + q, i, h, :] = v
        for q, v in post_phase(g, fluid, s, range(7)).items():
            post_ref[q, i, h, :] = v


def stream(posts, row):
    ref, at = spot(posts, row)
    for q in range(19):
        _, cy, cz = DIRS[q]
        if (cy or cz) and 0 <= row + DIRS[q][0] < 4:
            store_pair(ref, moved(load_pair(ref, 7 + q, at), -cy, -cz), 7 + q, at)


def inner_kernel(main_ref, rim_ref, phase_ref, seeds_ref, prim_ref, post_ref, moments_ref):
    prims, posts = (prim_ref, None), (post_ref, None)
    for row in (1, 2):
        put_gradients(prims, [load_pair(phase_ref, row + d) for d in (-1, 0, 1)], row)
        for t, cells_ref in enumerate((main_ref, rim_ref)):
            forward(cells_ref, prims, posts, row, t)
        stream(posts, row)

    def moments(i, carry):
        for h in HALVES:
            adj = {q: seeds_ref[SHIFTS.index(DIRS[q][1:]), i + 2 + 2 * DIRS[q][0], h, :] for q in range(19)}
            m0, m1, m2 = moments_of(adj)
            for k, v in enumerate([m0] + m1 + [m2[key] for key in M2_KEYS]):
                moments_ref[k, i, h, :] = v
        return carry

    lax.fori_loop(0, 8, moments, 0)


def middle_kernel(
    main_ref, rim_ref, phase_ref, odd_in_ref, even_in_ref, seeds_ref, moments_ref, prim_in_ref, post_in_ref,
    prim_ref, adj_ref, gamma_ref, edges_ref, odd_ref, even_ref,
    post_ref, phase_mid_ref, grad_mid_ref, back_ref, dphi_ref,
):
    prims, posts = (prim_in_ref, prim_ref), (post_in_ref, post_ref)
    from_left, from_right = received(odd_in_ref, even_in_ref, N_FIRST, WIDE_FIRST)
    sides = ((from_left, -1, TO_RIGHT, 1), (from_right, 4, TO_LEFT, 2))
    for got, row, crossing, out in sides:
        _, at = spot(prims, row)
        for i in range(3):
            store_pair(prim_ref, got[8 + i], 6 + i, at)
        store_pair(prim_ref, got[11], 9, at)
        for q, pair in zip(crossing, got[:5]):
            store_pair(post_ref, pair, 7 + q, at)
        store_pair(post_ref, got[5], out, at)
    phases = [from_left[12], from_left[7]] + [load_pair(phase_ref, r) for r in range(4)]
    phases += [from_right[7], from_right[12]]
    for row in (-1, 0, 3, 4):
        put_gradients(prims, phases[row + 1 : row + 4], row)
    for row in (0, 3):
        for t, cells_ref in enumerate((main_ref, rim_ref)):
            forward(cells_ref, prims, posts, row, t)
        stream(posts, row)

    mid_parts = {}
    for got, row, crossing, out in sides:
        _, at = spot(posts, row)
        spread = [[], [], []]
        for t in range(2):
            i = 2 * at + t
            halves = [[], [], []]
            for h in HALVES:
                vals = [prim_ref[k, i, h, :] for k in range(10) if k != 5]
                s = state_of(vals[0], vals[5:8], tuple(vals[1:4]), vals[4])
                fluid = vals[8] > 0.5
                vel, force, omega, kappa = s["vel"], s["force"], s["omega"], s["kappa"]
                base = -1.5 * omega * dot(vel, vel) - 3.0 * kappa * dot(vel, force)
                odd_vec = tuple(3.0 * (omega * v + kappa * f) for v, f in zip(vel, force))
                even_vec = tuple(4.5 * omega * v + 9.0 * kappa * f for v, f in zip(vel, force))
                for q in crossing:
                    step = DIRS[q]
                    gain = base + along(step, vel) * along(step, even_vec) + along(step, odd_vec)
                    kept = post_ref[7 + q, i, h, :]
                    post_ref[7 + q, i, h, :] = jnp.where(fluid, kept + W[q] * gain, kept)
                sharp, _ = sharpening(s)
                carried = tuple(s["phi"] * v + sharp * gr for v, gr in zip(vel, s["grad"]))
                kept = post_ref[out, i, h, :]
                gain = 0.15625 * s["phi"] + 0.625 * along(DIRS[out], carried)
                post_ref[out, i, h, :] = jnp.where(fluid, kept + gain, kept)
                halves[0].append(jnp.where(fluid, s["phi"], 0.0))
                halves[1].append(jnp.where(fluid, carried[1], 0.0))
                halves[2].append(jnp.where(fluid, carried[2], 0.0))
            for n in range(3):
                spread[n].append(jnp.concatenate(halves[n], axis=0))
        stream(posts, row)
        phi, cy, cz = (tuple(x) for x in spread)
        gain_y = lambda sign: both(lambda p, c: 0.15625 * p + sign * 0.625 * c, phi, cy)
        gain_z = lambda sign: both(lambda p, c: 0.15625 * p + sign * 0.625 * c, phi, cz)
        mid_parts[row] = [
            got[6], both(lambda p: 0.3125 * p, phi),
            moved(gain_y(1.0), -1, 0), moved(gain_y(-1.0), 1, 0),
            moved(gain_z(1.0), 0, -1), moved(gain_z(-1.0), 0, 1),
        ]
    def post_pair(q, row):
        ref, at = spot(posts, row)
        return load_pair(ref, q, at)

    for row in range(-1, 5):
        parts = mid_parts.get(row)
        if parts is None:
            parts = [post_pair(0, row)]
            for q in range(3, 7):
                parts.append(moved(post_pair(q, row), -DIRS[q][1], -DIRS[q][2]))
        if row > -1:
            parts.append(post_pair(1, row - 1))
        if row < 4:
            parts.append(post_pair(2, row + 1))
        store_pair(phase_mid_ref, both(lambda *p: total(p), *parts), row + 1)
    for row in range(4):
        grads = gradients(*(load_pair(phase_mid_ref, row + d) for d in (0, 1, 2)))
        for i in range(4):
            store_pair(grad_mid_ref, grads[i], i, row)
    def backward(row, t, h):
        i = 2 * row + t
        f = []
        for q in range(19):
            ref, at = spot(posts, row - DIRS[q][0])
            f.append(ref[7 + q, 2 * at + t, h, :])
        adj = {q: seeds_ref[SHIFTS.index(DIRS[q][1:]), i + 2 + 2 * DIRS[q][0], h, :] for q in range(19)}
        ref, at = spot(prims, row)
        fluid = ref[9, 2 * at + t, h, :] > 0.5
        phi = phase_mid_ref[i + 2, h, :]
        mom = [momentum_of(f, axis) for axis in range(3)]
        s = state_of(phi, mom, tuple(grad_mid_ref[k, i, h, :] for k in range(3)), grad_mid_ref[3, i, h, :])
        kept = total([adj[q] * f[q] for q in range(19)])
        m = [moments_ref[k, i, h, :] for k in range(10)]
        m2 = {}
        for key, value in zip(M2_KEYS, m[4:]):
            m2[key] = m2[key[::-1]] = value
        d_flow, d_phi, d_grad, d_lap = pull_all(s, total(f), adj, kept, m[0], m[1:4], m2, None, None)
        for q in range(19):
            adj_ref[q, i, h, :] = jnp.where(fluid, d_flow[q], adj[BACK[q]])
        dphi_ref[i, h, :] = jnp.where(fluid, d_phi, 0.0)
        for k in range(3):
            back_ref[k, i, h, :] = jnp.where(fluid, d_grad[k], 0.0)
        back_ref[3, i, h, :] = jnp.where(fluid, d_lap, 0.0)

    for row in range(4):
        for t in range(2):
            for h in HALVES:
                backward(row, t, h)

    for q in range(19):
        _, cy, cz = DIRS[q]
        if cy or cz:
            for row in range(4):
                store_pair(adj_ref, moved(load_pair(adj_ref, q, row), cy, cz), q, row)

    for row in range(4):
        store_pair(gamma_ref, stencil_back(back_ref, dphi_ref, row), row)
    edge_parts = []
    for row, part in ((0, ahead_part), (3, behind_part)):
        pair = both(part, load_pair(back_ref, 0, row), load_pair(back_ref, 3, row))
        store_pair(edges_ref, pair, 0 if row == 0 else 1)
        edge_parts.append(pair)

    messages = []
    for row, out_dirs, part, sign, edge_pair in (
        (3, TO_RIGHT, behind_part, -1.0, edge_parts[1]),
        (0, TO_LEFT, ahead_part, 1.0, edge_parts[0]),
    ):
        gamma = load_pair(gamma_ref, row)
        next_gamma = load_pair(gamma_ref, row - 1 if row == 3 else row + 1)
        n1 = turn_gamma(both(lambda a: sign * a, next_gamma), gamma)
        partial = []
        for t in range(2):
            s, _, fluid = prim_at(prims, row, t, slice(None))
            adj = {
                q: adj_ref[q, 2 * (row + DIRS[q][0]) + t] for q in range(19) if q not in out_dirs
            }
            m0, m1, m2 = moments_of(adj)
            d_grad, d_lap = pull_stencil(s, m0, m1, m2, [n[t] for n in n1])[:2]
            partial.append(jnp.where(fluid, part(d_grad[0], d_lap), 0.0))
        back_dirs = TO_LEFT if row == 3 else TO_RIGHT
        fields = [load_pair(adj_ref, q, row) for q in back_dirs]
        fields += [gamma, edge_pair, tuple(partial)]
        messages.append(fields)
    pack(odd_ref, even_ref, *messages)


def turn_gamma(along_x, centre):
    diff = lambda a, b: 0.125 * (a - b)
    return (
        both(lambda a: 0.125 * a, along_x),
        both(diff, moved(centre, 1, 0), moved(centre, -1, 0)),
        both(diff, moved(centre, 0, 1), moved(centre, 0, -1)),
    )


def stencil_back(back_ref, start_ref, row, first=None, last=None):
    gy, gz, lap = (load_pair(back_ref, k, row) for k in (1, 2, 3))
    fold = lambda l, gyb, gya, lyb, lya, gzb, gza, lzb, lza: (
        0.5 * (gyb - gya) + lyb + lya + 0.5 * (gzb - gza) + lzb + lza - 6.0 * l
    )
    out = both(
        fold, lap,
        moved(gy, -1, 0), moved(gy, 1, 0), moved(lap, -1, 0), moved(lap, 1, 0),
        moved(gz, 0, -1), moved(gz, 0, 1), moved(lap, 0, -1), moved(lap, 0, 1),
    )
    add = lambda a, b: a + b
    if start_ref is not None:
        out = both(add, out, load_pair(start_ref, row))
    if row > 0:
        out = both(add, out, both(behind_part, load_pair(back_ref, 0, row - 1), load_pair(back_ref, 3, row - 1)))
    elif first is not None:
        out = both(add, out, first)
    if row < 3:
        out = both(add, out, both(ahead_part, load_pair(back_ref, 0, row + 1), load_pair(back_ref, 3, row + 1)))
    elif last is not None:
        out = both(add, out, last)
    return out


def ahead_kernel(
    main_ref, prim_in_ref, prim_out_ref, adj_ref, gamma_ref,
    flow_ref, back_ref, dphi_ref,
    turned_ref,
):
    prims = (prim_in_ref, prim_out_ref)
    for row in (1, 2):
        centre = load_pair(gamma_ref, row)
        for n, (cy, cz) in enumerate(((1, 0), (-1, 0), (0, 1), (0, -1))):
            store_pair(turned_ref, moved(centre, cy, cz), n, row - 1)
    for row in range(4):
        for t in range(2):
            for h in HALVES:
                i = 2 * row + t
                s, pressure, fluid = prim_at(prims, row, t, h)
                adj = {
                    q: adj_ref[q, i + 2 * DIRS[q][0], h, :] for q in range(19) if 0 <= row + DIRS[q][0] < 4
                }
                m0, m1, m2 = moments_of(adj)
                n0 = n1 = None
                if row in (1, 2):
                    g = [gamma_ref[i + 2, h, :], gamma_ref[i - 2, h, :]]
                    g += [turned_ref[n, i - 2, h, :] for n in range(4)]
                    n1 = [0.125 * (g[a] - g[a + 1]) for a in (0, 2, 4)]
                if t == 1:
                    d_grad, d_lap = pull_stencil(s, m0, m1, m2, n1)[:2]
                else:
                    if row in (1, 2):
                        n0 = 0.25 * gamma_ref[i, h, :] + 0.125 * total(g)
                    kept = total([a * main_ref[7 + q, row, h, :] for q, a in adj.items()])
                    d_flow, d_phi, d_grad, d_lap = pull_all(s, pressure, adj, kept, m0, m1, m2, n0, n1)
                    for q in range(19):
                        flow_ref[q, row, h, :] = jnp.where(fluid, d_flow[q], adj.get(BACK[q], 0.0))
                    dphi_ref[row, h, :] = jnp.where(fluid, d_phi, 0.0)
                for k in range(3):
                    back_ref[k, i, h, :] = jnp.where(fluid, d_grad[k], 0.0)
                back_ref[3, i, h, :] = jnp.where(fluid, d_lap, 0.0)


def last_kernel(
    main_ref, prim_in_ref, prim_out_ref, adj_ref, gamma_ref, edges_ref, flow_ref, back_in_ref, dphi_in_ref,
    odd_in_ref, even_in_ref,
    out_g_ref, out_f_ref,
    gamma_wide_ref, turned_ref, back_ref, dphi_ref, g_ref, f_ref, sems,
):
    add = lambda a, b: a + b
    prims = (prim_in_ref, prim_out_ref)
    copies = []

    def send(src, dst):
        copies.append(pltpu.make_async_copy(src, dst, sems.at[len(copies)]))
        copies[-1].start()

    got_left, got_right = received(odd_in_ref, even_in_ref, N_SECOND)
    own_first = load_pair(edges_ref, 0)
    own_last = load_pair(edges_ref, 1)

    for row, more, sign in ((1, got_left[6], -0.125), (2, got_right[6], 0.125)):
        for t in range(2):
            for n, h in enumerate(HALVES):
                i = 2 * row + t
                s, _, fluid = prim_at(prims, row, t, h)
                delta = more[t][8 * n : 8 * n + 8]
                d_vel, d_phi, d_grad, d_lap = pull_along_x(s, 0.125 * delta, sign * delta)
                if t == 0:
                    lift = jnp.where(fluid, d_vel, 0.0)
                    for q in range(19):
                        base = flow_ref[q, row, h, :]
                        f_ref[q, row, h, :] = base + DIRS[q][0] * lift if DIRS[q][0] else base
                    dphi_ref[row, h, :] = dphi_in_ref[row, h, :] + jnp.where(fluid, d_phi, 0.0)
                for k in range(3):
                    back_ref[k, i, h, :] = back_in_ref[k, i, h, :] + jnp.where(fluid, d_grad[k], 0.0)
                back_ref[3, i, h, :] = back_in_ref[3, i, h, :] + jnp.where(fluid, d_lap, 0.0)
    send(f_ref.at[:, pl.ds(1, 2)], out_f_ref.at[:, pl.ds(1, 2)])

    for row in (1, 2):
        store_pair(gamma_wide_ref, load_pair(gamma_ref, row), row + 1)
    store_pair(gamma_wide_ref, both(add, load_pair(gamma_ref, 0), got_left[6]), 1)
    store_pair(gamma_wide_ref, both(add, load_pair(gamma_ref, 3), got_right[6]), 4)
    store_pair(gamma_wide_ref, both(add, got_left[5], own_first), 0)
    store_pair(gamma_wide_ref, both(add, got_right[5], own_last), 5)
    for row in range(4):
        centre = load_pair(gamma_wide_ref, row + 1)
        for n, (cy, cz) in enumerate(((1, 0), (-1, 0), (0, 1), (0, -1))):
            store_pair(turned_ref, moved(centre, cy, cz), n, row)

    def phase_adjoints(i, h):
        at = [gamma_wide_ref[i + 2, h, :], gamma_wide_ref[i + 4, h, :], gamma_wide_ref[i, h, :]]
        return at + [turned_ref[n, i, h, :] for n in range(4)]

    for row, got, dirs in ((0, got_left, TO_LEFT), (3, got_right, TO_RIGHT)):
        for t in range(2):
            for n, h in enumerate(HALVES):
                i = 2 * row + t
                s, pressure, fluid = prim_at(prims, row, t, h)
                adj = {q: pair[t][8 * n : 8 * n + 8] for q, pair in zip(dirs, got[:5])}
                g = phase_adjoints(i, h)
                n1 = [0.125 * (g[a] - g[a + 1]) for a in (1, 3, 5)]
                m0, m1, m2 = moments_of(adj)
                if t == 1:
                    d_grad, d_lap = pull_stencil(s, m0, m1, m2, n1)[:2]
                else:
                    n0 = 0.25 * g[0] + 0.125 * total(g[1:])
                    kept = total([a * main_ref[7 + q, row, h, :] for q, a in adj.items()])
                    d_flow, d_phi, d_grad, d_lap = pull_all(s, pressure, adj, kept, m0, m1, m2, n0, n1)
                    for q in range(19):
                        more = jnp.where(fluid, d_flow[q], adj.get(BACK[q], 0.0))
                        f_ref[q, row, h, :] = flow_ref[q, row, h, :] + more
                    dphi_ref[row, h, :] = dphi_in_ref[row, h, :] + jnp.where(fluid, d_phi, 0.0)
                for k in range(3):
                    back_ref[k, i, h, :] = back_in_ref[k, i, h, :] + jnp.where(fluid, d_grad[k], 0.0)
                back_ref[3, i, h, :] = back_in_ref[3, i, h, :] + jnp.where(fluid, d_lap, 0.0)
        send(f_ref.at[:, pl.ds(row, 1)], out_f_ref.at[:, pl.ds(row, 1)])

    edge_parts = []
    for got, prim_row, row, own, out_dirs, part, sign in (
        (got_left, -1, 0, own_first, TO_RIGHT, behind_part, 1.0),
        (got_right, 4, 3, own_last, TO_LEFT, ahead_part, -1.0),
    ):
        gamma = load_pair(gamma_wide_ref, row + 1)
        n1 = turn_gamma(both(lambda a: sign * a, gamma), own)
        pair = []
        for t in range(2):
            s, _, fluid = prim_at(prims, prim_row, t, slice(None))
            adj = {q: adj_ref[q, 2 * row + t] for q in out_dirs}
            m0, m1, m2 = moments_of(adj)
            d_grad, d_lap = pull_stencil(s, m0, m1, m2, [n[t] for n in n1])[:2]
            pair.append(got[7][t] + jnp.where(fluid, part(d_grad[0], d_lap), 0.0))
        edge_parts.append(tuple(pair))

    for row in range(4):
        rest = stencil_back(back_ref, None, row, edge_parts[0], edge_parts[1])[0]
        ref, at = spot(prims, row)
        fluid = ref[9, 2 * at] > 0.5
        base = rest + dphi_ref[row]
        phase_adj = phase_adjoints(2 * row, slice(None))
        for q in range(7):
            g_ref[q, row] = jnp.where(fluid, base - 0.25 * phase_adj[q], rest + phase_adj[BACK[q]])
    send(g_ref, out_g_ref)
    for copy in copies:
        copy.wait()


def call(kernel, outs, n_in, scratch=(), flops=0, name=None, any_in=0, any_out=False):
    vmem = pl.BlockSpec(memory_space=pltpu.VMEM)
    return pl.pallas_call(
        kernel,
        out_shape=[jax.ShapeDtypeStruct(x, F32) if isinstance(x, tuple) else x for x in outs],
        in_specs=[pl.BlockSpec(memory_space=pl.ANY)] * any_in + [vmem] * (n_in - any_in),
        out_specs=[pl.BlockSpec(memory_space=pl.ANY) if any_out else vmem] * len(outs),
        scratch_shapes=[pltpu.VMEM(x, F32) if isinstance(x, tuple) else x for x in scratch],
        compiler_params=pltpu.CompilerParams(vmem_limit_bytes=VMEM_LIMIT),
        cost_estimate=pl.CostEstimate(flops=flops, bytes_accessed=flops // 8, transcendentals=0),
        name=name,
    )


def swap(x, axis, first):
    pairs = []
    for i in range(first, lax.axis_size(axis) - 1, 2):
        pairs += [(i, i + 1), (i + 1, i)]
    return lax.ppermute(x, axis, pairs)


def shards(phase_init, flow_init, solid_mask, sensor_cells, sensor_weights):
    tile = (16, 128)
    cells = sensor_cells.reshape(3, -1, 128).transpose(1, 0, 2)
    weights = sensor_weights.reshape(-1, 128)
    main, probes, weights, odd, even = call(
        rim_kernel,
        [(27, 4) + tile, jax.ShapeDtypeStruct((3,) + weights.shape, jnp.int32), weights.shape] + [(2, 4) + tile] * 2,
        5, any_in=5, flops=10**6, name="rim",
        scratch=[pltpu.VMEM((4,) + tile, jnp.int32), pltpu.SemaphoreType.DMA((10,))],
    )(*(pltpu.with_memory_space_constraint(x, pltpu.HBM) for x in (phase_init, flow_init, solid_mask, cells, weights)))
    odd, even = swap(odd, "vert", 1), swap(even, "vert", 0)
    (seeds,) = call(probe_kernel, [(9, 12) + tile], 2, scratch=[(192, 144), pltpu.VMEM(weights.shape, jnp.int32)], flops=2 * 10**9, name="probes")(
        probes, weights
    )
    first = message_tiles(N_FIRST, WIDE_FIRST)
    rim, phase, odd, even = call(
        ring_kernel, [(27, 4) + tile, (8,) + tile] + [(first,) + tile] * 2, 4, any_in=1, flops=10**7, name="ring"
    )(seeds, main, odd, even)
    odd, even = swap(odd, "tile", 1), swap(even, "tile", 0)
    prim_in, post_in, moments = call(
        inner_kernel, [(10, 4) + tile, (26, 4) + tile, (10, 8) + tile], 4, flops=2 * 10**8, name="inner"
    )(main, rim, phase, seeds)
    second = message_tiles(N_SECOND)
    prim_out, adj, gamma, edges, odd, even = call(
        middle_kernel,
        [(10, 8) + tile, (19, 8) + tile, (8,) + tile, (4,) + tile] + [(second,) + tile] * 2,
        9,
        scratch=[(26, 8) + tile, (12,) + tile, (4, 8) + tile, (4, 8) + tile, (8,) + tile],
        flops=10**8, name="middle",
    )(main, rim, phase, odd, even, seeds, moments, prim_in, post_in)
    odd, even = swap(odd, "tile", 1), swap(even, "tile", 0)
    flow, back, dphi = call(
        ahead_kernel, [(19, 4) + tile, (4, 8) + tile, (4,) + tile], 5, scratch=[(4, 4) + tile], flops=2 * 10**8,
        name="ahead",
    )(main, prim_in, prim_out, adj, gamma)
    return tuple(
        call(
            last_kernel,
            [(7, 4) + tile, (19, 4) + tile],
            11,
            scratch=[
                (12,) + tile, (4, 8) + tile, (4, 8) + tile, (4,) + tile, (7, 4) + tile, (19, 4) + tile,
                pltpu.SemaphoreType.DMA((4,)),
            ],
            flops=10**8, name="last", any_out=True,
        )(main, prim_in, prim_out, adj, gamma, edges, flow, back, dphi, odd, even)
    )


def solution(mesh):
    return jax.shard_map(
        shards,
        mesh=mesh,
        in_specs=(
            P(None, "tile", None, "vert"),
            P(None, "tile", None, "vert"),
            P("tile", None, "vert"),
            P(),
            P(),
        ),
        out_specs=(P(None, "tile", None, "vert"), P(None, "tile", None, "vert")),
        check_vma=False,
    )
```

time: 53.4 us -> 38.7 us (0.72)
  the two profiles are of different devices: /device:TPU:25 before, /device:TPU:24 now
where the time goes in v2:
time: 38.7 us; the launch traced here: 38.5 us
  starting transfers between devices  20.5 us (53%)
  Pallas kernels  9.24 us (24%)
  waiting for transfers between devices  8.04 us (21%)
  between operations  0.73 us (2%)
    ppermute x6, starting transfers between devices, swap(): return lax.ppermute(x, axis, pairs)  20.5 us
    ppermute x6, waiting for transfers between devices, swap(): return lax.ppermute(x, axis, pairs)  8.04 us
    pallas_call x1, Pallas kernels, shards(): call(middle_kernel, [(10, 8) + tile, (19, 8) + tile, (8,) + tile, (4,) +...  2.13 us
    pallas_call x1, Pallas kernels, shards(): call(rim_kernel, [(27, 4) + tile, jax.ShapeDtypeStruct((3,) + weights.sha...  1.84 us
    pallas_call x1, Pallas kernels, shards(): call(probe_kernel, [(9, 12) + tile], 2, scratch=[(192, 144), pltpu.VMEM(w...  1.66 us
    pallas_call x1, Pallas kernels, shards(): call(last_kernel, [(7, 4) + tile, (19, 4) + tile], 11, scratch=[(12,) + t...  1.34 us
    pallas_call x1, Pallas kernels, shards(): call(ring_kernel, [(27, 4) + tile, (8,) + tile] + [(first,) + tile] * 2,...  0.79 us
  transfers between devices with their start and end apart: 6, of which 4 were waited for; matrix products, arithmetic and copies ran while one was open for 0% of the time, Pallas kernels for 8%

profile of v2, /device:TPU:24, one launch (start us, length us, event | category | flops | bytes accessed | tf_op | source)
XLA Modules:
  0.0 38.5 jit_solution(4702912117422948820)
XLA Ops:
  0.6 1.8 %rim.1 = (f32[27,4,16,128]{3,2,1,0:T(8,128)S(1)}, s32[3,256,128]{2,1,0:T(8,128)S(1)}, f32[256,128]{1,0:T(8,128)S(1)}, f32[2,4,16,128]{3,2,1,0:T(8,128)S(1)}, f32[2,4,16,128]{3,2,1,0:T(8,128)S(1)}) custom-call(f32[7,4,16,128]{3,2,1,0:T(8,128)} %g_ref.1, f32[19,4,16,128]{3,2,1,0:T(8,128)} %f_ref.1, s32[4,16,128]{2,1,0:T(8,128)} %solid_ref.1, ...), custom_call_target="tpu_custom_call" | custom-call | flops 1000000 | bytes 125000 | tf_op jit(solution)/shard_map/rim/pallas_call | solution.py:977
  2.5 0.7 %collective-permute-start = (f32[2,4,16,128]{3,2,1,0:T(8,128)S(1)}, f32[2,4,16,128]{3,2,1,0:T(8,128)S(1)}, u32[]{:S(2)}, u32[]{:S(2)}) collective-permute-start(f32[2,4,16,128]{3,2,1,0:T(8,128)S(1)} %get-tuple-element.26), channel_id=1, source_target_pairs={{1,2},{2,1},{5,6},{6,5},{9,10},{10,9},{13,14},{14,13},{17,18},{18,... | collective-permute-start | bytes 196616 | tf_op jit(solution)/shard_map/ppermute | solution.py:970
  3.2 2.9 %collective-permute-start.1 = (f32[2,4,16,128]{3,2,1,0:T(8,128)S(1)}, f32[2,4,16,128]{3,2,1,0:T(8,128)S(1)}, u32[]{:S(2)}, u32[]{:S(2)}) collective-permute-start(f32[2,4,16,128]{3,2,1,0:T(8,128)S(1)} %get-tuple-element.27), channel_id=1, source_target_pairs={{0,1},{1,0},{2,3},{3,2},{4,5},{5,4},{6,7},{7,6},{8,9},{9,8},{10,11... | collective-permute-start | bytes 196616 | tf_op jit(solution)/shard_map/ppermute | solution.py:970
  6.1 1.7 %probes.1.seeds_ref = f32[9,12,16,128]{3,2,1,0:T(8,128)S(1)} custom-call(s32[3,256,128]{2,1,0:T(8,128)S(1)} %get-tuple-element.24.probes_ref, f32[256,128]{1,0:T(8,128)S(1)} %get-tuple-element.25.weights_ref), custom_call_target="tpu_custom_call" | custom-call | flops 2000000000 | bytes 250000000 | tf_op jit(solution)/shard_map/probes/pallas_call | solution.py:984
  7.8 0.0 collective-permute-done.odd_in_ref
  7.8 0.0 collective-permute-done.1.even_in_ref
  7.8 0.8 %ring.1 = (f32[27,4,16,128]{3,2,1,0:T(8,128)S(1)}, f32[8,16,128]{2,1,0:T(8,128)S(1)}, f32[14,16,128]{2,1,0:T(8,128)S(1)}, f32[14,16,128]{2,1,0:T(8,128)S(1)}) custom-call(f32[9,12,16,128]{3,2,1,0:T(8,128)S(1)} %probes.1.seeds_ref, f32[27,4,16,128]{3,2,1,0:T(8,128)S(1)} %get-tuple-element.23.main_ref, f32[2,4,16,128]{3,2,1,0:T(8,128)S(1)} %collective-permute-done.odd_in_ref, ...), custom_call_target="tpu_custom_call" | custom-call | flops 10000000 | bytes 1250000 | tf_op jit(solution)/shard_map/ring/pallas_call | solution.py:988
  8.6 10.1 %collective-permute-start.2 = (f32[14,16,128]{2,1,0:T(8,128)S(1)}, f32[14,16,128]{2,1,0:T(8,128)S(1)}, u32[]{:S(2)}, u32[]{:S(2)}) collective-permute-start(f32[14,16,128]{2,1,0:T(8,128)S(1)} %get-tuple-element.31), channel_id=1, source_target_pairs={{4,8},{8,4},{12,16},{16,12},{20,24},{24,20},{28,32},{32,28},{36,40... | collective-permute-start | bytes 344072 | tf_op jit(solution)/shard_map/ppermute | solution.py:970
  18.7 0.1 collective-permute-start.3
  18.8 0.7 %inner.1 = (f32[10,4,16,128]{3,2,1,0:T(8,128)S(1)}, f32[26,4,16,128]{3,2,1,0:T(8,128)S(1)}, f32[10,8,16,128]{3,2,1,0:T(8,128)S(1)}) custom-call(f32[27,4,16,128]{3,2,1,0:T(8,128)S(1)} %get-tuple-element.23.main_ref, f32[27,4,16,128]{3,2,1,0:T(8,128)S(1)} %get-tuple-element.28.rim_ref, f32[8,16,128]{2,1,0:T(8,128)S(1)} %get-tuple-element.29.phase_ref, ...), custom_call_target="tpu_custom_call" | custom-call | flops 200000000 | bytes 25000000 | tf_op jit(solution)/shard_map/inner/pallas_call | solution.py:992
  19.5 2.9 %collective-permute-done.2.odd_in_ref = f32[14,16,128]{2,1,0:T(8,128)S(1)} collective-permute-done((f32[14,16,128]{2,1,0:T(8,128)S(1)}, f32[14,16,128]{2,1,0:T(8,128)S(1)}, u32[]{:S(2)}, u32[]{:S(2)}) %collective-permute-start.2) | collective-permute-done | bytes 114720 | tf_op jit(solution)/shard_map/ppermute | solution.py:970
  22.4 1.6 %collective-permute-done.3.even_in_ref = f32[14,16,128]{2,1,0:T(8,128)S(1)} collective-permute-done((f32[14,16,128]{2,1,0:T(8,128)S(1)}, f32[14,16,128]{2,1,0:T(8,128)S(1)}, u32[]{:S(2)}, u32[]{:S(2)}) %collective-permute-start.3) | collective-permute-done | bytes 114720 | tf_op jit(solution)/shard_map/ppermute | solution.py:970
  24.0 2.1 %middle.1 = (f32[10,8,16,128]{3,2,1,0:T(8,128)S(1)}, f32[19,8,16,128]{3,2,1,0:T(8,128)S(1)}, f32[8,16,128]{2,1,0:T(8,128)S(1)}, f32[4,16,128]{2,1,0:T(8,128)S(1)...) custom-call(f32[27,4,16,128]{3,2,1,0:T(8,128)S(1)} %get-tuple-element.23.main_ref, ...), custom_call_target="tpu_custom_call" | custom-call | flops 100000000 | bytes 12500000 | tf_op jit(solution)/shard_map/middle/pallas_call | solution.py:996
  26.1 6.6 %collective-permute-start.4 = (f32[9,16,128]{2,1,0:T(8,128)S(1)}, f32[9,16,128]{2,1,0:T(8,128)S(1)}, u32[]{:S(2)}, u32[]{:S(2)}) collective-permute-start(f32[9,16,128]{2,1,0:T(8,128)S(1)} %get-tuple-element.42), channel_id=1, source_target_pairs={{4,8},{8,4},{12,16},{16,12},{20,24},{24,20},{28,32},{32,28},{36,40... | collective-permute-start | bytes 221192 | tf_op jit(solution)/shard_map/ppermute | solution.py:970
  32.7 0.1 collective-permute-start.5
  32.8 0.7 %ahead.1 = (f32[19,4,16,128]{3,2,1,0:T(8,128)S(1)}, f32[4,8,16,128]{3,2,1,0:T(8,128)S(1)}, f32[4,16,128]{2,1,0:T(8,128)S(1)}) custom-call(f32[27,4,16,128]{3,2,1,0:T(8,128)S(1)} %get-tuple-element.23.main_ref, f32[10,4,16,128]{3,2,1,0:T(8,128)S(1)} %get-tuple-element.30.prim_in_ref, f32[10,8,16,128]{3,2,1,0:T(8,128)S(1)} %get-tuple-element.35.prim_out_ref, ...), custom_call_target="tpu_custom_call" | custom-call | flops 200000000 | bytes 25000000 | tf_op jit(solution)/shard_map/ahead/pallas_call | solution.py:1004
  33.6 3.3 %collective-permute-done.4.odd_in_ref = f32[9,16,128]{2,1,0:T(8,128)S(1)} collective-permute-done((f32[9,16,128]{2,1,0:T(8,128)S(1)}, f32[9,16,128]{2,1,0:T(8,128)S(1)}, u32[]{:S(2)}, u32[]{:S(2)}) %collective-permute-start.4) | collective-permute-done | bytes 73760 | tf_op jit(solution)/shard_map/ppermute | solution.py:970
  36.9 0.3 collective-permute-done.5.even_in_ref
  37.2 1.3 %last.1 = (f32[7,4,16,128]{3,2,1,0:T(8,128)}, f32[19,4,16,128]{3,2,1,0:T(8,128)}) custom-call(f32[27,4,16,128]{3,2,1,0:T(8,128)S(1)} %get-tuple-element.23.main_ref, f32[10,4,16,128]{3,2,1,0:T(8,128)S(1)} %get-tuple-element.30.prim_in_ref, f32[10,8,16,128]{3,2,1,0:T(8,128)S(1)} %get-tuple-element.35.prim_out_ref, ...), custom_call_target="tpu_custom_call" | custom-call | flops 100000000 | bytes 12500000 | tf_op jit(solution)/shard_map/last/pallas_call | solution.py:1009
Async XLA Ops:
  2.5 5.3 %collective-permute-start = (f32[2,4,16,128]{3,2,1,0:T(8,128)S(1)}, f32[2,4,16,128]{3,2,1,0:T(8,128)S(1)}, u32[]{:S(2)}, u32[]{:S(2)}) collective-permute-start(f32[2,4,16,128]{3,2,1,0:T(8,128)S(1)} %get-tuple-element.26), channel_id=1, source_target_pairs={{1,2},{2,1},{5,6},{6,5},{9,10},{10,9},{13,14},{14,13},{17,18},{18,... | collective-permute-start | bytes 196616 | tf_op jit(solution)/shard_map/ppermute | solution.py:970
  3.2 4.6 %collective-permute-start.1 = (f32[2,4,16,128]{3,2,1,0:T(8,128)S(1)}, f32[2,4,16,128]{3,2,1,0:T(8,128)S(1)}, u32[]{:S(2)}, u32[]{:S(2)}) collective-permute-start(f32[2,4,16,128]{3,2,1,0:T(8,128)S(1)} %get-tuple-element.27), channel_id=1, source_target_pairs={{0,1},{1,0},{2,3},{3,2},{4,5},{5,4},{6,7},{7,6},{8,9},{9,8},{10,11... | collective-permute-start | bytes 196616 | tf_op jit(solution)/shard_map/ppermute | solution.py:970
  8.6 13.8 %collective-permute-start.2 = (f32[14,16,128]{2,1,0:T(8,128)S(1)}, f32[14,16,128]{2,1,0:T(8,128)S(1)}, u32[]{:S(2)}, u32[]{:S(2)}) collective-permute-start(f32[14,16,128]{2,1,0:T(8,128)S(1)} %get-tuple-element.31), channel_id=1, source_target_pairs={{4,8},{8,4},{12,16},{16,12},{20,24},{24,20},{28,32},{32,28},{36,40... | collective-permute-start | bytes 344072 | tf_op jit(solution)/shard_map/ppermute | solution.py:970
  18.7 5.3 %collective-permute-start.3 = (f32[14,16,128]{2,1,0:T(8,128)S(1)}, f32[14,16,128]{2,1,0:T(8,128)S(1)}, u32[]{:S(2)}, u32[]{:S(2)}) collective-permute-start(f32[14,16,128]{2,1,0:T(8,128)S(1)} %get-tuple-element.32), channel_id=1, source_target_pairs={{0,4},{4,0},{8,12},{12,8},{16,20},{20,16},{24,28},{28,24},{32,36},... | collective-permute-start | bytes 344072 | tf_op jit(solution)/shard_map/ppermute | solution.py:970
  26.1 10.8 %collective-permute-start.4 = (f32[9,16,128]{2,1,0:T(8,128)S(1)}, f32[9,16,128]{2,1,0:T(8,128)S(1)}, u32[]{:S(2)}, u32[]{:S(2)}) collective-permute-start(f32[9,16,128]{2,1,0:T(8,128)S(1)} %get-tuple-element.42), channel_id=1, source_target_pairs={{4,8},{8,4},{12,16},{16,12},{20,24},{24,20},{28,32},{32,28},{36,40... | collective-permute-start | bytes 221192 | tf_op jit(solution)/shard_map/ppermute | solution.py:970
  32.7 4.4 %collective-permute-start.5 = (f32[9,16,128]{2,1,0:T(8,128)S(1)}, f32[9,16,128]{2,1,0:T(8,128)S(1)}, u32[]{:S(2)}, u32[]{:S(2)}) collective-permute-start(f32[9,16,128]{2,1,0:T(8,128)S(1)} %get-tuple-element.43), channel_id=1, source_target_pairs={{0,4},{4,0},{8,12},{12,8},{16,20},{20,16},{24,28},{28,24},{32,36},... | collective-permute-start | bytes 221192 | tf_op jit(solution)/shard_map/ppermute | solution.py:970

commit v3 on v2

--- a/solution.py
+++ b/solution.py
@@ -105,8 +105,12 @@
     odd = is_odd("tile")
     slots = rim_slots(count, wide)
     tiles = message_tiles(count, wide)
-    got_odd = [odd_ref[n] for n in range(tiles)]
-    got_even = [even_ref[n] for n in range(tiles)]
+    at = lax.axis_index("tile")
+    last = lax.axis_size("tile") - 1
+    parity = lax.rem(at, 2)
+    ends = jnp.full((16, 128), jnp.where((at == 0) | (at == last), 1, 0), jnp.int32) == 1
+    got_odd = [jnp.where(ends, 0.0, odd_ref[parity, n]) for n in range(tiles)]
+    got_even = [even_ref[1 - parity, n] for n in range(tiles)]
     sides = []
     for one, two in ((got_even, got_odd), (got_odd, got_even)):
         msg = [jnp.where(odd, a, b) for a, b in zip(one, two)]
@@ -970,6 +974,12 @@
     return lax.ppermute(x, axis, pairs)
 
 
+def pair_gather(x, axis, first):
+    size = lax.axis_size(axis)
+    groups = [[i, (i + 1) % size] for i in range(first, size, 2)]
+    return lax.all_gather(x, axis, axis_index_groups=groups)
+
+
 def shards(phase_init, flow_init, solid_mask, sensor_cells, sensor_weights):
     tile = (16, 128)
     cells = sensor_cells.reshape(3, -1, 128).transpose(1, 0, 2)
@@ -988,7 +998,7 @@
     rim, phase, odd, even = call(
         ring_kernel, [(27, 4) + tile, (8,) + tile] + [(first,) + tile] * 2, 4, any_in=1, flops=10**7, name="ring"
     )(seeds, main, odd, even)
-    odd, even = swap(odd, "tile", 1), swap(even, "tile", 0)
+    odd, even = pair_gather(odd, "tile", 1), pair_gather(even, "tile", 0)
     prim_in, post_in, moments = call(
         inner_kernel, [(10, 4) + tile, (26, 4) + tile, (10, 8) + tile], 4, flops=2 * 10**8, name="inner"
     )(main, rim, phase, seeds)
@@ -1000,7 +1010,7 @@
         scratch=[(26, 8) + tile, (12,) + tile, (4, 8) + tile, (4, 8) + tile, (8,) + tile],
         flops=10**8, name="middle",
     )(main, rim, phase, odd, even, seeds, moments, prim_in, post_in)
-    odd, even = swap(odd, "tile", 1), swap(even, "tile", 0)
+    odd, even = pair_gather(odd, "tile", 1), pair_gather(even, "tile", 0)
     flow, back, dphi = call(
         ahead_kernel, [(19, 4) + tile, (4, 8) + tile, (4,) + tile], 5, scratch=[(4, 4) + tile], flops=2 * 10**8,
         name="ahead",

time: 38.7 us -> 48.5 us (1.25)
  the two profiles are of different devices: /device:TPU:24 before, /device:TPU:2 now
where the time goes in v3:
time: 48.5 us; the launch traced here: 48.4 us
  blocking collectives  34.5 us (71%)
  Pallas kernels  8.91 us (18%)
  waiting for transfers between devices  2.24 us (5%)
  starting transfers between devices  2.01 us (4%)
  between operations  0.69 us (1%)
    all_gather x4, blocking collectives, pair_gather(): return lax.all_gather(x, axis, axis_index_groups=groups)  34.5 us
    ppermute x2, waiting for transfers between devices, swap(): return lax.ppermute(x, axis, pairs)  2.24 us
    pallas_call x1, Pallas kernels, shards(): call(middle_kernel, [(10, 8) + tile, (19, 8) + tile, (8,) + tile, (4,) +...  2.14 us
    ppermute x2, starting transfers between devices, swap(): return lax.ppermute(x, axis, pairs)  2.01 us
    pallas_call x1, Pallas kernels, shards(): call(rim_kernel, [(27, 4) + tile, jax.ShapeDtypeStruct((3,) + weights.sha...  1.84 us
    pallas_call x1, Pallas kernels, shards(): call(last_kernel, [(7, 4) + tile, (19, 4) + tile], 11, scratch=[(12,) + t...  1.36 us
    pallas_call x1, Pallas kernels, shards(): call(probe_kernel, [(9, 12) + tile], 2, scratch=[(192, 144), pltpu.VMEM(w...  1.31 us
  transfers between devices with their start and end apart: 2, of which 1 were waited for; matrix products, arithmetic and copies ran while one was open for 0% of the time, Pallas kernels for 3%

profile of v3, /device:TPU:2, one launch (start us, length us, event | category | flops | bytes accessed | tf_op | source)
XLA Modules:
  0.0 48.4 jit_solution(1813395066624905469)
XLA Ops:
  0.6 1.8 %rim.1 = (f32[27,4,16,128]{3,2,1,0:T(8,128)S(1)}, s32[3,256,128]{2,1,0:T(8,128)S(1)}, f32[256,128]{1,0:T(8,128)S(1)}, f32[2,4,16,128]{3,2,1,0:T(8,128)S(1)}, f32[2,4,16,128]{3,2,1,0:T(8,128)S(1)}) custom-call(f32[7,4,16,128]{3,2,1,0:T(8,128)} %g_ref.1, f32[19,4,16,128]{3,2,1,0:T(8,128)} %f_ref.1, s32[4,16,128]{2,1,0:T(8,128)} %solid_ref.1, ...), custom_call_target="tpu_custom_call" | custom-call | flops 1000000 | bytes 125000 | tf_op jit(solution)/shard_map/rim/pallas_call | solution.py:987
  2.5 1.9 %collective-permute-start = (f32[2,4,16,128]{3,2,1,0:T(8,128)S(1)}, f32[2,4,16,128]{3,2,1,0:T(8,128)S(1)}, u32[]{:S(2)}, u32[]{:S(2)}) collective-permute-start(f32[2,4,16,128]{3,2,1,0:T(8,128)S(1)} %get-tuple-element.26), channel_id=1, source_target_pairs={{1,2},{2,1},{5,6},{6,5},{9,10},{10,9},{13,14},{14,13},{17,18},{18,... | collective-permute-start | bytes 196616 | tf_op jit(solution)/shard_map/ppermute | solution.py:974
  4.4 0.1 collective-permute-start.1
  4.5 1.3 %probes.1.seeds_ref = f32[9,12,16,128]{3,2,1,0:T(8,128)S(1)} custom-call(s32[3,256,128]{2,1,0:T(8,128)S(1)} %get-tuple-element.24.probes_ref, f32[256,128]{1,0:T(8,128)S(1)} %get-tuple-element.25.weights_ref), custom_call_target="tpu_custom_call" | custom-call | flops 2000000000 | bytes 250000000 | tf_op jit(solution)/shard_map/probes/pallas_call | solution.py:994
  5.8 2.2 %collective-permute-done.odd_in_ref = f32[2,4,16,128]{3,2,1,0:T(8,128)S(1)} collective-permute-done((f32[2,4,16,128]{3,2,1,0:T(8,128)S(1)}, f32[2,4,16,128]{3,2,1,0:T(8,128)S(1)}, u32[]{:S(2)}, u32[]{:S(2)}) %collective-permute-start) | collective-permute-done | bytes 65568 | tf_op jit(solution)/shard_map/ppermute | solution.py:974
  8.1 0.0 collective-permute-done.1.even_in_ref
  8.1 0.8 %ring.1 = (f32[27,4,16,128]{3,2,1,0:T(8,128)S(1)}, f32[8,16,128]{2,1,0:T(8,128)S(1)}, f32[14,16,128]{2,1,0:T(8,128)S(1)}, f32[14,16,128]{2,1,0:T(8,128)S(1)}) custom-call(f32[9,12,16,128]{3,2,1,0:T(8,128)S(1)} %probes.1.seeds_ref, f32[27,4,16,128]{3,2,1,0:T(8,128)S(1)} %get-tuple-element.23.main_ref, f32[2,4,16,128]{3,2,1,0:T(8,128)S(1)} %collective-permute-done.odd_in_ref, ...), custom_call_target="tpu_custom_call" | custom-call | flops 10000000 | bytes 1250000 | tf_op jit(solution)/shard_map/ring/pallas_call | solution.py:998
  8.9 13.3 %all-gather = f32[28,16,128]{2,1,0:T(8,128)S(1)} all-gather(f32[14,16,128]{2,1,0:T(8,128)S(1)} %get-tuple-element.31), channel_id=2, replica_groups={{4,8},{12,16},{20,24},{28,32},{36,40},{44,48},{52,56},{60,64},{68,72},{..., dimensions={0}, use_global_device_ids=true | all-gather | bytes 344064 | tf_op jit(solution)/shard_map/all_gather | solution.py:980
  22.2 5.5 %all-gather.1 = f32[28,16,128]{2,1,0:T(8,128)S(1)} all-gather(f32[14,16,128]{2,1,0:T(8,128)S(1)} %get-tuple-element.32), channel_id=3, replica_groups={{0,4},{8,12},{16,20},{24,28},{32,36},{40,44},{48,52},{56,60},{64,68},{7..., dimensions={0}, use_global_device_ids=true | all-gather | bytes 344064 | tf_op jit(solution)/shard_map/all_gather | solution.py:980
  27.6 0.7 %inner.1 = (f32[10,4,16,128]{3,2,1,0:T(8,128)S(1)}, f32[26,4,16,128]{3,2,1,0:T(8,128)S(1)}, f32[10,8,16,128]{3,2,1,0:T(8,128)S(1)}) custom-call(f32[27,4,16,128]{3,2,1,0:T(8,128)S(1)} %get-tuple-element.23.main_ref, f32[27,4,16,128]{3,2,1,0:T(8,128)S(1)} %get-tuple-element.28.rim_ref, f32[8,16,128]{2,1,0:T(8,128)S(1)} %get-tuple-element.29.phase_ref, ...), custom_call_target="tpu_custom_call" | custom-call | flops 200000000 | bytes 25000000 | tf_op jit(solution)/shard_map/inner/pallas_call | solution.py:1002
  28.4 2.1 %middle.1 = (f32[10,8,16,128]{3,2,1,0:T(8,128)S(1)}, f32[19,8,16,128]{3,2,1,0:T(8,128)S(1)}, f32[8,16,128]{2,1,0:T(8,128)S(1)}, f32[4,16,128]{2,1,0:T(8,128)S(1)...) custom-call(f32[27,4,16,128]{3,2,1,0:T(8,128)S(1)} %get-tuple-element.23.main_ref, ...), custom_call_target="tpu_custom_call" | custom-call | flops 100000000 | bytes 12500000 | tf_op jit(solution)/shard_map/middle/pallas_call | solution.py:1006
  30.5 10.7 %all-gather.2 = f32[18,16,128]{2,1,0:T(8,128)S(1)} all-gather(f32[9,16,128]{2,1,0:T(8,128)S(1)} %get-tuple-element.42), channel_id=4, replica_groups={{4,8},{12,16},{20,24},{28,32},{36,40},{44,48},{52,56},{60,64},{68,72},{..., dimensions={0}, use_global_device_ids=true | all-gather | bytes 221184 | tf_op jit(solution)/shard_map/all_gather | solution.py:980
  41.2 5.0 %all-gather.3 = f32[18,16,128]{2,1,0:T(8,128)S(1)} all-gather(f32[9,16,128]{2,1,0:T(8,128)S(1)} %get-tuple-element.43), channel_id=5, replica_groups={{0,4},{8,12},{16,20},{24,28},{32,36},{40,44},{48,52},{56,60},{64,68},{7..., dimensions={0}, use_global_device_ids=true | all-gather | bytes 221184 | tf_op jit(solution)/shard_map/all_gather | solution.py:980
  46.3 0.7 %ahead.1 = (f32[19,4,16,128]{3,2,1,0:T(8,128)S(1)}, f32[4,8,16,128]{3,2,1,0:T(8,128)S(1)}, f32[4,16,128]{2,1,0:T(8,128)S(1)}) custom-call(f32[27,4,16,128]{3,2,1,0:T(8,128)S(1)} %get-tuple-element.23.main_ref, f32[10,4,16,128]{3,2,1,0:T(8,128)S(1)} %get-tuple-element.30.prim_in_ref, f32[10,8,16,128]{3,2,1,0:T(8,128)S(1)} %get-tuple-element.35.prim_out_ref, ...), custom_call_target="tpu_custom_call" | custom-call | flops 200000000 | bytes 25000000 | tf_op jit(solution)/shard_map/ahead/pallas_call | solution.py:1014
  47.0 1.4 %last.1 = (f32[7,4,16,128]{3,2,1,0:T(8,128)}, f32[19,4,16,128]{3,2,1,0:T(8,128)}) custom-call(f32[27,4,16,128]{3,2,1,0:T(8,128)S(1)} %get-tuple-element.23.main_ref, f32[10,4,16,128]{3,2,1,0:T(8,128)S(1)} %get-tuple-element.30.prim_in_ref, f32[10,8,16,128]{3,2,1,0:T(8,128)S(1)} %get-tuple-element.35.prim_out_ref, ...), custom_call_target="tpu_custom_call" | custom-call | flops 100000000 | bytes 12500000 | tf_op jit(solution)/shard_map/last/pallas_call | solution.py:1019
Async XLA Ops:
  2.5 5.6 %collective-permute-start = (f32[2,4,16,128]{3,2,1,0:T(8,128)S(1)}, f32[2,4,16,128]{3,2,1,0:T(8,128)S(1)}, u32[]{:S(2)}, u32[]{:S(2)}) collective-permute-start(f32[2,4,16,128]{3,2,1,0:T(8,128)S(1)} %get-tuple-element.26), channel_id=1, source_target_pairs={{1,2},{2,1},{5,6},{6,5},{9,10},{10,9},{13,14},{14,13},{17,18},{18,... | collective-permute-start | bytes 196616 | tf_op jit(solution)/shard_map/ppermute | solution.py:974
  4.4 3.7 %collective-permute-start.1 = (f32[2,4,16,128]{3,2,1,0:T(8,128)S(1)}, f32[2,4,16,128]{3,2,1,0:T(8,128)S(1)}, u32[]{:S(2)}, u32[]{:S(2)}) collective-permute-start(f32[2,4,16,128]{3,2,1,0:T(8,128)S(1)} %get-tuple-element.27), channel_id=1, source_target_pairs={{0,1},{1,0},{2,3},{3,2},{4,5},{5,4},{6,7},{7,6},{8,9},{9,8},{10,11... | collective-permute-start | bytes 196616 | tf_op jit(solution)/shard_map/ppermute | solution.py:974

commit v4 on v2

--- a/solution.py
+++ b/solution.py
@@ -369,42 +369,38 @@
     g_ref, f_ref, solid_ref, cells_ref, weights_ref,
     main_ref, probes_ref, probe_weights_ref, odd_ref, even_ref, mask_ref, sems,
 ):
-    copies = [pltpu.make_async_copy(solid_ref, mask_ref, sems.at[0])]
-    copies.append(pltpu.make_async_copy(g_ref, main_ref.at[pl.ds(0, 7)], sems.at[1]))
+    parts = [(range(0, 7), pltpu.make_async_copy(g_ref, main_ref.at[pl.ds(0, 7)], sems.at[1]))]
     for n, (first, count) in enumerate(((0, 5), (5, 5), (10, 5), (15, 4))):
-        copies.append(
-            pltpu.make_async_copy(
-                f_ref.at[pl.ds(first, count)], main_ref.at[pl.ds(7 + first, count)], sems.at[2 + n]
-            )
+        copy = pltpu.make_async_copy(
+            f_ref.at[pl.ds(first, count)], main_ref.at[pl.ds(7 + first, count)], sems.at[2 + n]
         )
+        parts.append((range(7 + first, 7 + first + count), copy))
+    parts.append((range(FLUID, FLUID + 1), pltpu.make_async_copy(solid_ref, mask_ref, sems.at[0])))
     later = [pltpu.make_async_copy(weights_ref, probe_weights_ref, sems.at[6])]
     for i in range(3):
         later.append(pltpu.make_async_copy(cells_ref.at[:, i, :], probes_ref.at[i], sems.at[7 + i]))
-    for copy in copies + later:
+    for _, copy in parts:
         copy.start()
-    for copy in copies:
-        copy.wait()
+    for copy in later:
+        copy.start()
     lane = lanes()
     odd = is_odd("vert")
-
-    def row(x, carry):
-        main_ref[FLUID, x] = 1.0 - mask_ref[x].astype(F32)
-        for tile in range(2):
-            up = jnp.zeros((16, 128), F32)
-            down = jnp.zeros((16, 128), F32)
-            for slot in range(16):
-                k = 16 * tile + slot
-                if k > FLUID:
-                    continue
-                cells = main_ref[k, x]
-                turned = roll(cells, 8 * slot + 8, 1)
-                up = jnp.where(lane // RIM == slot, turned, up)
-                down = jnp.where(lane // RIM == (slot + 1) % 16, turned, down)
-            odd_ref[tile, x] = jnp.where(odd, up, down)
-            even_ref[tile, x] = jnp.where(odd, down, up)
-        return carry
-
-    lax.fori_loop(0, 4, row, 0)
+    up = [[jnp.zeros((16, 128), F32)] * 4 for _ in range(2)]
+    down = [[jnp.zeros((16, 128), F32)] * 4 for _ in range(2)]
+    for fields, copy in parts:
+        copy.wait()
+        for k in fields:
+            tile, slot = k // 16, k % 16
+            for x in range(4):
+                if k == FLUID:
+                    main_ref[FLUID, x] = 1.0 - mask_ref[x].astype(F32)
+                turned = roll(main_ref[k, x], 8 * slot + 8, 1)
+                up[tile][x] = jnp.where(lane // RIM == slot, turned, up[tile][x])
+                down[tile][x] = jnp.where(lane // RIM == (slot + 1) % 16, turned, down[tile][x])
+    for tile in range(2):
+        for x in range(4):
+            odd_ref[tile, x] = jnp.where(odd, up[tile][x], down[tile][x])
+            even_ref[tile, x] = jnp.where(odd, down[tile][x], up[tile][x])
     for copy in later:
         copy.wait()
 
@@ -414,7 +410,7 @@
     lane = lanes()
     odd = is_odd("vert")
 
-    def row(x, carry):
+    def row(x):
         above = [jnp.where(odd, odd_in_ref[t, x], even_in_ref[t, x]) for t in range(2)]
         below = [jnp.where(odd, even_in_ref[t, x], odd_in_ref[t, x]) for t in range(2)]
         even_group = lane // RIM % 2 == 0
@@ -431,9 +427,9 @@
                 sums = [a if b is None else a + b for a, b in zip((cells, rim), sums)]
         phase_ref[2 * x] = sums[0]
         phase_ref[2 * x + 1] = sums[1]
-        return carry
-
-    lax.fori_loop(0, 4, row, 0)
+
+    for x in (3, 2, 1, 0):
+        row(x)
 
     def cells_of(k, row):
         return (main_ref[k, row], rim_ref[k, row])
@@ -554,6 +550,7 @@
 WIDE_FIRST = (7,)
 N_SECOND = 8
 HALVES = (slice(0, 8), slice(8, 16))
+SENT_ROWS = ((0, 1), (1,), (-1,), (0, -1))
 M2_KEYS = ((0, 0), (0, 1), (0, 2), (1, 1), (1, 2), (2, 2))
 
 
@@ -735,11 +732,10 @@
             for h in HALVES:
                 backward(row, t, h)
 
-    for q in range(19):
-        _, cy, cz = DIRS[q]
-        if cy or cz:
-            for row in range(4):
-                store_pair(adj_ref, moved(load_pair(adj_ref, q, row), cy, cz), q, row)
+    for row in range(4):
+        for q in range(19):
+            if DIRS[q][1:] != (0, 0) and DIRS[q][0] in SENT_ROWS[row]:
+                store_pair(adj_ref, moved(load_pair(adj_ref, q, row), *DIRS[q][1:]), q, row)
 
     for row in range(4):
         store_pair(gamma_ref, stencil_back(back_ref, dphi_ref, row), row)
@@ -809,9 +805,20 @@
 def ahead_kernel(
     main_ref, prim_in_ref, prim_out_ref, adj_ref, gamma_ref,
     flow_ref, back_ref, dphi_ref,
-    turned_ref,
+    turned_ref, shifted_ref,
 ):
     prims = (prim_in_ref, prim_out_ref)
+    for row in range(4):
+        for q in range(19):
+            if DIRS[q][1:] != (0, 0) and DIRS[q][0] not in SENT_ROWS[row]:
+                store_pair(shifted_ref, moved(load_pair(adj_ref, q, row), *DIRS[q][1:]), q, row)
+
+    def adjoint(q, row, t, h):
+        step = DIRS[q]
+        at = row + step[0]
+        ref = adj_ref if step[1:] == (0, 0) or step[0] in SENT_ROWS[at] else shifted_ref
+        return ref[q, 2 * at + t, h, :]
+
     for row in (1, 2):
         centre = load_pair(gamma_ref, row)
         for n, (cy, cz) in enumerate(((1, 0), (-1, 0), (0, 1), (0, -1))):
@@ -821,9 +828,7 @@
             for h in HALVES:
                 i = 2 * row + t
                 s, pressure, fluid = prim_at(prims, row, t, h)
-                adj = {
-                    q: adj_ref[q, i + 2 * DIRS[q][0], h, :] for q in range(19) if 0 <= row + DIRS[q][0] < 4
-                }
+                adj = {q: adjoint(q, row, t, h) for q in range(19) if 0 <= row + DIRS[q][0] < 4}
                 m0, m1, m2 = moments_of(adj)
                 n0 = n1 = None
                 if row in (1, 2):
@@ -944,7 +949,7 @@
         phase_adj = phase_adjoints(2 * row, slice(None))
         for q in range(7):
             g_ref[q, row] = jnp.where(fluid, base - 0.25 * phase_adj[q], rest + phase_adj[BACK[q]])
-    send(g_ref, out_g_ref)
+        send(g_ref.at[:, pl.ds(row, 1)], out_g_ref.at[:, pl.ds(row, 1)])
     for copy in copies:
         copy.wait()
 
@@ -1002,8 +1007,8 @@
     )(main, rim, phase, odd, even, seeds, moments, prim_in, post_in)
     odd, even = swap(odd, "tile", 1), swap(even, "tile", 0)
     flow, back, dphi = call(
-        ahead_kernel, [(19, 4) + tile, (4, 8) + tile, (4,) + tile], 5, scratch=[(4, 4) + tile], flops=2 * 10**8,
-        name="ahead",
+        ahead_kernel, [(19, 4) + tile, (4, 8) + tile, (4,) + tile], 5, scratch=[(4, 4) + tile, (19, 8) + tile],
+        flops=2 * 10**8, name="ahead",
     )(main, prim_in, prim_out, adj, gamma)
     return tuple(
         call(
@@ -1012,7 +1017,7 @@
             11,
             scratch=[
                 (12,) + tile, (4, 8) + tile, (4, 8) + tile, (4,) + tile, (7, 4) + tile, (19, 4) + tile,
-                pltpu.SemaphoreType.DMA((4,)),
+                pltpu.SemaphoreType.DMA((7,)),
             ],
             flops=10**8, name="last", any_out=True,
         )(main, prim_in, prim_out, adj, gamma, edges, flow, back, dphi, odd, even)

time: 38.7 us -> 38.1 us (0.984)
  Pallas kernels: 9.24 us -> 8.78 us
where the time goes in v4:
time: 38.1 us; the launch traced here: 37.9 us
  starting transfers between devices  20.2 us (53%)
  Pallas kernels  8.78 us (23%)
  waiting for transfers between devices  8.28 us (22%)
  between operations  0.72 us (2%)
    ppermute x6, starting transfers between devices, swap(): return lax.ppermute(x, axis, pairs)  20.2 us
    ppermute x6, waiting for transfers between devices, swap(): return lax.ppermute(x, axis, pairs)  8.28 us
    pallas_call x1, Pallas kernels, shards(): call(middle_kernel, [(10, 8) + tile, (19, 8) + tile, (8,) + tile, (4,) +...  2.06 us
    pallas_call x1, Pallas kernels, shards(): call(rim_kernel, [(27, 4) + tile, jax.ShapeDtypeStruct((3,) + weights.sha...  1.66 us
    pallas_call x1, Pallas kernels, shards(): call(probe_kernel, [(9, 12) + tile], 2, scratch=[(192, 144), pltpu.VMEM(w...  1.63 us
    pallas_call x1, Pallas kernels, shards(): call(last_kernel, [(7, 4) + tile, (19, 4) + tile], 11, scratch=[(12,) + t...  1.35 us
    pallas_call x1, Pallas kernels, shards(): call(ahead_kernel, [(19, 4) + tile, (4, 8) + tile, (4,) + tile], 5, scrat...  0.83 us
  transfers between devices with their start and end apart: 6, of which 4 were waited for; matrix products, arithmetic and copies ran while one was open for 0% of the time, Pallas kernels for 8%

profile of v4, /device:TPU:24, one launch (start us, length us, event | category | flops | bytes accessed | tf_op | source)
XLA Modules:
  0.0 37.9 jit_solution(5541479775892101572)
XLA Ops:
  0.6 1.7 %rim.1 = (f32[27,4,16,128]{3,2,1,0:T(8,128)S(1)}, s32[3,256,128]{2,1,0:T(8,128)S(1)}, f32[256,128]{1,0:T(8,128)S(1)}, f32[2,4,16,128]{3,2,1,0:T(8,128)S(1)}, f32[2,4,16,128]{3,2,1,0:T(8,128)S(1)}) custom-call(f32[7,4,16,128]{3,2,1,0:T(8,128)} %g_ref.1, f32[19,4,16,128]{3,2,1,0:T(8,128)} %f_ref.1, s32[4,16,128]{2,1,0:T(8,128)} %solid_ref.1, ...), custom_call_target="tpu_custom_call" | custom-call | flops 1000000 | bytes 125000 | tf_op jit(solution)/shard_map/rim/pallas_call | solution.py:982
  2.3 0.7 %collective-permute-start = (f32[2,4,16,128]{3,2,1,0:T(8,128)S(1)}, f32[2,4,16,128]{3,2,1,0:T(8,128)S(1)}, u32[]{:S(2)}, u32[]{:S(2)}) collective-permute-start(f32[2,4,16,128]{3,2,1,0:T(8,128)S(1)} %get-tuple-element.26), channel_id=1, source_target_pairs={{1,2},{2,1},{5,6},{6,5},{9,10},{10,9},{13,14},{14,13},{17,18},{18,... | collective-permute-start | bytes 196616 | tf_op jit(solution)/shard_map/ppermute | solution.py:975
  3.0 2.9 %collective-permute-start.1 = (f32[2,4,16,128]{3,2,1,0:T(8,128)S(1)}, f32[2,4,16,128]{3,2,1,0:T(8,128)S(1)}, u32[]{:S(2)}, u32[]{:S(2)}) collective-permute-start(f32[2,4,16,128]{3,2,1,0:T(8,128)S(1)} %get-tuple-element.27), channel_id=1, source_target_pairs={{0,1},{1,0},{2,3},{3,2},{4,5},{5,4},{6,7},{7,6},{8,9},{9,8},{10,11... | collective-permute-start | bytes 196616 | tf_op jit(solution)/shard_map/ppermute | solution.py:975
  5.9 1.6 %probes.1.seeds_ref = f32[9,12,16,128]{3,2,1,0:T(8,128)S(1)} custom-call(s32[3,256,128]{2,1,0:T(8,128)S(1)} %get-tuple-element.24.probes_ref, f32[256,128]{1,0:T(8,128)S(1)} %get-tuple-element.25.weights_ref), custom_call_target="tpu_custom_call" | custom-call | flops 2000000000 | bytes 250000000 | tf_op jit(solution)/shard_map/probes/pallas_call | solution.py:989
  7.6 0.0 collective-permute-done.odd_in_ref
  7.6 0.0 collective-permute-done.1.even_in_ref
  7.6 0.5 %ring.1 = (f32[27,4,16,128]{3,2,1,0:T(8,128)S(1)}, f32[8,16,128]{2,1,0:T(8,128)S(1)}, f32[14,16,128]{2,1,0:T(8,128)S(1)}, f32[14,16,128]{2,1,0:T(8,128)S(1)}) custom-call(f32[9,12,16,128]{3,2,1,0:T(8,128)S(1)} %probes.1.seeds_ref, f32[27,4,16,128]{3,2,1,0:T(8,128)S(1)} %get-tuple-element.23.main_ref, f32[2,4,16,128]{3,2,1,0:T(8,128)S(1)} %collective-permute-done.odd_in_ref, ...), custom_call_target="tpu_custom_call" | custom-call | flops 10000000 | bytes 1250000 | tf_op jit(solution)/shard_map/ring/pallas_call | solution.py:993
  8.1 9.8 %collective-permute-start.2 = (f32[14,16,128]{2,1,0:T(8,128)S(1)}, f32[14,16,128]{2,1,0:T(8,128)S(1)}, u32[]{:S(2)}, u32[]{:S(2)}) collective-permute-start(f32[14,16,128]{2,1,0:T(8,128)S(1)} %get-tuple-element.31), channel_id=1, source_target_pairs={{4,8},{8,4},{12,16},{16,12},{20,24},{24,20},{28,32},{32,28},{36,40... | collective-permute-start | bytes 344072 | tf_op jit(solution)/shard_map/ppermute | solution.py:975
  17.9 0.1 collective-permute-start.3
  18.0 0.7 %inner.1 = (f32[10,4,16,128]{3,2,1,0:T(8,128)S(1)}, f32[26,4,16,128]{3,2,1,0:T(8,128)S(1)}, f32[10,8,16,128]{3,2,1,0:T(8,128)S(1)}) custom-call(f32[27,4,16,128]{3,2,1,0:T(8,128)S(1)} %get-tuple-element.23.main_ref, f32[27,4,16,128]{3,2,1,0:T(8,128)S(1)} %get-tuple-element.28.rim_ref, f32[8,16,128]{2,1,0:T(8,128)S(1)} %get-tuple-element.29.phase_ref, ...), custom_call_target="tpu_custom_call" | custom-call | flops 200000000 | bytes 25000000 | tf_op jit(solution)/shard_map/inner/pallas_call | solution.py:997
  18.7 3.1 %collective-permute-done.2.odd_in_ref = f32[14,16,128]{2,1,0:T(8,128)S(1)} collective-permute-done((f32[14,16,128]{2,1,0:T(8,128)S(1)}, f32[14,16,128]{2,1,0:T(8,128)S(1)}, u32[]{:S(2)}, u32[]{:S(2)}) %collective-permute-start.2) | collective-permute-done | bytes 114720 | tf_op jit(solution)/shard_map/ppermute | solution.py:975
  21.8 1.7 %collective-permute-done.3.even_in_ref = f32[14,16,128]{2,1,0:T(8,128)S(1)} collective-permute-done((f32[14,16,128]{2,1,0:T(8,128)S(1)}, f32[14,16,128]{2,1,0:T(8,128)S(1)}, u32[]{:S(2)}, u32[]{:S(2)}) %collective-permute-start.3) | collective-permute-done | bytes 114720 | tf_op jit(solution)/shard_map/ppermute | solution.py:975
  23.5 2.1 %middle.1 = (f32[10,8,16,128]{3,2,1,0:T(8,128)S(1)}, f32[19,8,16,128]{3,2,1,0:T(8,128)S(1)}, f32[8,16,128]{2,1,0:T(8,128)S(1)}, f32[4,16,128]{2,1,0:T(8,128)S(1)...) custom-call(f32[27,4,16,128]{3,2,1,0:T(8,128)S(1)} %get-tuple-element.23.main_ref, ...), custom_call_target="tpu_custom_call" | custom-call | flops 100000000 | bytes 12500000 | tf_op jit(solution)/shard_map/middle/pallas_call | solution.py:1001
  25.6 6.6 %collective-permute-start.4 = (f32[9,16,128]{2,1,0:T(8,128)S(1)}, f32[9,16,128]{2,1,0:T(8,128)S(1)}, u32[]{:S(2)}, u32[]{:S(2)}) collective-permute-start(f32[9,16,128]{2,1,0:T(8,128)S(1)} %get-tuple-element.42), channel_id=1, source_target_pairs={{4,8},{8,4},{12,16},{16,12},{20,24},{24,20},{28,32},{32,28},{36,40... | collective-permute-start | bytes 221192 | tf_op jit(solution)/shard_map/ppermute | solution.py:975
  32.1 0.1 collective-permute-start.5
  32.2 0.8 %ahead.1 = (f32[19,4,16,128]{3,2,1,0:T(8,128)S(1)}, f32[4,8,16,128]{3,2,1,0:T(8,128)S(1)}, f32[4,16,128]{2,1,0:T(8,128)S(1)}) custom-call(f32[27,4,16,128]{3,2,1,0:T(8,128)S(1)} %get-tuple-element.23.main_ref, f32[10,4,16,128]{3,2,1,0:T(8,128)S(1)} %get-tuple-element.30.prim_in_ref, f32[10,8,16,128]{3,2,1,0:T(8,128)S(1)} %get-tuple-element.35.prim_out_ref, ...), custom_call_target="tpu_custom_call" | custom-call | flops 200000000 | bytes 25000000 | tf_op jit(solution)/shard_map/ahead/pallas_call | solution.py:1009
  33.1 3.2 %collective-permute-done.4.odd_in_ref = f32[9,16,128]{2,1,0:T(8,128)S(1)} collective-permute-done((f32[9,16,128]{2,1,0:T(8,128)S(1)}, f32[9,16,128]{2,1,0:T(8,128)S(1)}, u32[]{:S(2)}, u32[]{:S(2)}) %collective-permute-start.4) | collective-permute-done | bytes 73760 | tf_op jit(solution)/shard_map/ppermute | solution.py:975
  36.3 0.3 collective-permute-done.5.even_in_ref
  36.6 1.4 %last.1 = (f32[7,4,16,128]{3,2,1,0:T(8,128)}, f32[19,4,16,128]{3,2,1,0:T(8,128)}) custom-call(f32[27,4,16,128]{3,2,1,0:T(8,128)S(1)} %get-tuple-element.23.main_ref, f32[10,4,16,128]{3,2,1,0:T(8,128)S(1)} %get-tuple-element.30.prim_in_ref, f32[10,8,16,128]{3,2,1,0:T(8,128)S(1)} %get-tuple-element.35.prim_out_ref, ...), custom_call_target="tpu_custom_call" | custom-call | flops 100000000 | bytes 12500000 | tf_op jit(solution)/shard_map/last/pallas_call | solution.py:1014
Async XLA Ops:
  2.3 5.3 %collective-permute-start = (f32[2,4,16,128]{3,2,1,0:T(8,128)S(1)}, f32[2,4,16,128]{3,2,1,0:T(8,128)S(1)}, u32[]{:S(2)}, u32[]{:S(2)}) collective-permute-start(f32[2,4,16,128]{3,2,1,0:T(8,128)S(1)} %get-tuple-element.26), channel_id=1, source_target_pairs={{1,2},{2,1},{5,6},{6,5},{9,10},{10,9},{13,14},{14,13},{17,18},{18,... | collective-permute-start | bytes 196616 | tf_op jit(solution)/shard_map/ppermute | solution.py:975
  3.0 4.6 %collective-permute-start.1 = (f32[2,4,16,128]{3,2,1,0:T(8,128)S(1)}, f32[2,4,16,128]{3,2,1,0:T(8,128)S(1)}, u32[]{:S(2)}, u32[]{:S(2)}) collective-permute-start(f32[2,4,16,128]{3,2,1,0:T(8,128)S(1)} %get-tuple-element.27), channel_id=1, source_target_pairs={{0,1},{1,0},{2,3},{3,2},{4,5},{5,4},{6,7},{7,6},{8,9},{9,8},{10,11... | collective-permute-start | bytes 196616 | tf_op jit(solution)/shard_map/ppermute | solution.py:975
  8.1 13.7 %collective-permute-start.2 = (f32[14,16,128]{2,1,0:T(8,128)S(1)}, f32[14,16,128]{2,1,0:T(8,128)S(1)}, u32[]{:S(2)}, u32[]{:S(2)}) collective-permute-start(f32[14,16,128]{2,1,0:T(8,128)S(1)} %get-tuple-element.31), channel_id=1, source_target_pairs={{4,8},{8,4},{12,16},{16,12},{20,24},{24,20},{28,32},{32,28},{36,40... | collective-permute-start | bytes 344072 | tf_op jit(solution)/shard_map/ppermute | solution.py:975
  17.9 5.6 %collective-permute-start.3 = (f32[14,16,128]{2,1,0:T(8,128)S(1)}, f32[14,16,128]{2,1,0:T(8,128)S(1)}, u32[]{:S(2)}, u32[]{:S(2)}) collective-permute-start(f32[14,16,128]{2,1,0:T(8,128)S(1)} %get-tuple-element.32), channel_id=1, source_target_pairs={{0,4},{4,0},{8,12},{12,8},{16,20},{20,16},{24,28},{28,24},{32,36},... | collective-permute-start | bytes 344072 | tf_op jit(solution)/shard_map/ppermute | solution.py:975
  25.6 10.8 %collective-permute-start.4 = (f32[9,16,128]{2,1,0:T(8,128)S(1)}, f32[9,16,128]{2,1,0:T(8,128)S(1)}, u32[]{:S(2)}, u32[]{:S(2)}) collective-permute-start(f32[9,16,128]{2,1,0:T(8,128)S(1)} %get-tuple-element.42), channel_id=1, source_target_pairs={{4,8},{8,4},{12,16},{16,12},{20,24},{24,20},{28,32},{32,28},{36,40... | collective-permute-start | bytes 221192 | tf_op jit(solution)/shard_map/ppermute | solution.py:975
  32.1 4.4 %collective-permute-start.5 = (f32[9,16,128]{2,1,0:T(8,128)S(1)}, f32[9,16,128]{2,1,0:T(8,128)S(1)}, u32[]{:S(2)}, u32[]{:S(2)}) collective-permute-start(f32[9,16,128]{2,1,0:T(8,128)S(1)} %get-tuple-element.43), channel_id=1, source_target_pairs={{0,4},{4,0},{8,12},{12,8},{16,20},{20,16},{24,28},{28,24},{32,36},... | collective-permute-start | bytes 221192 | tf_op jit(solution)/shard_map/ppermute | solution.py:975

commit v5 on v4

--- a/solution.py
+++ b/solution.py
@@ -101,12 +101,12 @@
         even_ref[n] = jnp.where(odd, l, r)
 
 
-def received(odd_ref, even_ref, count, wide=()):
+def received(odd_ref, even_refs, count, wide=()):
     odd = is_odd("tile")
     slots = rim_slots(count, wide)
     tiles = message_tiles(count, wide)
     got_odd = [odd_ref[n] for n in range(tiles)]
-    got_even = [even_ref[n] for n in range(tiles)]
+    got_even = [total([ref[n] for ref in even_refs]) for n in range(tiles)]
     sides = []
     for one, two in ((got_even, got_odd), (got_odd, got_even)):
         msg = [jnp.where(odd, a, b) for a, b in zip(one, two)]
@@ -405,7 +405,7 @@
         copy.wait()
 
 
-def ring_kernel(seeds_ref, main_ref, odd_in_ref, even_in_ref, rim_ref, phase_ref, odd_ref, even_ref):
+def ring_kernel(seeds_ref, main_ref, odd_in_ref, even_in_ref, rim_ref, phase_ref, odd_ref, even_ref, rest_ref):
     del seeds_ref
     lane = lanes()
     odd = is_odd("vert")
@@ -478,6 +478,8 @@
         fields.append(inner_phi)
         messages.append(fields)
     pack(odd_ref, even_ref, *messages, wide=WIDE_FIRST)
+    for n in range(message_tiles(N_FIRST, WIDE_FIRST)):
+        rest_ref[n] = even_ref[n]
 
 
 SHIFTS = sorted({c[1:] for c in DIRS})
@@ -620,12 +622,12 @@
 
 
 def middle_kernel(
-    main_ref, rim_ref, phase_ref, odd_in_ref, even_in_ref, seeds_ref, moments_ref, prim_in_ref, post_in_ref,
+    main_ref, rim_ref, phase_ref, near_in_ref, odd_in_ref, rest_in_ref, seeds_ref, moments_ref, prim_in_ref, post_in_ref,
     prim_ref, adj_ref, gamma_ref, edges_ref, odd_ref, even_ref,
     post_ref, phase_mid_ref, grad_mid_ref, back_ref, dphi_ref,
 ):
     prims, posts = (prim_in_ref, prim_ref), (post_in_ref, post_ref)
-    from_left, from_right = received(odd_in_ref, even_in_ref, N_FIRST, WIDE_FIRST)
+    from_left, from_right = received(odd_in_ref, (near_in_ref, rest_in_ref), N_FIRST, WIDE_FIRST)
     sides = ((from_left, -1, TO_RIGHT, 1), (from_right, 4, TO_LEFT, 2))
     for got, row, crossing, out in sides:
         _, at = spot(prims, row)
@@ -852,7 +854,7 @@
 
 def last_kernel(
     main_ref, prim_in_ref, prim_out_ref, adj_ref, gamma_ref, edges_ref, flow_ref, back_in_ref, dphi_in_ref,
-    odd_in_ref, even_in_ref,
+    even_in_ref, odd_in_ref,
     out_g_ref, out_f_ref,
     gamma_wide_ref, turned_ref, back_ref, dphi_ref, g_ref, f_ref, sems,
 ):
@@ -864,7 +866,7 @@
         copies.append(pltpu.make_async_copy(src, dst, sems.at[len(copies)]))
         copies[-1].start()
 
-    got_left, got_right = received(odd_in_ref, even_in_ref, N_SECOND)
+    got_left, got_right = received(odd_in_ref, (even_in_ref,), N_SECOND)
     own_first = load_pair(edges_ref, 0)
     own_last = load_pair(edges_ref, 1)
 
@@ -968,11 +970,19 @@
     )
 
 
-def swap(x, axis, first):
+def swap(x, axis, first, wanted=lambda i: True):
     pairs = []
     for i in range(first, lax.axis_size(axis) - 1, 2):
-        pairs += [(i, i + 1), (i + 1, i)]
+        if wanted(i):
+            pairs += [(i, i + 1), (i + 1, i)]
     return lax.ppermute(x, axis, pairs)
+
+
+LINE = 8
+
+
+def before_long(i):
+    return i % LINE == LINE - 2
 
 
 def shards(phase_init, flow_init, solid_mask, sensor_cells, sensor_weights):
@@ -990,10 +1000,12 @@
         probes, weights
     )
     first = message_tiles(N_FIRST, WIDE_FIRST)
-    rim, phase, odd, even = call(
-        ring_kernel, [(27, 4) + tile, (8,) + tile] + [(first,) + tile] * 2, 4, any_in=1, flops=10**7, name="ring"
+    rim, phase, odd, even, rest = call(
+        ring_kernel, [(27, 4) + tile, (8,) + tile] + [(first,) + tile] * 3, 4, any_in=1, flops=10**7, name="ring"
     )(seeds, main, odd, even)
-    odd, even = swap(odd, "tile", 1), swap(even, "tile", 0)
+    near = swap(even, "tile", 0, lambda i: not before_long(i))
+    odd = swap(odd, "tile", 1)
+    rest = swap(rest, "tile", 0, before_long)
     prim_in, post_in, moments = call(
         inner_kernel, [(10, 4) + tile, (26, 4) + tile, (10, 8) + tile], 4, flops=2 * 10**8, name="inner"
     )(main, rim, phase, seeds)
@@ -1001,11 +1013,12 @@
     prim_out, adj, gamma, edges, odd, even = call(
         middle_kernel,
         [(10, 8) + tile, (19, 8) + tile, (8,) + tile, (4,) + tile] + [(second,) + tile] * 2,
-        9,
+        10,
         scratch=[(26, 8) + tile, (12,) + tile, (4, 8) + tile, (4, 8) + tile, (8,) + tile],
         flops=10**8, name="middle",
-    )(main, rim, phase, odd, even, seeds, moments, prim_in, post_in)
-    odd, even = swap(odd, "tile", 1), swap(even, "tile", 0)
+    )(main, rim, phase, near, odd, rest, seeds, moments, prim_in, post_in)
+    even = swap(even, "tile", 0)
+    odd = swap(odd, "tile", 1)
     flow, back, dphi = call(
         ahead_kernel, [(19, 4) + tile, (4, 8) + tile, (4,) + tile], 5, scratch=[(4, 4) + tile, (19, 8) + tile],
         flops=2 * 10**8, name="ahead",
@@ -1020,7 +1033,7 @@
                 pltpu.SemaphoreType.DMA((7,)),
             ],
             flops=10**8, name="last", any_out=True,
-        )(main, prim_in, prim_out, adj, gamma, edges, flow, back, dphi, odd, even)
+        )(main, prim_in, prim_out, adj, gamma, edges, flow, back, dphi, even, odd)
     )
 
 

time: 38.1 us -> 37.9 us (level)
  waiting for transfers between devices: 8.28 us -> 4.45 us
  starting transfers between devices: 20.2 us -> 24 us
    ppermute x6 -> x7, starting transfers between devices: 20.2 us -> 24 us  [swap(): return lax.ppermute(x, axis, pairs)]
    ppermute x6 -> x7, waiting for transfers between devices: 8.28 us -> 4.45 us  [swap(): return lax.ppermute(x, axis, pairs)]
  transfers between devices with their start and end apart: 6 -> 7, of which waited for: 4 -> 2; matrix products, arithmetic and copies ran while one was open for 0% -> 0% of each run, Pallas kernels for 8% -> 8%
where the time goes in v5:
time: 37.9 us; the launch traced here: 37.6 us
  starting transfers between devices  24 us (63%)
  Pallas kernels  8.43 us (22%)
  waiting for transfers between devices  4.45 us (12%)
  between operations  0.75 us (2%)
    ppermute x7, starting transfers between devices, swap(): return lax.ppermute(x, axis, pairs)  24 us
    ppermute x7, waiting for transfers between devices, swap(): return lax.ppermute(x, axis, pairs)  4.45 us
    pallas_call x1, Pallas kernels, shards(): call(middle_kernel, [(10, 8) + tile, (19, 8) + tile, (8,) + tile, (4,) +...  2.06 us
    pallas_call x1, Pallas kernels, shards(): call(rim_kernel, [(27, 4) + tile, jax.ShapeDtypeStruct((3,) + weights.sha...  1.66 us
    pallas_call x1, Pallas kernels, shards(): call(last_kernel, [(7, 4) + tile, (19, 4) + tile], 11, scratch=[(12,) + t...  1.35 us
    pallas_call x1, Pallas kernels, shards(): call(probe_kernel, [(9, 12) + tile], 2, scratch=[(192, 144), pltpu.VMEM(w...  1.31 us
    pallas_call x1, Pallas kernels, shards(): call(ahead_kernel, [(19, 4) + tile, (4, 8) + tile, (4,) + tile], 5, scrat...  0.83 us
  transfers between devices with their start and end apart: 7, of which 2 were waited for; matrix products, arithmetic and copies ran while one was open for 0% of the time, Pallas kernels for 8%

profile of v5, /device:TPU:24, one launch (start us, length us, event | category | flops | bytes accessed | tf_op | source)
XLA Modules:
  0.0 37.6 jit_solution(7005390494401773797)
XLA Ops:
  0.6 1.7 %rim.1 = (f32[27,4,16,128]{3,2,1,0:T(8,128)S(1)}, s32[3,256,128]{2,1,0:T(8,128)S(1)}, f32[256,128]{1,0:T(8,128)S(1)}, f32[2,4,16,128]{3,2,1,0:T(8,128)S(1)}, f32[2,4,16,128]{3,2,1,0:T(8,128)S(1)}) custom-call(f32[7,4,16,128]{3,2,1,0:T(8,128)} %g_ref.1, f32[19,4,16,128]{3,2,1,0:T(8,128)} %f_ref.1, s32[4,16,128]{2,1,0:T(8,128)} %solid_ref.1, ...), custom_call_target="tpu_custom_call" | custom-call | flops 1000000 | bytes 125000 | tf_op jit(solution)/shard_map/rim/pallas_call | solution.py:992
  2.3 0.7 %collective-permute-start = (f32[2,4,16,128]{3,2,1,0:T(8,128)S(1)}, f32[2,4,16,128]{3,2,1,0:T(8,128)S(1)}, u32[]{:S(2)}, u32[]{:S(2)}) collective-permute-start(f32[2,4,16,128]{3,2,1,0:T(8,128)S(1)} %get-tuple-element.27), channel_id=1, source_target_pairs={{1,2},{2,1},{5,6},{6,5},{9,10},{10,9},{13,14},{14,13},{17,18},{18,... | collective-permute-start | bytes 196616 | tf_op jit(solution)/shard_map/ppermute | solution.py:978
  3.0 2.9 %collective-permute-start.1 = (f32[2,4,16,128]{3,2,1,0:T(8,128)S(1)}, f32[2,4,16,128]{3,2,1,0:T(8,128)S(1)}, u32[]{:S(2)}, u32[]{:S(2)}) collective-permute-start(f32[2,4,16,128]{3,2,1,0:T(8,128)S(1)} %get-tuple-element.28), channel_id=1, source_target_pairs={{0,1},{1,0},{2,3},{3,2},{4,5},{5,4},{6,7},{7,6},{8,9},{9,8},{10,11... | collective-permute-start | bytes 196616 | tf_op jit(solution)/shard_map/ppermute | solution.py:978
  5.9 1.3 %probes.1.seeds_ref = f32[9,12,16,128]{3,2,1,0:T(8,128)S(1)} custom-call(s32[3,256,128]{2,1,0:T(8,128)S(1)} %get-tuple-element.25.probes_ref, f32[256,128]{1,0:T(8,128)S(1)} %get-tuple-element.26.weights_ref), custom_call_target="tpu_custom_call" | custom-call | flops 2000000000 | bytes 250000000 | tf_op jit(solution)/shard_map/probes/pallas_call | solution.py:999
  7.2 0.0 collective-permute-done.odd_in_ref
  7.2 0.0 collective-permute-done.1.even_in_ref
  7.3 0.5 %ring.1 = (f32[27,4,16,128]{3,2,1,0:T(8,128)S(1)}, f32[8,16,128]{2,1,0:T(8,128)S(1)}, f32[14,16,128]{2,1,0:T(8,128)S(1)}, f32[14,16,128]{2,1,0:T(8,128)S(1)}, f32[14,16,128]{2,1,0:T(8,128)S(1)}) custom-call(f32[9,12,16,128]{3,2,1,0:T(8,128)S(1)} %probes.1.seeds_ref, f32[27,4,16,128]{3,2,1,0:T(8,128)S(1)} %get-tuple-element.24.main_ref, ...), custom_call_target="tpu_custom_call" | custom-call | flops 10000000 | bytes 1250000 | tf_op jit(solution)/shard_map/ring/pallas_call | solution.py:1003
  7.7 4.2 %collective-permute-start.2 = (f32[14,16,128]{2,1,0:T(8,128)S(1)}, f32[14,16,128]{2,1,0:T(8,128)S(1)}, u32[]{:S(2)}, u32[]{:S(2)}) collective-permute-start(f32[14,16,128]{2,1,0:T(8,128)S(1)} %get-tuple-element.32), channel_id=1, source_target_pairs={{0,4},{4,0},{8,12},{12,8},{16,20},{20,16},{32,36},{36,32},{40,44},... | collective-permute-start | bytes 344072 | tf_op jit(solution)/shard_map/ppermute | solution.py:978
  11.9 6.9 %collective-permute-start.3 = (f32[14,16,128]{2,1,0:T(8,128)S(1)}, f32[14,16,128]{2,1,0:T(8,128)S(1)}, u32[]{:S(2)}, u32[]{:S(2)}) collective-permute-start(f32[14,16,128]{2,1,0:T(8,128)S(1)} %get-tuple-element.33), channel_id=1, source_target_pairs={{4,8},{8,4},{12,16},{16,12},{20,24},{24,20},{28,32},{32,28},{36,40... | collective-permute-start | bytes 344072 | tf_op jit(solution)/shard_map/ppermute | solution.py:978
  18.9 0.7 %collective-permute-start.4 = (f32[14,16,128]{2,1,0:T(8,128)S(1)}, f32[14,16,128]{2,1,0:T(8,128)S(1)}, u32[]{:S(2)}, u32[]{:S(2)}) collective-permute-start(f32[14,16,128]{2,1,0:T(8,128)S(1)} %get-tuple-element.34), channel_id=1, source_target_pairs={{24,28},{28,24},{56,60},{60,56},{88,92},{92,88},{120,124},{124,120... | collective-permute-start | bytes 344072 | tf_op jit(solution)/shard_map/ppermute | solution.py:978
  19.5 0.7 %inner.1 = (f32[10,4,16,128]{3,2,1,0:T(8,128)S(1)}, f32[26,4,16,128]{3,2,1,0:T(8,128)S(1)}, f32[10,8,16,128]{3,2,1,0:T(8,128)S(1)}) custom-call(f32[27,4,16,128]{3,2,1,0:T(8,128)S(1)} %get-tuple-element.24.main_ref, f32[27,4,16,128]{3,2,1,0:T(8,128)S(1)} %get-tuple-element.29.rim_ref, f32[8,16,128]{2,1,0:T(8,128)S(1)} %get-tuple-element.30.phase_ref, ...), custom_call_target="tpu_custom_call" | custom-call | flops 200000000 | bytes 25000000 | tf_op jit(solution)/shard_map/inner/pallas_call | solution.py:1009
  20.3 0.0 collective-permute-done.2.near_in_ref
  20.3 3.0 %collective-permute-done.3.odd_in_ref = f32[14,16,128]{2,1,0:T(8,128)S(1)} collective-permute-done((f32[14,16,128]{2,1,0:T(8,128)S(1)}, f32[14,16,128]{2,1,0:T(8,128)S(1)}, u32[]{:S(2)}, u32[]{:S(2)}) %collective-permute-start.3) | collective-permute-done | bytes 114720 | tf_op jit(solution)/shard_map/ppermute | solution.py:978
  23.3 0.0 collective-permute-done.4.rest_in_ref
  23.3 2.1 %middle.1 = (f32[10,8,16,128]{3,2,1,0:T(8,128)S(1)}, f32[19,8,16,128]{3,2,1,0:T(8,128)S(1)}, f32[8,16,128]{2,1,0:T(8,128)S(1)}, f32[4,16,128]{2,1,0:T(8,128)S(1)...) custom-call(f32[27,4,16,128]{3,2,1,0:T(8,128)S(1)} %get-tuple-element.24.main_ref, ...), custom_call_target="tpu_custom_call" | custom-call | flops 100000000 | bytes 12500000 | tf_op jit(solution)/shard_map/middle/pallas_call | solution.py:1013
  25.3 0.1 collective-permute-start.5
  25.4 8.6 %collective-permute-start.6 = (f32[9,16,128]{2,1,0:T(8,128)S(1)}, f32[9,16,128]{2,1,0:T(8,128)S(1)}, u32[]{:S(2)}, u32[]{:S(2)}) collective-permute-start(f32[9,16,128]{2,1,0:T(8,128)S(1)} %get-tuple-element.45), channel_id=1, source_target_pairs={{4,8},{8,4},{12,16},{16,12},{20,24},{24,20},{28,32},{32,28},{36,40... | collective-permute-start | bytes 221192 | tf_op jit(solution)/shard_map/ppermute | solution.py:978
  34.0 0.8 %ahead.1 = (f32[19,4,16,128]{3,2,1,0:T(8,128)S(1)}, f32[4,8,16,128]{3,2,1,0:T(8,128)S(1)}, f32[4,16,128]{2,1,0:T(8,128)S(1)}) custom-call(f32[27,4,16,128]{3,2,1,0:T(8,128)S(1)} %get-tuple-element.24.main_ref, f32[10,4,16,128]{3,2,1,0:T(8,128)S(1)} %get-tuple-element.31.prim_in_ref, f32[10,8,16,128]{3,2,1,0:T(8,128)S(1)} %get-tuple-element.37.prim_out_ref, ...), custom_call_target="tpu_custom_call" | custom-call | flops 200000000 | bytes 25000000 | tf_op jit(solution)/shard_map/ahead/pallas_call | solution.py:1022
  34.8 0.0 collective-permute-done.5.even_in_ref
  34.8 1.5 %collective-permute-done.6.odd_in_ref = f32[9,16,128]{2,1,0:T(8,128)S(1)} collective-permute-done((f32[9,16,128]{2,1,0:T(8,128)S(1)}, f32[9,16,128]{2,1,0:T(8,128)S(1)}, u32[]{:S(2)}, u32[]{:S(2)}) %collective-permute-start.6) | collective-permute-done | bytes 73760 | tf_op jit(solution)/shard_map/ppermute | solution.py:978
  36.3 1.3 %last.1 = (f32[7,4,16,128]{3,2,1,0:T(8,128)}, f32[19,4,16,128]{3,2,1,0:T(8,128)}) custom-call(f32[27,4,16,128]{3,2,1,0:T(8,128)S(1)} %get-tuple-element.24.main_ref, f32[10,4,16,128]{3,2,1,0:T(8,128)S(1)} %get-tuple-element.31.prim_in_ref, f32[10,8,16,128]{3,2,1,0:T(8,128)S(1)} %get-tuple-element.37.prim_out_ref, ...), custom_call_target="tpu_custom_call" | custom-call | flops 100000000 | bytes 12500000 | tf_op jit(solution)/shard_map/last/pallas_call | solution.py:1027
Async XLA Ops:
  2.3 4.9 %collective-permute-start = (f32[2,4,16,128]{3,2,1,0:T(8,128)S(1)}, f32[2,4,16,128]{3,2,1,0:T(8,128)S(1)}, u32[]{:S(2)}, u32[]{:S(2)}) collective-permute-start(f32[2,4,16,128]{3,2,1,0:T(8,128)S(1)} %get-tuple-element.27), channel_id=1, source_target_pairs={{1,2},{2,1},{5,6},{6,5},{9,10},{10,9},{13,14},{14,13},{17,18},{18,... | collective-permute-start | bytes 196616 | tf_op jit(solution)/shard_map/ppermute | solution.py:978
  3.0 4.3 %collective-permute-start.1 = (f32[2,4,16,128]{3,2,1,0:T(8,128)S(1)}, f32[2,4,16,128]{3,2,1,0:T(8,128)S(1)}, u32[]{:S(2)}, u32[]{:S(2)}) collective-permute-start(f32[2,4,16,128]{3,2,1,0:T(8,128)S(1)} %get-tuple-element.28), channel_id=1, source_target_pairs={{0,1},{1,0},{2,3},{3,2},{4,5},{5,4},{6,7},{7,6},{8,9},{9,8},{10,11... | collective-permute-start | bytes 196616 | tf_op jit(solution)/shard_map/ppermute | solution.py:978
  7.7 12.6 %collective-permute-start.2 = (f32[14,16,128]{2,1,0:T(8,128)S(1)}, f32[14,16,128]{2,1,0:T(8,128)S(1)}, u32[]{:S(2)}, u32[]{:S(2)}) collective-permute-start(f32[14,16,128]{2,1,0:T(8,128)S(1)} %get-tuple-element.32), channel_id=1, source_target_pairs={{0,4},{4,0},{8,12},{12,8},{16,20},{20,16},{32,36},{36,32},{40,44},... | collective-permute-start | bytes 344072 | tf_op jit(solution)/shard_map/ppermute | solution.py:978
  11.9 11.3 %collective-permute-start.3 = (f32[14,16,128]{2,1,0:T(8,128)S(1)}, f32[14,16,128]{2,1,0:T(8,128)S(1)}, u32[]{:S(2)}, u32[]{:S(2)}) collective-permute-start(f32[14,16,128]{2,1,0:T(8,128)S(1)} %get-tuple-element.33), channel_id=1, source_target_pairs={{4,8},{8,4},{12,16},{16,12},{20,24},{24,20},{28,32},{32,28},{36,40... | collective-permute-start | bytes 344072 | tf_op jit(solution)/shard_map/ppermute | solution.py:978
  18.9 4.4 %collective-permute-start.4 = (f32[14,16,128]{2,1,0:T(8,128)S(1)}, f32[14,16,128]{2,1,0:T(8,128)S(1)}, u32[]{:S(2)}, u32[]{:S(2)}) collective-permute-start(f32[14,16,128]{2,1,0:T(8,128)S(1)} %get-tuple-element.34), channel_id=1, source_target_pairs={{24,28},{28,24},{56,60},{60,56},{88,92},{92,88},{120,124},{124,120... | collective-permute-start | bytes 344072 | tf_op jit(solution)/shard_map/ppermute | solution.py:978
  25.3 9.5 %collective-permute-start.5 = (f32[9,16,128]{2,1,0:T(8,128)S(1)}, f32[9,16,128]{2,1,0:T(8,128)S(1)}, u32[]{:S(2)}, u32[]{:S(2)}) collective-permute-start(f32[9,16,128]{2,1,0:T(8,128)S(1)} %get-tuple-element.44), channel_id=1, source_target_pairs={{0,4},{4,0},{8,12},{12,8},{16,20},{20,16},{24,28},{28,24},{32,36},... | collective-permute-start | bytes 221192 | tf_op jit(solution)/shard_map/ppermute | solution.py:978
  25.4 10.9 %collective-permute-start.6 = (f32[9,16,128]{2,1,0:T(8,128)S(1)}, f32[9,16,128]{2,1,0:T(8,128)S(1)}, u32[]{:S(2)}, u32[]{:S(2)}) collective-permute-start(f32[9,16,128]{2,1,0:T(8,128)S(1)} %get-tuple-element.45), channel_id=1, source_target_pairs={{4,8},{8,4},{12,16},{16,12},{20,24},{24,20},{28,32},{32,28},{36,40... | collective-permute-start | bytes 221192 | tf_op jit(solution)/shard_map/ppermute | solution.py:978

commit v6 on v4

--- a/solution.py
+++ b/solution.py
@@ -365,6 +365,14 @@
     return d_lap - 0.5 * d_grad
 
 
+NEAR = 5
+OWN_TILE = 24
+
+
+def rim_place(k, x):
+    return (x, NEAR * k) if k < OWN_TILE else (4, 30 * x + NEAR * (k - OWN_TILE))
+
+
 def rim_kernel(
     g_ref, f_ref, solid_ref, cells_ref, weights_ref,
     main_ref, probes_ref, probe_weights_ref, odd_ref, even_ref, mask_ref, sems,
@@ -385,46 +393,58 @@
         copy.start()
     lane = lanes()
     odd = is_odd("vert")
-    up = [[jnp.zeros((16, 128), F32)] * 4 for _ in range(2)]
-    down = [[jnp.zeros((16, 128), F32)] * 4 for _ in range(2)]
+    up = [jnp.zeros((16, 128), F32)] * 5
+    down = [jnp.zeros((16, 128), F32)] * 5
+    phase = [None] * 4
+
+    def put(cells, width, tile, first):
+        turned = roll(cells, first + width, 1)
+        up[tile] = jnp.where((lane >= first) & (lane < first + width), turned, up[tile])
+        down[tile] = jnp.where((lane >= first + width) & (lane < first + 2 * width), turned, down[tile])
+
     for fields, copy in parts:
         copy.wait()
         for k in fields:
-            tile, slot = k // 16, k % 16
             for x in range(4):
                 if k == FLUID:
                     main_ref[FLUID, x] = 1.0 - mask_ref[x].astype(F32)
-                turned = roll(main_ref[k, x], 8 * slot + 8, 1)
-                up[tile][x] = jnp.where(lane // RIM == slot, turned, up[tile][x])
-                down[tile][x] = jnp.where(lane // RIM == (slot + 1) % 16, turned, down[tile][x])
-    for tile in range(2):
-        for x in range(4):
-            odd_ref[tile, x] = jnp.where(odd, up[tile][x], down[tile][x])
-            even_ref[tile, x] = jnp.where(odd, down[tile][x], up[tile][x])
+                cells = main_ref[k, x]
+                put(cells, NEAR, *rim_place(k, x))
+                if k < 7:
+                    phase[x] = cells if k == 0 else phase[x] + cells
+    for x in range(4):
+        tile, first = rim_place(FLUID + 2, x)
+        up[tile] = jnp.where(lane == first, roll(phase[x], first - (127 - NEAR), 1), up[tile])
+        down[tile] = jnp.where(lane == first, roll(phase[x], first - NEAR, 1), down[tile])
+    for tile in range(5):
+        odd_ref[tile] = jnp.where(odd, up[tile], down[tile])
+        even_ref[tile] = jnp.where(odd, down[tile], up[tile])
     for copy in later:
         copy.wait()
 
 
-def ring_kernel(seeds_ref, main_ref, odd_in_ref, even_in_ref, rim_ref, phase_ref, odd_ref, even_ref):
-    del seeds_ref
+def ring_kernel(main_ref, odd_in_ref, even_in_ref, rim_ref, phase_ref, odd_ref, even_ref):
     lane = lanes()
     odd = is_odd("vert")
 
     def row(x):
-        above = [jnp.where(odd, odd_in_ref[t, x], even_in_ref[t, x]) for t in range(2)]
-        below = [jnp.where(odd, even_in_ref[t, x], odd_in_ref[t, x]) for t in range(2)]
-        even_group = lane // RIM % 2 == 0
-        mixed = [
-            (jnp.where(even_group, b, a), jnp.where(even_group, a, b)) for a, b in zip(above, below)
-        ]
+        mixed = []
+        for tile in (x, 4):
+            above = jnp.where(odd, odd_in_ref[tile], even_in_ref[tile])
+            below = jnp.where(odd, even_in_ref[tile], odd_in_ref[tile])
+            even_group = lane // NEAR % 2 == 0
+            mixed.append((jnp.where(even_group, below, above), jnp.where(even_group, above, below)))
         sums = [None, None]
         for k in range(27):
             cells = main_ref[k, x]
-            slot = k % 16
-            rim = roll(mixed[k // 16][slot % 2], 120 - 8 * slot, 1)
+            tile, first = rim_place(k, x)
+            rim = roll(mixed[tile == 4][first // NEAR % 2], 128 - NEAR - first, 1)
             rim_ref[k, x] = rim
             if k < 7:
                 sums = [a if b is None else a + b for a, b in zip((cells, rim), sums)]
+        _, first = rim_place(FLUID + 2, x)
+        sums[1] = jnp.where(lane == NEAR, roll(above, NEAR - first, 1), sums[1])
+        sums[1] = jnp.where(lane == 127 - NEAR, roll(below, 127 - NEAR - first, 1), sums[1])
         phase_ref[2 * x] = sums[0]
         phase_ref[2 * x + 1] = sums[1]
 
@@ -981,7 +1001,7 @@
     weights = sensor_weights.reshape(-1, 128)
     main, probes, weights, odd, even = call(
         rim_kernel,
-        [(27, 4) + tile, jax.ShapeDtypeStruct((3,) + weights.shape, jnp.int32), weights.shape] + [(2, 4) + tile] * 2,
+        [(27, 4) + tile, jax.ShapeDtypeStruct((3,) + weights.shape, jnp.int32), weights.shape] + [(5,) + tile] * 2,
         5, any_in=5, flops=10**6, name="rim",
         scratch=[pltpu.VMEM((4,) + tile, jnp.int32), pltpu.SemaphoreType.DMA((10,))],
     )(*(pltpu.with_memory_space_constraint(x, pltpu.HBM) for x in (phase_init, flow_init, solid_mask, cells, weights)))
@@ -991,8 +1011,8 @@
     )
     first = message_tiles(N_FIRST, WIDE_FIRST)
     rim, phase, odd, even = call(
-        ring_kernel, [(27, 4) + tile, (8,) + tile] + [(first,) + tile] * 2, 4, any_in=1, flops=10**7, name="ring"
-    )(seeds, main, odd, even)
+        ring_kernel, [(27, 4) + tile, (8,) + tile] + [(first,) + tile] * 2, 3, flops=10**7, name="ring"
+    )(main, odd, even)
     odd, even = swap(odd, "tile", 1), swap(even, "tile", 0)
     prim_in, post_in, moments = call(
         inner_kernel, [(10, 4) + tile, (26, 4) + tile, (10, 8) + tile], 4, flops=2 * 10**8, name="inner"

time: 38.1 us -> 37.9 us (level)
  waiting for transfers between devices: 8.28 us -> 7.7 us
    ppermute x6, waiting for transfers between devices: 8.28 us -> 7.7 us  [swap(): return lax.ppermute(x, axis, pairs)]
  transfers between devices with their start and end apart: 6 -> 6, of which waited for: 4 -> 5; matrix products, arithmetic and copies ran while one was open for 0% -> 0% of each run, Pallas kernels for 8% -> 9%
where the time goes in v6:
time: 37.9 us; the launch traced here: 37.7 us
  starting transfers between devices  20.5 us (54%)
  Pallas kernels  8.84 us (23%)
  waiting for transfers between devices  7.7 us (20%)
  between operations  0.71 us (2%)
    ppermute x6, starting transfers between devices, swap(): return lax.ppermute(x, axis, pairs)  20.5 us
    ppermute x6, waiting for transfers between devices, swap(): return lax.ppermute(x, axis, pairs)  7.7 us
    pallas_call x1, Pallas kernels, shards(): call(middle_kernel, [(10, 8) + tile, (19, 8) + tile, (8,) + tile, (4,) +...  2.06 us
    pallas_call x1, Pallas kernels, shards(): call(rim_kernel, [(27, 4) + tile, jax.ShapeDtypeStruct((3,) + weights.sha...  1.69 us
    pallas_call x1, Pallas kernels, shards(): call(probe_kernel, [(9, 12) + tile], 2, scratch=[(192, 144), pltpu.VMEM(w...  1.64 us
    pallas_call x1, Pallas kernels, shards(): call(last_kernel, [(7, 4) + tile, (19, 4) + tile], 11, scratch=[(12,) + t...  1.35 us
    pallas_call x1, Pallas kernels, shards(): call(ahead_kernel, [(19, 4) + tile, (4, 8) + tile, (4,) + tile], 5, scrat...  0.83 us
  transfers between devices with their start and end apart: 6, of which 5 were waited for; matrix products, arithmetic and copies ran while one was open for 0% of the time, Pallas kernels for 9%

profile of v6, /device:TPU:24, one launch (start us, length us, event | category | flops | bytes accessed | tf_op | source)
XLA Modules:
  0.0 37.7 jit_solution(700865464309521726)
XLA Ops:
  0.6 1.7 %rim.1 = (f32[27,4,16,128]{3,2,1,0:T(8,128)S(1)}, s32[3,256,128]{2,1,0:T(8,128)S(1)}, f32[256,128]{1,0:T(8,128)S(1)}, f32[5,16,128]{2,1,0:T(8,128)S(1)}, f32[5,16,128]{2,1,0:T(8,128)S(1)}) custom-call(f32[7,4,16,128]{3,2,1,0:T(8,128)} %g_ref.1, f32[19,4,16,128]{3,2,1,0:T(8,128)} %f_ref.1, s32[4,16,128]{2,1,0:T(8,128)} %solid_ref.1, s32[256,3,128]{2,1,0:T(4,128)} %bitcast.4, ...), custom_call_target="tpu_custom_call" | custom-call | flops 1000000 | bytes 125000 | tf_op jit(solution)/shard_map/rim/pallas_call | solution.py:1002
  2.3 0.7 %collective-permute-start = (f32[5,16,128]{2,1,0:T(8,128)S(1)}, f32[5,16,128]{2,1,0:T(8,128)S(1)}, u32[]{:S(2)}, u32[]{:S(2)}) collective-permute-start(f32[5,16,128]{2,1,0:T(8,128)S(1)} %get-tuple-element.24), channel_id=1, source_target_pairs={{1,2},{2,1},{5,6},{6,5},{9,10},{10,9},{13,14},{14,13},{17,18},{18,... | collective-permute-start | bytes 122888 | tf_op jit(solution)/shard_map/ppermute | solution.py:995
  3.0 2.9 %collective-permute-start.1 = (f32[5,16,128]{2,1,0:T(8,128)S(1)}, f32[5,16,128]{2,1,0:T(8,128)S(1)}, u32[]{:S(2)}, u32[]{:S(2)}) collective-permute-start(f32[5,16,128]{2,1,0:T(8,128)S(1)} %get-tuple-element.25), channel_id=1, source_target_pairs={{0,1},{1,0},{2,3},{3,2},{4,5},{5,4},{6,7},{7,6},{8,9},{9,8},{10,11... | collective-permute-start | bytes 122888 | tf_op jit(solution)/shard_map/ppermute | solution.py:995
  5.9 0.0 collective-permute-done.odd_in_ref
  5.9 0.9 %collective-permute-done.1.even_in_ref = f32[5,16,128]{2,1,0:T(8,128)S(1)} collective-permute-done((f32[5,16,128]{2,1,0:T(8,128)S(1)}, f32[5,16,128]{2,1,0:T(8,128)S(1)}, u32[]{:S(2)}, u32[]{:S(2)}) %collective-permute-start.1) | collective-permute-done | bytes 40992 | tf_op jit(solution)/shard_map/ppermute | solution.py:995
  6.8 0.5 %ring.1 = (f32[27,4,16,128]{3,2,1,0:T(8,128)S(1)}, f32[8,16,128]{2,1,0:T(8,128)S(1)}, f32[14,16,128]{2,1,0:T(8,128)S(1)}, f32[14,16,128]{2,1,0:T(8,128)S(1)}) custom-call(f32[27,4,16,128]{3,2,1,0:T(8,128)S(1)} %get-tuple-element.23.main_ref, f32[5,16,128]{2,1,0:T(8,128)S(1)} %collective-permute-done.odd_in_ref, ...), custom_call_target="tpu_custom_call" | custom-call | flops 10000000 | bytes 1250000 | tf_op jit(solution)/shard_map/ring/pallas_call | solution.py:1013
  7.3 10.1 %collective-permute-start.2 = (f32[14,16,128]{2,1,0:T(8,128)S(1)}, f32[14,16,128]{2,1,0:T(8,128)S(1)}, u32[]{:S(2)}, u32[]{:S(2)}) collective-permute-start(f32[14,16,128]{2,1,0:T(8,128)S(1)} %get-tuple-element.31), channel_id=1, source_target_pairs={{4,8},{8,4},{12,16},{16,12},{20,24},{24,20},{28,32},{32,28},{36,40... | collective-permute-start | bytes 344072 | tf_op jit(solution)/shard_map/ppermute | solution.py:995
  17.5 0.1 collective-permute-start.3
  17.6 1.6 %probes.1.seeds_ref = f32[9,12,16,128]{3,2,1,0:T(8,128)S(1)} custom-call(s32[3,256,128]{2,1,0:T(8,128)S(1)} %get-tuple-element.28.probes_ref, f32[256,128]{1,0:T(8,128)S(1)} %get-tuple-element.29.weights_ref), custom_call_target="tpu_custom_call" | custom-call | flops 2000000000 | bytes 250000000 | tf_op jit(solution)/shard_map/probes/pallas_call | solution.py:1009
  19.2 0.7 %inner.1 = (f32[10,4,16,128]{3,2,1,0:T(8,128)S(1)}, f32[26,4,16,128]{3,2,1,0:T(8,128)S(1)}, f32[10,8,16,128]{3,2,1,0:T(8,128)S(1)}) custom-call(f32[27,4,16,128]{3,2,1,0:T(8,128)S(1)} %get-tuple-element.23.main_ref, f32[27,4,16,128]{3,2,1,0:T(8,128)S(1)} %get-tuple-element.26.rim_ref, f32[8,16,128]{2,1,0:T(8,128)S(1)} %get-tuple-element.27.phase_ref, ...), custom_call_target="tpu_custom_call" | custom-call | flops 200000000 | bytes 25000000 | tf_op jit(solution)/shard_map/inner/pallas_call | solution.py:1017
  20.0 1.2 %collective-permute-done.2.odd_in_ref = f32[14,16,128]{2,1,0:T(8,128)S(1)} collective-permute-done((f32[14,16,128]{2,1,0:T(8,128)S(1)}, f32[14,16,128]{2,1,0:T(8,128)S(1)}, u32[]{:S(2)}, u32[]{:S(2)}) %collective-permute-start.2) | collective-permute-done | bytes 114720 | tf_op jit(solution)/shard_map/ppermute | solution.py:995
  21.2 2.1 %collective-permute-done.3.even_in_ref = f32[14,16,128]{2,1,0:T(8,128)S(1)} collective-permute-done((f32[14,16,128]{2,1,0:T(8,128)S(1)}, f32[14,16,128]{2,1,0:T(8,128)S(1)}, u32[]{:S(2)}, u32[]{:S(2)}) %collective-permute-start.3) | collective-permute-done | bytes 114720 | tf_op jit(solution)/shard_map/ppermute | solution.py:995
  23.3 2.1 %middle.1 = (f32[10,8,16,128]{3,2,1,0:T(8,128)S(1)}, f32[19,8,16,128]{3,2,1,0:T(8,128)S(1)}, f32[8,16,128]{2,1,0:T(8,128)S(1)}, f32[4,16,128]{2,1,0:T(8,128)S(1)...) custom-call(f32[27,4,16,128]{3,2,1,0:T(8,128)S(1)} %get-tuple-element.23.main_ref, ...), custom_call_target="tpu_custom_call" | custom-call | flops 100000000 | bytes 12500000 | tf_op jit(solution)/shard_map/middle/pallas_call | solution.py:1021
  25.3 6.6 %collective-permute-start.4 = (f32[9,16,128]{2,1,0:T(8,128)S(1)}, f32[9,16,128]{2,1,0:T(8,128)S(1)}, u32[]{:S(2)}, u32[]{:S(2)}) collective-permute-start(f32[9,16,128]{2,1,0:T(8,128)S(1)} %get-tuple-element.42), channel_id=1, source_target_pairs={{4,8},{8,4},{12,16},{16,12},{20,24},{24,20},{28,32},{32,28},{36,40... | collective-permute-start | bytes 221192 | tf_op jit(solution)/shard_map/ppermute | solution.py:995
  31.9 0.1 collective-permute-start.5
  32.0 0.8 %ahead.1 = (f32[19,4,16,128]{3,2,1,0:T(8,128)S(1)}, f32[4,8,16,128]{3,2,1,0:T(8,128)S(1)}, f32[4,16,128]{2,1,0:T(8,128)S(1)}) custom-call(f32[27,4,16,128]{3,2,1,0:T(8,128)S(1)} %get-tuple-element.23.main_ref, f32[10,4,16,128]{3,2,1,0:T(8,128)S(1)} %get-tuple-element.30.prim_in_ref, f32[10,8,16,128]{3,2,1,0:T(8,128)S(1)} %get-tuple-element.35.prim_out_ref, ...), custom_call_target="tpu_custom_call" | custom-call | flops 200000000 | bytes 25000000 | tf_op jit(solution)/shard_map/ahead/pallas_call | solution.py:1029
  32.9 3.2 %collective-permute-done.4.odd_in_ref = f32[9,16,128]{2,1,0:T(8,128)S(1)} collective-permute-done((f32[9,16,128]{2,1,0:T(8,128)S(1)}, f32[9,16,128]{2,1,0:T(8,128)S(1)}, u32[]{:S(2)}, u32[]{:S(2)}) %collective-permute-start.4) | collective-permute-done | bytes 73760 | tf_op jit(solution)/shard_map/ppermute | solution.py:995
  36.1 0.3 collective-permute-done.5.even_in_ref
  36.4 1.4 %last.1 = (f32[7,4,16,128]{3,2,1,0:T(8,128)}, f32[19,4,16,128]{3,2,1,0:T(8,128)}) custom-call(f32[27,4,16,128]{3,2,1,0:T(8,128)S(1)} %get-tuple-element.23.main_ref, f32[10,4,16,128]{3,2,1,0:T(8,128)S(1)} %get-tuple-element.30.prim_in_ref, f32[10,8,16,128]{3,2,1,0:T(8,128)S(1)} %get-tuple-element.35.prim_out_ref, ...), custom_call_target="tpu_custom_call" | custom-call | flops 100000000 | bytes 12500000 | tf_op jit(solution)/shard_map/last/pallas_call | solution.py:1034
Async XLA Ops:
  2.3 3.6 %collective-permute-start = (f32[5,16,128]{2,1,0:T(8,128)S(1)}, f32[5,16,128]{2,1,0:T(8,128)S(1)}, u32[]{:S(2)}, u32[]{:S(2)}) collective-permute-start(f32[5,16,128]{2,1,0:T(8,128)S(1)} %get-tuple-element.24), channel_id=1, source_target_pairs={{1,2},{2,1},{5,6},{6,5},{9,10},{10,9},{13,14},{14,13},{17,18},{18,... | collective-permute-start | bytes 122888 | tf_op jit(solution)/shard_map/ppermute | solution.py:995
  3.0 3.8 %collective-permute-start.1 = (f32[5,16,128]{2,1,0:T(8,128)S(1)}, f32[5,16,128]{2,1,0:T(8,128)S(1)}, u32[]{:S(2)}, u32[]{:S(2)}) collective-permute-start(f32[5,16,128]{2,1,0:T(8,128)S(1)} %get-tuple-element.25), channel_id=1, source_target_pairs={{0,1},{1,0},{2,3},{3,2},{4,5},{5,4},{6,7},{7,6},{8,9},{9,8},{10,11... | collective-permute-start | bytes 122888 | tf_op jit(solution)/shard_map/ppermute | solution.py:995
  7.3 13.8 %collective-permute-start.2 = (f32[14,16,128]{2,1,0:T(8,128)S(1)}, f32[14,16,128]{2,1,0:T(8,128)S(1)}, u32[]{:S(2)}, u32[]{:S(2)}) collective-permute-start(f32[14,16,128]{2,1,0:T(8,128)S(1)} %get-tuple-element.31), channel_id=1, source_target_pairs={{4,8},{8,4},{12,16},{16,12},{20,24},{24,20},{28,32},{32,28},{36,40... | collective-permute-start | bytes 344072 | tf_op jit(solution)/shard_map/ppermute | solution.py:995
  17.5 5.8 %collective-permute-start.3 = (f32[14,16,128]{2,1,0:T(8,128)S(1)}, f32[14,16,128]{2,1,0:T(8,128)S(1)}, u32[]{:S(2)}, u32[]{:S(2)}) collective-permute-start(f32[14,16,128]{2,1,0:T(8,128)S(1)} %get-tuple-element.32), channel_id=1, source_target_pairs={{0,4},{4,0},{8,12},{12,8},{16,20},{20,16},{24,28},{28,24},{32,36},... | collective-permute-start | bytes 344072 | tf_op jit(solution)/shard_map/ppermute | solution.py:995
  25.3 10.8 %collective-permute-start.4 = (f32[9,16,128]{2,1,0:T(8,128)S(1)}, f32[9,16,128]{2,1,0:T(8,128)S(1)}, u32[]{:S(2)}, u32[]{:S(2)}) collective-permute-start(f32[9,16,128]{2,1,0:T(8,128)S(1)} %get-tuple-element.42), channel_id=1, source_target_pairs={{4,8},{8,4},{12,16},{16,12},{20,24},{24,20},{28,32},{32,28},{36,40... | collective-permute-start | bytes 221192 | tf_op jit(solution)/shard_map/ppermute | solution.py:995
  31.9 4.4 %collective-permute-start.5 = (f32[9,16,128]{2,1,0:T(8,128)S(1)}, f32[9,16,128]{2,1,0:T(8,128)S(1)}, u32[]{:S(2)}, u32[]{:S(2)}) collective-permute-start(f32[9,16,128]{2,1,0:T(8,128)S(1)} %get-tuple-element.43), channel_id=1, source_target_pairs={{0,4},{4,0},{8,12},{12,8},{16,20},{20,16},{24,28},{28,24},{32,36},... | collective-permute-start | bytes 221192 | tf_op jit(solution)/shard_map/ppermute | solution.py:995
